TPU v7x, 32 devices: a whole 2x2x4 slice. The times are simulated.
32 devices in a mesh: facet: 8 (over y, x, core), band: 4 (over z).
Axes of the slice: x: 2, y: 2, z: 4, core: 2. Of those that a mesh axis runs over, the one named last changes fastest.
Arguments:
- visibility: bfloat16 [8, 256, 64, 64], P('band', 'facet'), may hold values from -6 to 6
- uv_positions: int32 [8, 256, 2, 64], P('band', 'facet'), may hold values from 0 to 248
- destinations: int32 [8, 256, 1], P('band', 'facet'), may hold values from 0 to 7; in each aligned block of 32 rows (0 to 31, 32 to 63, ..., all dimensions but the last counted through in order) at most 8 rows name the same one
- column_slots: int32 [8, 256], P('band', 'facet'), may hold values from 0 to 1
- image_cube: float32 [8, 256, 3072], P('band', None, 'facet'), may hold values from 0 to 1
- dual_cube: float32 [8, 256, 3072], P('band', None, 'facet'), may hold values from -2 to 2
- step_sizes: float32 [8], P('band'), may hold values from 0.05 to 0.2
- conv_first: bfloat16 [64, 8, 3, 3], replicated, may hold values from -0.75 to 0.75
- conv_middle: bfloat16 [64, 64, 3, 3], replicated, may hold values from -0.25 to 0.25
- conv_last: bfloat16 [8, 64, 3, 3], replicated, may hold values from -0.25 to 0.25
Outputs:
- image_next: float32 [8, 256, 3072], P('band', None, 'facet')
- dual_next: float32 [8, 256, 3072], P('band', None, 'facet')
Inputs may be any that keep to these rules, and one draw needn't show every extreme that they name: `destinations`: in each aligned block of 32 rows (the blocks of one subband held by one device), no facet is named by more than 8 rows, a bound that some block reaches.
All inputs are finite; a program needn't handle non-finite values.
Results may differ from a plain program's by a relative error of at most 0.0067.
Values may be sent and summed in bfloat16 or wider, within the bound.
No kernel may reach another device: no remote copies, remote signals or barrier semaphores. Data moves between devices by JAX's collectives and lax.ppermute only.
A program may use at most 128 MiB of HBM per device.

v0:
```python
import jax
import jax.numpy as jnp
from jax import lax
from jax.sharding import PartitionSpec as P

P_SIZE = 256
KW = 8
S = 64


def extended(cells, sides, width):
    for axis, dim in sides:
        count = lax.axis_size(axis)
        ends = count - 1
        head = lax.slice_in_dim(cells, 0, width, axis=dim)
        tail = lax.slice_in_dim(cells, cells.shape[dim] - width, cells.shape[dim], axis=dim)
        cells = jnp.concatenate(
            [
                lax.ppermute(tail, axis, [(i, (i + 1) % count) for i in range(ends)]),
                cells,
                lax.ppermute(head, axis, [((i + 1) % count, i) for i in range(ends)]),
            ],
            axis=dim,
        )
    return cells


def kernel_matrix(positions):
    cell_index = jnp.arange(P_SIZE, dtype=jnp.float32)
    offset = cell_index[None, :] - positions[:, None]
    centre = (KW - 1) / 2.0
    spread = KW / 4.0
    tap_values = jnp.exp(-0.5 * ((offset - centre) / spread) ** 2)
    inside = (offset >= 0.0) & (offset < KW)
    return jnp.where(inside, tap_values, 0.0).astype(jnp.bfloat16)


def kernel_matrix_t(positions):
    cell_index = jnp.arange(P_SIZE, dtype=jnp.float32)
    offset = cell_index[:, None] - positions[None, :]
    centre = (KW - 1) / 2.0
    spread = KW / 4.0
    tap_values = jnp.exp(-0.5 * ((offset - centre) / spread) ** 2)
    inside = (offset >= 0.0) & (offset < KW)
    return jnp.where(inside, tap_values, 0.0).astype(jnp.bfloat16)


def make_panels(vis_set, pos_set):
    lead_shape = vis_set.shape[:-2]
    flat_pos = pos_set.reshape((-1, 2, S))
    rows_kernel = jax.vmap(kernel_matrix_t)(flat_pos[:, 0]).reshape(lead_shape + (P_SIZE, S))
    cols_kernel = jax.vmap(kernel_matrix)(flat_pos[:, 1]).reshape(lead_shape + (S, P_SIZE))
    half_product = jnp.einsum(
        "...ab,...bj->...aj", vis_set, cols_kernel, preferred_element_type=jnp.float32
    ).astype(jnp.bfloat16)
    return jnp.einsum(
        "...ia,...aj->...ij", rows_kernel, half_product, preferred_element_type=jnp.float32
    ).astype(jnp.bfloat16)


def accumulate(received, placement):
    item_count = received.shape[0]
    slot_count = received.shape[1] * received.shape[2]
    panel_rows = received.reshape(item_count, slot_count, P_SIZE, P_SIZE)
    weights = placement.reshape(item_count, slot_count, placement.shape[3])
    half_width = P_SIZE // 2
    tile_sum = None
    for part_index in range(2):
        panel_part = panel_rows[..., part_index * half_width : (part_index + 1) * half_width]
        contribution = jnp.einsum(
            "nmk,nmrc->nrkc", weights, panel_part, preferred_element_type=jnp.float32
        )
        shifted_part = jnp.pad(contribution, ((0, 0), (0, 0), (part_index, 1 - part_index), (0, 0)))
        tile_sum = shifted_part if tile_sum is None else tile_sum + shifted_part
    tile_count = tile_sum.shape[2]
    return tile_sum.reshape(item_count, P_SIZE, tile_count * half_width)


def conv_valid(padded, kernel, dilation, row_pad):
    result = lax.conv_general_dilated(
        padded[None],
        kernel,
        (1, 1),
        [(row_pad, row_pad), (0, 0)],
        rhs_dilation=(dilation, dilation),
        dimension_numbers=("NCHW", "OIHW", "NCHW"),
        preferred_element_type=jnp.float32,
    )
    return result[0]


def denoise(field, layer_fn, conv_first, conv_middle, conv_last):
    hidden_one = jnp.maximum(layer_fn(field, conv_first, 1), 0.0).astype(jnp.bfloat16)
    hidden_two = jnp.maximum(layer_fn(hidden_one, conv_middle, 2), 0.0).astype(jnp.bfloat16)
    return layer_fn(hidden_two, conv_last, 1).astype(jnp.bfloat16)


def body(
    visibility,
    uv_positions,
    destinations,
    column_slots,
    image_cube,
    dual_cube,
    step_sizes,
    conv_first,
    conv_middle,
    conv_last,
):
    local_subbands = visibility.shape[0]
    block_count = visibility.shape[1]
    facet_count = lax.axis_size("facet")
    capacity = max(2, 2 * block_count // facet_count)
    facet_width = image_cube.shape[2]
    offset_count = 2 * facet_width // P_SIZE - 1
    placement = (column_slots[..., None] == jnp.arange(offset_count, dtype=jnp.int32)).astype(
        jnp.bfloat16
    )
    target_facet = destinations[..., 0]
    facet_onehot = (target_facet[..., None] == jnp.arange(facet_count, dtype=jnp.int32)).astype(
        jnp.int32
    )
    arrival = jnp.sum((jnp.cumsum(facet_onehot, axis=1) - 1) * facet_onehot, axis=2)
    slot_index = target_facet * capacity + arrival

    def pack_slots(values):
        empty = jnp.zeros((local_subbands, facet_count * capacity) + values.shape[2:], values.dtype)

        def fill_one(buffer, entries, where):
            return buffer.at[where].set(entries)

        filled = jax.vmap(fill_one)(empty, values, slot_index)
        return filled.reshape((local_subbands, facet_count, capacity) + values.shape[2:])

    panel_set = make_panels(visibility, uv_positions.astype(jnp.float32))
    gradient = accumulate(
        lax.all_to_all(pack_slots(panel_set), "facet", split_axis=1, concat_axis=1, tiled=True),
        lax.all_to_all(pack_slots(placement), "facet", split_axis=1, concat_axis=1, tiled=True),
    )
    stepped = image_cube - step_sizes[:, None, None] * gradient
    shifted = stepped + dual_cube
    denoise_in = shifted.astype(jnp.bfloat16)
    spectral_cube = lax.all_gather(denoise_in, "band", axis=0, tiled=True)

    def layer_cols(field, kernel, dilation):
        padded = extended(field, (("facet", 2),), dilation)
        return conv_valid(padded, kernel, dilation, dilation)

    denoised = denoise(spectral_cube, layer_cols, conv_first, conv_middle, conv_last)
    own_denoised = lax.dynamic_slice_in_dim(
        denoised, lax.axis_index("band") * local_subbands, local_subbands, 0
    )
    image_next = jnp.maximum(shifted - own_denoised.astype(jnp.float32), 0.0)
    dual_next = dual_cube + stepped - image_next
    return (image_next, dual_next)


def solution(mesh):
    return jax.shard_map(
        body,
        mesh=mesh,
        in_specs=(
            P("band", "facet", None, None),
            P("band", "facet", None, None),
            P("band", "facet", None),
            P("band", "facet"),
            P("band", None, "facet"),
            P("band", None, "facet"),
            P("band"),
            P(),
            P(),
            P(),
        ),
        out_specs=(P("band", None, "facet"), P("band", None, "facet")),
        check_vma=False,
    )
```

profile of v0, /device:TPU:4, one launch (start us, length us, event | category | flops | bytes accessed | tf_op | source)
XLA Modules:
  0.0 725.1 jit_solution(11025821736990351634)
XLA Ops:
  7.2 0.8 fusion.65
  8.1 0.9 select_reduce_fusion
  10.5 3.8 scatter_fusion.1
  15.1 4.2 all-to-all-start.1
  19.3 0.9 convert_element_type.54
  20.3 8.4 %convolution_convert_fusion = bf16[2,32,256,256]{3,2,1,0:T(8,128)(2,1)} fusion(f32[2,32,64]{2,1,0:T(8,128)S(1)} %bitcast.106, bf16[2,32,64,64]{3,2,1,0:T(8,128)(2,1)S(1)} %copy-done, f32[2,32,64]{2,1,0:T(8,128)S(1)} %bitcast.105), kind=kOutput, calls=%fused_computation.40 | convolution fusion | flops 697303040 | bytes 8945664 | tf_op jit(solution)/shard_map/...ia,...aj->...ij/dot_general | solution.py:56
  28.7 5.9 broadcast_in_dim.14
  34.6 22.5 %scatter_fusion = bf16[2,64,256,256]{3,2,1,0:T(8,128)(2,1)} fusion(bf16[2,64,256,256]{3,2,1,0:T(8,128)(2,1)} %broadcast_in_dim.14, s32[64]{0:T(128)S(1)} %reshape.85, bf16[64,256,256]{2,1,0:T(8,128)(2,1)} %bitcast.99), kind=kCustom, calls=%fused_computation | custom fusion | bytes 25166336 | tf_op jit(solution)/shard_map/vmap()/scatter | solution.py:130
  57.0 17.8 %copy.85 = bf16[2,8,8,256,256]{4,2,3,0,1:T(8,128)(2,1)} copy(bf16[2,8,8,256,256]{4,3,2,1,0:T(8,128)(2,1)} %bitcast.92) | data formatting | bytes 33554432 | tf_op jit(solution)/shard_map/reshape | solution.py:133
  74.9 5.9 all-to-all-start
  81.5 181.7 %all-to-all-done = bf16[2,8,8,256,256]{4,2,3,0,1:T(8,128)(2,1)} async-done(((bf16[2,8,8,256,256]{4,2,3,0,1:T(8,128)(2,1)}), bf16[2,8,8,256,256]{4,2,3,0,1:T(8,128)(2,1)}, u32[]{:S(2)}, u32[]{:S(2)}) %all-to-all-start) | async-done | bytes 16777248 | tf_op jit(solution)/shard_map/all_to_all | solution.py:137
  263.2 8.6 %copy.118 = bf16[2,8,8,256,256]{4,2,1,3,0:T(8,128)(2,1)S(1)} copy(bf16[2,8,8,256,256]{4,2,3,0,1:T(8,128)(2,1)} %all-to-all-done) | data formatting | bytes 33554432 | tf_op jit(solution)/shard_map/all_to_all | solution.py:137
  271.8 1.2 fusion.58
  273.0 1.2 fusion.55
  275.0 1.1 fusion.89
  276.1 0.9 copy.94
  277.0 37.7 %all-gather.2.cloned.1.call-done = bf16[8,256,384]{2,1,0:T(8,128)(2,1)} async-done(((bf16[2,256,384]{2,1,0:T(8,128)(2,1)}), bf16[8,256,384]{2,1,0:T(8,128)(2,1)}) %all-gather.2.cloned.1.call-update) | async-done | bytes 1572880 | tf_op jit(solution)/shard_map/all_gather | solution.py:143
  314.7 2.3 copy.95
  317.0 2.7 collective-permute-start.1
  319.7 1.9 collective-permute-start
  321.7 3.9 collective-permute-done
  325.9 18.0 %copy.99 = bf16[8,256,1,8,49]{0,3,4,1,2:T(8,128)(2,1)} copy(bf16[8,256,1,8,49]{1,0,4,3,2:T(8,128)(2,1)S(1)} %bitcast.100) | data formatting | bytes 3211264 | tf_op jit(solution)/shard_map/conv_general_dilated | solution.py:80
  343.9 1.5 slice.56
  345.4 36.3 %maximum_convert_fusion.1 = bf16[256,8,49,64]{3,1,2,0:T(8,128)(2,1)} fusion(pred[8,49]{0,1:T(8,128)(4,1)S(1)} %copy-done.11, bf16[64,8,3,3]{0,1,3,2:T(8,128)(2,1)S(1)} %copy-done.9, bf16[8,256,1,7,2]{0,3,4,1,2:T(8,128)(2,1)S(1)} %slice.56, bf16[8,256,1,8,49]{0,3,4,1,2:T(8,128)(2,1)} %copy.99), kind=kOutput, calls=%fused_computation.9 | convolution fusion | flops 946716672 | bytes 14517640 | tf_op jit(solution)/shard_map/conv_general_dilated | solution.py:80
  381.7 30.0 %copy.100 = bf16[256,8,49,64]{0,3,2,1:T(8,128)(2,1)} copy(bf16[256,8,49,64]{3,1,2,0:T(8,128)(2,1)} %maximum_convert_fusion.1) | data formatting | bytes 25690112 | tf_op jit(solution)/shard_map/convert_element_type | solution.py:93
  411.8 6.1 slice_bitcast_fusion.1
  417.9 1.9 collective-permute-start.3
  419.9 2.6 collective-permute-start.2
  422.5 3.8 collective-permute-done.2
  426.3 3.3 maximum_bitcast_fusion
  429.7 5.9 pad.12
  435.6 30.8 %copy.102 = bf16[64,256,1,8,49]{0,3,4,1,2:T(8,128)(2,1)} copy(bf16[64,256,1,8,49]{1,0,4,3,2:T(8,128)(2,1)} %bitcast.96) | data formatting | bytes 25690112 | tf_op jit(solution)/shard_map/conv_general_dilated | solution.py:80
  466.4 2.2 slice.60
  468.6 65.0 %maximum_convert_fusion = bf16[256,8,49,64]{3,1,2,0:T(8,128)(2,1)} fusion(pred[8,49]{0,1:T(8,128)(4,1)S(1)} %copy-done.11, bf16[64,64,3,3]{1,0,3,2:T(8,128)(2,1)S(1)} %copy-done.8, bf16[64,256,1,7,4]{0,3,4,1,2:T(8,128)(2,1)S(1)} %slice.60, bf16[64,256,1,8,49]{0,3,4,1,2:T(8,128)(2,1)} %copy.102), kind=kOutput, calls=%fused_computation.8 | convolution fusion | flops 7421165568 | bytes 26681736 | tf_op jit(solution)/shard_map/conv_general_dilated | solution.py:80
  533.5 30.0 %copy.103 = bf16[256,8,49,64]{0,3,2,1:T(8,128)(2,1)} copy(bf16[256,8,49,64]{3,1,2,0:T(8,128)(2,1)} %maximum_convert_fusion) | data formatting | bytes 25690112 | tf_op jit(solution)/shard_map/convert_element_type | solution.py:94
  563.6 6.1 slice_bitcast_fusion
  569.7 4.5 copy-done.2
  574.2 1.9 collective-permute-start.5
  576.2 2.7 collective-permute-start.4
  578.8 3.5 collective-permute-done.4
  582.3 7.0 maximum_bitcast_fusion.1
  589.3 5.7 pad.14
  595.0 30.8 %copy.105 = bf16[64,256,1,8,49]{0,3,4,1,2:T(8,128)(2,1)} copy(bf16[64,256,1,8,49]{1,0,4,3,2:T(8,128)(2,1)} %bitcast.95) | data formatting | bytes 25690112 | tf_op jit(solution)/shard_map/conv_general_dilated | solution.py:80
  625.8 1.5 slice.64
  627.3 64.6 %fusion.12 = bf16[256,8,49,8]{3,1,2,0:T(8,128)(2,1)} fusion(bf16[8,64,3,3]{1,0,3,2:T(8,128)(2,1)S(1)} %copy-done.10, bf16[64,256,1,7,2]{0,3,4,1,2:T(8,128)(2,1)S(1)} %slice.64, bf16[64,256,1,8,49]{0,3,4,1,2:T(8,128)(2,1)} %copy.105), kind=kOutput, calls=%fused_computation.18 | convolution fusion | flops 962543616 | bytes 14918656 | tf_op jit(solution)/shard_map/conv_general_dilated | solution.py:80
  692.0 22.3 %copy.106 = bf16[256,8,49,8]{0,3,2,1:T(8,128)(2,1)S(1)} copy(bf16[256,8,49,8]{3,1,2,0:T(8,128)(2,1)} %fusion.12) | data formatting | bytes 3211264 | tf_op jit(solution)/shard_map/conv_general_dilated | solution.py:80
  715.6 1.1 copy.108
  716.7 1.1 copy.109
  (52 shorter events, 5.5 us)
Async XLA Ops:
  7.2 13.1 %copy-start = (bf16[2,32,64,64]{3,2,1,0:T(8,128)(2,1)S(1)}, bf16[2,32,64,64]{3,2,1,0:T(8,128)(2,1)}, u32[]{:S(2)}) copy-start(bf16[2,32,64,64]{3,2,1,0:T(8,128)(2,1)} %param.10) | copy-start | bytes 1572868
  15.1 59.8 %all-to-all-start.1 = ((bf16[2,8,8,2]{2,3,0,1:T(2,128)(2,1)}), bf16[2,8,8,2]{2,3,0,1:T(2,128)(2,1)S(1)}, u32[]{:S(2)}, u32[]{:S(2)}) async-start(bf16[2,8,8,2]{2,3,0,1:T(2,128)(2,1)} %copy.88), calls=%async_computation.1 | async-start | bytes 16384 | tf_op jit(solution)/shard_map/all_to_all | solution.py:138
  74.9 6.0 copy-start.4
  74.9 6.2 copy-start.5
  74.9 188.3 %all-to-all-start = ((bf16[2,8,8,256,256]{4,2,3,0,1:T(8,128)(2,1)}), bf16[2,8,8,256,256]{4,2,3,0,1:T(8,128)(2,1)}, u32[]{:S(2)}, u32[]{:S(2)}) async-start(bf16[2,8,8,256,256]{4,2,3,0,1:T(8,128)(2,1)} %copy.85), calls=%async_computation | async-start | bytes 33554432 | tf_op jit(solution)/shard_map/all_to_all | solution.py:137
  80.8 233.9 %all-gather.2.cloned.1.call-start = ((), (), s32[]{:S(2)}) async-start(), calls=%async_computation.2 | async-start | bytes 1966080 | tf_op jit(solution)/shard_map/all_gather | solution.py:143
  271.8 3.2 copy-start.7
  317.0 4.6 collective-permute-start.1
  319.7 5.8 collective-permute-start
  325.9 19.5 %copy-start.9 = (bf16[64,8,3,3]{0,1,3,2:T(8,128)(2,1)S(1)}, bf16[64,8,3,3]{0,1,3,2:T(8,128)(2,1)}, u32[]{:S(2)}) copy-start(bf16[64,8,3,3]{0,1,3,2:T(8,128)(2,1)} %param.17) | copy-start | bytes 27652
  325.9 19.5 %copy-start.11 = (pred[8,49]{0,1:T(8,128)(4,1)S(1)}, pred[8,49]{0,1:T(8,128)(4,1)}, u32[]{:S(2)}) copy-start(pred[8,49]{0,1:T(8,128)(4,1)} %constant.106) | copy-start | bytes 1180
  417.9 4.6 collective-permute-start.3
  419.9 6.5 collective-permute-start.2
  435.6 33.0 %copy-start.8 = (bf16[64,64,3,3]{1,0,3,2:T(8,128)(2,1)S(1)}, bf16[64,64,3,3]{1,0,3,2:T(8,128)(2,1)}, u32[]{:S(2)}) copy-start(bf16[64,64,3,3]{1,0,3,2:T(8,128)(2,1)} %param.18) | copy-start | bytes 221188
  569.7 4.5 copy-start.2
  574.2 4.6 collective-permute-start.5
  576.2 6.1 collective-permute-start.4
  595.0 32.3 %copy-start.10 = (bf16[8,64,3,3]{1,0,3,2:T(8,128)(2,1)S(1)}, bf16[8,64,3,3]{1,0,3,2:T(8,128)(2,1)}, u32[]{:S(2)}) copy-start(bf16[8,64,3,3]{1,0,3,2:T(8,128)(2,1)} %param.19) | copy-start | bytes 27652
  692.0 22.3 %copy-start.6 = (pred[8,49]{1,0:T(8,128)(4,1)S(1)}, pred[8,49]{1,0:T(8,128)(4,1)}, u32[]{:S(2)}) copy-start(pred[8,49]{1,0:T(8,128)(4,1)} %constant.71) | copy-start | bytes 1180
  692.0 23.4 %copy-start.3 = (f32[2,256,384]{1,2,0:T(8,128)S(1)}, f32[2,256,384]{1,2,0:T(8,128)}, u32[]{:S(2)}) copy-start(f32[2,256,384]{1,2,0:T(8,128)} %get-tuple-element.11) | copy-start | bytes 2359300
  692.0 25.9 %copy-start.1 = (bf16[2,32,64,64]{3,2,1,0:T(8,128)(2,1)S(1)}, bf16[2,32,64,64]{3,2,1,0:T(8,128)(2,1)}, u32[]{:S(2)}) copy-start(bf16[2,32,64,64]{3,2,1,0:T(8,128)(2,1)} %param.10) | copy-start | bytes 1572868
Sparse Core Ops, SparseCore 0:
  277.1 37.5 all-gather.1
where the time goes:
time: 737 us; the launch traced here: 725 us
  local copies, waits for them, and re-layouts  262 us (36%)
  waiting for transfers between devices  231 us (31%)
  matrix products  177 us (24%)
  starting transfers between devices  23.9 us (3%)
  other arithmetic  16.8 us (2%)
  between operations  14.9 us (2%)
    all_to_all x1, waiting for transfers between devices, body(): lax.all_to_all(pack_slots(panel_set), 'facet', split_axis=1, concat_axis=...  182 us
    conv_general_dilated x3, matrix products, conv_valid(): lax.conv_general_dilated(padded[None], kernel, (1, 1), [(row_pad, row_pad...  166 us
    conv_general_dilated x7, local copies, waits for them, and re-layouts, conv_valid(): lax.conv_general_dilated(padded[None], kernel, (1, 1), [(row_pad, row_pad...  107 us
    all_gather x1, waiting for transfers between devices, body(): spectral_cube = lax.all_gather(denoise_in, 'band', axis=0, tiled=True)  37.7 us
    convert_element_type x2, local copies, waits for them, and re-layouts, denoise(): jnp.maximum(layer_fn(hidden_one, conv_middle, 2), 0.0).astype(jnp.bfloat16)  36.2 us
    convert_element_type x2, local copies, waits for them, and re-layouts, denoise(): jnp.maximum(layer_fn(field, conv_first, 1), 0.0).astype(jnp.bfloat16)  36.2 us
    scatter x3, local copies, waits for them, and re-layouts, fill_one(): return buffer.at[where].set(entries)  26.3 us
    reshape x2, local copies, waits for them, and re-layouts, pack_slots(): filled.reshape((local_subbands, facet_count, capacity) + values.shape[2:])  18.6 us
  transfers between devices with their start and end apart: 9, of which 5 were waited for; matrix products, arithmetic and copies ran while one was open for 8% of the time, Pallas kernels for 0%

commit v1 on v0

v1 whole, which is shorter than its diff:
```python
import jax
import jax.numpy as jnp
from jax import lax
from jax.experimental import pallas as pl
from jax.experimental.pallas import tpu as pltpu
from jax.sharding import PartitionSpec as P

P_SIZE = 256
KW = 8
S = 64
HALF = P_SIZE // 2
CENTRE = (P_SIZE - KW + HALF) // 2
HALO = 4
PAD = 8
GROUP = 8
CH = 64
BF = jnp.bfloat16
F32 = jnp.float32


def params(mib=48):
    return pltpu.CompilerParams(vmem_limit_bytes=mib << 20)


def vmem():
    return pl.BlockSpec(memory_space=pltpu.VMEM)


def smem():
    return pl.BlockSpec(memory_space=pltpu.SMEM)


def pack_blocks(visibility, uv_positions, destinations, column_slots, facets, pairs):
    subs, blocks = visibility.shape[:2]
    vis_rows = subs * pairs * S
    pos_rows = -(-2 * subs * pairs // 16) * 16

    def kernel(dest_ref, slot_ref, vis_ref, pos_ref, out_ref, count_ref, place_ref):
        out_ref[...] = jnp.zeros(out_ref.shape, BF)
        place_ref[...] = jnp.zeros(place_ref.shape, F32)
        for n in range(subs * facets):
            count_ref[n] = 0
        lane = lax.broadcasted_iota(jnp.int32, (1, 2 * S), 1) // S

        def one(n, carry):
            for sub in range(subs):
                facet = dest_ref[sub, n, 0]
                slot = slot_ref[sub, n]
                count = count_ref[sub * facets + facet]
                count_ref[sub * facets + facet] = count + 1
                pair = count // 2
                side = count - 2 * pair
                half_mask = jnp.where(lane == side, 1.0, 0.0).astype(BF)
                block = vis_ref[sub, n]
                wide = jnp.concatenate([block, block], axis=1) * half_mask
                row = pl.multiple_of((sub * pairs + pair) * S, S)
                out_ref[facet, pl.ds(row, S), :] += wide
                where = facet * pos_rows + sub * pairs + pair
                place = pos_ref[sub, n].astype(F32)
                shift = (slot * HALF - CENTRE).astype(F32)
                place_ref[side, pl.ds(where, 1), :] = place[0:1]
                place_ref[side, pl.ds(where + subs * pairs, 1), :] = place[1:2] + shift
            return carry

        lax.fori_loop(0, blocks, one, 0)
        both = jnp.concatenate([place_ref[0], place_ref[1]], axis=1).astype(BF)
        out_ref[:, vis_rows:, :] = both.reshape(facets, pos_rows, 2 * S)

    return pl.pallas_call(
        kernel,
        out_shape=jax.ShapeDtypeStruct((facets, vis_rows + pos_rows, 2 * S), BF),
        in_specs=[smem(), smem(), vmem(), vmem()],
        out_specs=vmem(),
        scratch_shapes=[
            pltpu.SMEM((subs * facets,), jnp.int32),
            pltpu.VMEM((2, facets * pos_rows, S), F32),
        ],
        compiler_params=params(),
        name="pack_blocks",
    )(destinations, column_slots, visibility, uv_positions)


def taps(row, col):
    offset = col - row
    value = jnp.exp(-0.5 * ((offset.astype(F32) - (KW - 1) / 2.0) / (KW / 4.0)) ** 2)
    return jnp.where((offset >= 0) & (offset < KW), value, 0.0).astype(BF)


def contract_last(a, b):
    return lax.dot_general(a, b, (((1,), (1,)), ((), ())), preferred_element_type=F32)


def contract_first(a, b):
    return lax.dot_general(a, b, (((0,), (0,)), ((), ())), preferred_element_type=F32)


def dot(a, b):
    return jnp.dot(a, b, preferred_element_type=F32)


def grid_and_step(received, image, dual, steps, pairs, bands):
    facets = received.shape[0]
    subs, rows, width = image.shape
    vis_rows = subs * pairs * S
    per = 4
    sources = per // pairs
    band_rows = rows // bands
    piece = band_rows + 2 * HALO

    def kernel(step_ref, rec_ref, img_ref, dual_ref, shift_ref, edge_l, edge_r, *rest):
        piece_refs = rest[:bands]
        acc_ref, den_ref = rest[bands:]
        acc_ref[...] = jnp.zeros(acc_ref.shape, F32)
        lane = lax.broadcasted_iota(jnp.int32, (1, 2 * S), 1)
        left = jnp.where(lane < S, 1.0, 0.0).astype(BF)
        right = jnp.where(lane < S, 0.0, 1.0).astype(BF)
        zero = jnp.zeros((2 * S, 2 * S), BF)
        row_id = lax.broadcasted_iota(jnp.int32, (rows, 2 * S), 0).astype(F32)
        col_id = lax.broadcasted_iota(jnp.int32, (width, 2 * S), 0).astype(F32) - CENTRE

        def one(it, carry):
            for sub in range(subs):
                first, second = [], []
                for q in range(per):
                    source = it * sources + q // pairs
                    pair = q % pairs
                    block = rec_ref[source, pl.ds((sub * pairs + pair) * S, S), :]
                    diag = jnp.concatenate([block * left, block * right], axis=0)
                    place = rec_ref[source, vis_rows : vis_rows + 16, :].astype(F32)
                    at = sub * pairs + pair
                    u_row = place[at : at + 1]
                    v_row = place[at + subs * pairs : at + subs * pairs + 1]
                    u_hot = jnp.where(row_id == u_row, 1.0, 0.0).astype(BF)
                    v_hot = jnp.where(col_id == v_row, 1.0, 0.0).astype(BF)
                    first.append((u_hot, diag))
                    second.append(v_hot)
                spread = []
                for q in range(0, per, 2):
                    hot = jnp.concatenate([first[q][0], first[q + 1][0]], axis=1)
                    block = jnp.concatenate(
                        [
                            jnp.concatenate([first[q][1], zero], axis=1),
                            jnp.concatenate([zero, first[q + 1][1]], axis=1),
                        ],
                        axis=0,
                    )
                    spread.append(dot(hot, block).astype(BF))
                acc_ref[sub] += contract_last(
                    jnp.concatenate(spread, axis=1), jnp.concatenate(second, axis=1)
                )
            return carry

        lax.fori_loop(0, facets // sources, one, 0)
        u_taps = taps(
            lax.broadcasted_iota(jnp.int32, (rows, rows), 1),
            lax.broadcasted_iota(jnp.int32, (rows, rows), 0),
        )
        v_taps = taps(
            lax.broadcasted_iota(jnp.int32, (width, width), 0),
            lax.broadcasted_iota(jnp.int32, (width, width), 1),
        )
        den_ref[...] = jnp.zeros(den_ref.shape, F32)
        me = lax.axis_index("band")
        for sub in range(subs):
            total = acc_ref[sub]
            high = total.astype(BF)
            low = (total - high.astype(F32)).astype(BF)
            half = dot(u_taps, high) + dot(u_taps, low)
            gradient = dot(half.astype(BF), v_taps)
            stepped = img_ref[sub] - step_ref[sub] * gradient
            shifted = stepped + dual_ref[sub]
            shift_ref[sub] = shifted
            den_ref[sub, HALO : HALO + rows, :] = shifted
        for k in range(bands):
            start = pl.multiple_of(lax.rem(me + k, bands) * band_rows, band_rows)
            piece_refs[k][...] = jnp.concatenate(
                [den_ref[sub, pl.ds(start, piece), :] for sub in range(subs)], axis=0
            ).astype(BF)
        pick_row = lax.broadcasted_iota(jnp.int32, (subs * HALO, HALF), 0)
        pick_lane = lax.broadcasted_iota(jnp.int32, (subs * HALO, HALF), 1)
        for k in range(bands):
            for ref, at, base in ((edge_l, 0, 0), (edge_r, width - HALF, HALF - HALO)):
                total = None
                for sub in range(subs):
                    pick = jnp.where(
                        (pick_row // HALO == sub) & (pick_lane == base + pick_row % HALO), 1.0, 0.0
                    ).astype(BF)
                    part = den_ref[sub, k * band_rows : k * band_rows + HALF, at : at + HALF].astype(BF)
                    term = contract_last(pick, part)
                    total = term if total is None else total + term
                ref[k] = total.astype(BF)

    edge = jax.ShapeDtypeStruct((bands, subs * HALO, HALF), BF)
    return pl.pallas_call(
        kernel,
        out_shape=[jax.ShapeDtypeStruct(image.shape, F32), edge, edge]
        + [jax.ShapeDtypeStruct((subs * piece, width), BF)] * bands,
        in_specs=[smem(), vmem(), vmem(), vmem()],
        out_specs=[vmem()] * (3 + bands),
        scratch_shapes=[
            pltpu.VMEM((subs, rows, width), F32),
            pltpu.VMEM((subs, (bands - 1) * band_rows + HALF, width), F32),
        ],
        compiler_params=params(),
        name="grid_and_step",
    )(steps, received, image, dual)


def toeplitz(weights, outs, ins):
    w = weights.transpose(3, 2, 1, 0)
    cols = [jnp.pad(w, ((0, 0), (o, ins - 3 - o), (0, 0), (0, 0))) for o in range(outs)]
    return jnp.stack(cols, axis=3)


def weight_matrices(conv_first, conv_middle, conv_last):
    first = toeplitz(conv_first, GROUP, GROUP + 2)
    ci = conv_first.shape[1]
    first = first.reshape(3 * (GROUP + 2) * ci, GROUP // 2, 2, CH)
    first = first.transpose(0, 2, 1, 3).reshape(3 * (GROUP + 2) * ci, GROUP * CH)
    middle = toeplitz(conv_middle, GROUP // 2, GROUP // 2 + 2).reshape(
        3 * (GROUP // 2 + 2) * CH, GROUP // 2 * CH
    )
    last = toeplitz(conv_last, GROUP, GROUP + 2)
    co = conv_last.shape[0]
    last = last.transpose(1, 2, 0, 4, 3).reshape(GROUP + 2, CH, 3 * co * GROUP)
    main = last[:GROUP].reshape(GROUP // 2, 2, CH, -1).transpose(1, 0, 2, 3)
    main = main.reshape(GROUP * CH, 3 * co * GROUP)
    tail = jnp.pad(last[GROUP:], ((0, 0), (0, CH), (0, 0))).reshape(4 * CH, 3 * co * GROUP)
    return first, middle, jnp.concatenate([main, tail], axis=0)


def denoise(pieces, edges, first, middle, last, subs, bands, band_rows, width):
    channels = subs * bands
    piece = band_rows + 2 * HALO
    groups = band_rows // GROUP + 1
    cols = width + 2 * PAD
    lanes = -(-cols // 128) * 128
    tall = -(-(cols + 2 * HALO) // 16) * 16
    in_rows = GROUP + 2
    facets = lax.axis_size("facet")

    def kernel(first_ref, mid_ref, last_ref, *rest):
        piece_refs = rest[:bands]
        edge_refs = rest[bands : 2 * bands]
        out_refs = rest[2 * bands : 3 * bands]
        x_ref, one_ref, two_ref, noise_ref = rest[3 * bands :]
        me = lax.axis_index("band")
        facet = lax.axis_index("facet")
        x_ref[:, piece * channels :, :] = jnp.zeros((lanes // 128, 2 * channels, 128), F32)
        one_ref[groups] = jnp.zeros(one_ref.shape[1:], BF)
        place_row = lax.broadcasted_iota(jnp.int32, (2 * subs * HALO, lanes), 0)
        place_lane = lax.broadcasted_iota(jnp.int32, (2 * subs * HALO, lanes), 1)
        side = place_row // (subs * HALO)
        spot = jnp.where(side == 0, PAD - HALO, PAD + width) + place_row % HALO
        for k in range(bands):
            band = lax.rem(me + bands - k, bands)
            for sub in range(subs):
                put = jnp.where(
                    (place_lane == spot) & (place_row // HALO % subs == sub), 1.0, 0.0
                ).astype(BF)
                halo = contract_first(edge_refs[k][...], put)[:piece]
                own = piece_refs[k][sub * piece : (sub + 1) * piece, :].astype(F32)
                own = jnp.concatenate([own, jnp.zeros((piece, lanes - width), F32)], axis=1)
                own = pltpu.roll(own, PAD, 1) + halo
                for part in range(lanes // 128):
                    x_ref[part, pl.ds(band * subs + sub, piece, stride=channels), :] = own[
                        :, part * 128 : (part + 1) * 128
                    ]

        col = lax.broadcasted_iota(jnp.int32, (1, lanes), 1) - PAD
        inside = ((col >= 0) | (facet > 0)) & ((col < width) | (facet < facets - 1))
        inside = jnp.where(inside, 1.0, 0.0)
        lane_id = lax.broadcasted_iota(jnp.int32, (1, GROUP * CH), 1)
        lane_row = lane_id // (GROUP // 2 * CH) + 2 * (lane_id // CH % (GROUP // 2))

        def layer_one(g, carry):
            top = pl.multiple_of(g * GROUP * channels, GROUP)
            x = jnp.concatenate(
                [x_ref[part, pl.ds(top, in_rows * channels), :] for part in range(lanes // 128)], axis=1
            )
            stack = jnp.concatenate(
                [pltpu.roll(x, 1, 1) * inside, x * inside, pltpu.roll(x, lanes - 1, 1) * inside], axis=0
            )
            stack = stack.astype(BF).T[:cols]
            hidden = dot(stack, first_ref[...])
            row = lane_row + (g * GROUP + 1 - HALO) + me * band_rows
            keep = jnp.where((row >= 0) & (row < band_rows * bands), 1.0, 0.0)
            one_ref[g, 0:cols, :] = (jnp.maximum(hidden, 0.0) * keep).astype(BF)
            return carry

        lax.fori_loop(0, groups, layer_one, 0)
        block = GROUP // 2 * CH

        def layer_two(g, carry):
            row = lane_row + (g * GROUP - 1) + me * band_rows
            keep = jnp.where((row >= 0) & (row < band_rows * bands), 1.0, 0.0)
            for phase in range(2):
                here = one_ref[g, :, phase * block : (phase + 1) * block]
                after = one_ref[g + 1, :, phase * block : phase * block + 2 * CH]
                parts = []
                for t in range(3):
                    parts += [here[2 * t : 2 * t + cols], after[2 * t : 2 * t + cols]]
                hidden = dot(jnp.concatenate(parts, axis=1), mid_ref[...])
                part = keep[:, phase * block : (phase + 1) * block]
                two_ref[g, :, phase * block : (phase + 1) * block] = (
                    jnp.maximum(hidden, 0.0) * part
                ).astype(BF)
            return carry

        lax.fori_loop(0, groups, layer_two, 0)
        out_ch = channels * GROUP
        out_col = lax.broadcasted_iota(jnp.int32, (1, width), 1)
        has_left = jnp.where((out_col > 0) | (facet > 0), 1.0, 0.0)
        has_right = jnp.where((out_col < width - 1) | (facet < facets - 1), 1.0, 0.0)

        def layer_three(g, carry):
            hidden = jnp.concatenate(
                [
                    two_ref[g],
                    two_ref[g + 1, :, 0 : 2 * CH],
                    two_ref[g + 1, :, block : block + 2 * CH],
                ],
                axis=1,
            )
            y = dot(hidden, last_ref[...]).T
            base = PAD - 2
            noise = (
                y[:out_ch, base - 1 : base - 1 + width] * has_left
                + y[out_ch : 2 * out_ch, base : base + width]
                + y[2 * out_ch :, base + 1 : base + 1 + width] * has_right
            )
            noise_ref[:, pl.ds(pl.multiple_of(g * GROUP, GROUP), GROUP), :] = noise.reshape(
                channels, GROUP, width
            )
            return carry

        lax.fori_loop(0, groups - 1, layer_three, 0)
        for k in range(bands):
            band = lax.rem(me + k, bands)
            for sub in range(subs):
                out_refs[k][sub * band_rows : (sub + 1) * band_rows, :] = noise_ref[
                    band * subs + sub
                ].astype(BF)

    return pl.pallas_call(
        kernel,
        out_shape=[jax.ShapeDtypeStruct((subs * band_rows, width), BF)] * bands,
        in_specs=[vmem()] * (3 + 2 * bands),
        out_specs=[vmem()] * bands,
        scratch_shapes=[
            pltpu.VMEM((lanes // 128, (groups * GROUP + 2) * channels, 128), F32),
            pltpu.VMEM((groups + 1, tall, GROUP * CH), BF),
            pltpu.VMEM((groups, cols, GROUP * CH), BF),
            pltpu.VMEM((channels, band_rows, width), F32),
        ],
        compiler_params=params(),
        name="denoise",
    )(first, middle, last, *pieces, *edges)


def finish(shifted, noises, bands):
    subs, rows, width = shifted.shape
    band_rows = rows // bands

    def kernel(shift_ref, *rest):
        noise_refs = rest[:bands]
        img_ref, dual_ref = rest[bands:]
        me = lax.axis_index("band")
        for k in range(bands):
            start = pl.multiple_of(lax.rem(me + bands - k, bands) * band_rows, band_rows)
            for sub in range(subs):
                noise = noise_refs[k][sub * band_rows : (sub + 1) * band_rows, :].astype(F32)
                shifted_part = shift_ref[sub, pl.ds(start, band_rows), :]
                image_next = jnp.maximum(shifted_part - noise, 0.0)
                img_ref[sub, pl.ds(start, band_rows), :] = image_next
                dual_ref[sub, pl.ds(start, band_rows), :] = shifted_part - image_next

    return pl.pallas_call(
        kernel,
        out_shape=[jax.ShapeDtypeStruct(shifted.shape, F32)] * 2,
        in_specs=[vmem()] * (1 + bands),
        out_specs=[vmem()] * 2,
        compiler_params=params(),
        name="finish",
    )(shifted, *noises)


def exchange(parts, bands):
    return [parts[0]] + [
        lax.ppermute(parts[k], "band", [(i, (i + k) % bands) for i in range(bands)])
        for k in range(1, bands)
    ]


def body(
    visibility,
    uv_positions,
    destinations,
    column_slots,
    image_cube,
    dual_cube,
    step_sizes,
    conv_first,
    conv_middle,
    conv_last,
):
    facets = lax.axis_size("facet")
    bands = lax.axis_size("band")
    subs, blocks = visibility.shape[:2]
    rows, width = image_cube.shape[1:]
    pairs = max(2, 2 * blocks // facets) // 2
    packed = pack_blocks(visibility, uv_positions, destinations, column_slots, facets, pairs)
    received = lax.all_to_all(packed, "facet", split_axis=0, concat_axis=0, tiled=True)
    weights = weight_matrices(conv_first, conv_middle, conv_last)
    shifted, edge_l, edge_r, *pieces = grid_and_step(
        received, image_cube, dual_cube, step_sizes, pairs, bands
    )
    from_left = lax.ppermute(edge_r, "facet", [(i, i + 1) for i in range(facets - 1)])
    from_right = lax.ppermute(edge_l, "facet", [(i + 1, i) for i in range(facets - 1)])
    edge = jnp.concatenate([from_left, from_right], axis=1)
    me = lax.axis_index("band")
    edge_parts = [
        lax.dynamic_index_in_dim(edge, (me + k) % bands, 0, keepdims=False) for k in range(bands)
    ]
    pieces = exchange(pieces, bands)
    edges = exchange(edge_parts, bands)
    noises = denoise(pieces, edges, *weights, subs, bands, rows // bands, width)
    return tuple(finish(shifted, exchange(noises, bands), bands))


def solution(mesh):
    return jax.shard_map(
        body,
        mesh=mesh,
        in_specs=(
            P("band", "facet", None, None),
            P("band", "facet", None, None),
            P("band", "facet", None),
            P("band", "facet"),
            P("band", None, "facet"),
            P("band", None, "facet"),
            P("band"),
            P(),
            P(),
            P(),
        ),
        out_specs=(P("band", None, "facet"), P("band", None, "facet")),
        check_vma=False,
    )
```

time: 737 us -> 93.6 us (0.13)
  the two profiles are of different devices: /device:TPU:4 before, /device:TPU:0 now
where the time goes in v1:
time: 93.6 us; the launch traced here: 92.9 us
  Pallas kernels  30 us (32%)
  starting transfers between devices  20.9 us (22%)
  local copies, waits for them, and re-layouts  20 us (21%)
  waiting for transfers between devices  19.6 us (21%)
  other arithmetic  1.43 us (2%)
    pallas_call x1, Pallas kernels, denoise(): pl.pallas_call(kernel, out_shape=[jax.ShapeDtypeStruct((subs * band_rows,...  16.2 us
    ppermute x9, starting transfers between devices, exchange(): lax.ppermute(parts[k], 'band', [(i, (i + k) % bands) for i in range(bands)])  13.1 us
    all_to_all x1, waiting for transfers between devices, body(): lax.all_to_all(packed, 'facet', split_axis=0, concat_axis=0, tiled=True)  9.92 us
    unnamed x37, local copies, waits for them, and re-layouts  9.41 us
    pallas_call x1, Pallas kernels, grid_and_step(): pl.pallas_call(kernel, out_shape=[jax.ShapeDtypeStruct(image.shape, F32),...  7.7 us
    ppermute x9, waiting for transfers between devices, exchange(): lax.ppermute(parts[k], 'band', [(i, (i + k) % bands) for i in range(bands)])  7.22 us
    all_to_all x1, starting transfers between devices, body(): lax.all_to_all(packed, 'facet', split_axis=0, concat_axis=0, tiled=True)  5.3 us
    pallas_call x1, Pallas kernels, pack_blocks(): pl.pallas_call(kernel, out_shape=jax.ShapeDtypeStruct((facets, vis_rows +...  4.86 us
  transfers between devices with their start and end apart: 12, of which 4 were waited for; matrix products, arithmetic and copies ran while one was open for 18% of the time, Pallas kernels for 0%

profile of v1, /device:TPU:0, one launch (start us, length us, event | category | flops | bytes accessed | tf_op | source)
XLA Modules:
  0.0 92.9 jit_solution(5434936921860336263)
XLA Ops:
  0.6 0.8 copy.14.dest_ref
  1.4 1.2 %copy-done = bf16[2,32,64,64]{3,2,1,0:T(8,128)(2,1)S(1)} copy-done((bf16[2,32,64,64]{3,2,1,0:T(8,128)(2,1)S(1)}, bf16[2,32,64,64]{3,2,1,0:T(8,128)(2,1)}, u32[]{:S(2)}) %copy-start) | copy-done | bytes 524312
  2.6 0.8 copy-done.3
  3.5 0.7 copy-done.4
  4.1 4.9 %pack_blocks.1 = bf16[8,528,128]{2,1,0:T(8,128)(2,1)} custom-call(s32[2,32,1]{2,1,0:T(8,128)S(1)} %copy.14.dest_ref, s32[2,32]{1,0:T(2,128)S(1)} %copy-done.4, bf16[2,32,64,64]{3,2,1,0:T(8,128)(2,1)S(1)} %copy-done, s32[2,32,2,64]{3,2,1,0:T(2,128)S(1)} %copy-done.3), custom_call_target="tpu_custom_call" | custom-call | tf_op jit(solution)/shard_map/pack_blocks/pallas_call | solution.py:69
  9.0 5.3 %all-to-all-start = ((bf16[8,528,128]{2,1,0:T(8,128)(2,1)}), bf16[8,528,128]{2,1,0:T(8,128)(2,1)S(1)}, u32[]{:S(2)}, u32[]{:S(2)}) async-start(bf16[8,528,128]{2,1,0:T(8,128)(2,1)} %pack_blocks.1), calls=%async_computation | async-start | bytes 2162688 | tf_op jit(solution)/shard_map/all_to_all | solution.py:413
  14.6 0.0 copy-start.8
  14.6 0.1 copy.23
  14.7 0.3 copy.18
  15.0 0.0 copy-start.9
  15.0 0.2 copy.19
  15.2 0.1 copy-done.8
  15.3 0.6 bitcast_dynamic-update-slice_fusion.15
  15.9 0.6 bitcast_dynamic-update-slice_fusion.14
  16.6 0.6 bitcast_dynamic-update-slice_fusion.13
  17.2 0.6 bitcast_dynamic-update-slice_fusion.12
  17.8 0.6 bitcast_dynamic-update-slice_fusion.11
  18.5 0.1 pad_maximum_fusion.1.last_ref
  18.5 0.2 pad_bitcast_fusion.3
  18.8 0.0 copy-start.5
  18.8 1.4 %pad_maximum_fusion = bf16[3,6,64,4,64]{2,4,0,1,3:T(8,128)(2,1)} fusion(bf16[3,6,64,1,64]{2,4,0,1,3:T(8,128)(2,1)S(1)} %get-tuple-element.25, bf16[3,6,64,1,64]{2,4,0,1,3:T(8,128)(2,1)S(1)} %get-tuple-element.26, bf16[3,6,64,1,64]{2,4,0,1,3:T(8,128)(2,1)S(1)} %get-tuple-element.27, bf16[3,6,64,1,64]{2,4,0,1,3:T(8,128)(2,1)S(1)} %get-tuple-element.24), kind=kLoop, calls=%fused_computation | loop fusion | flops 884736 | bytes 1179648 | tf_op jit(solution)/shard_map/stack | solution.py:212
  20.1 9.9 %all-to-all-done.rec_ref = bf16[8,528,128]{2,1,0:T(8,128)(2,1)S(1)} async-done(((bf16[8,528,128]{2,1,0:T(8,128)(2,1)}), bf16[8,528,128]{2,1,0:T(8,128)(2,1)S(1)}, u32[]{:S(2)}, u32[]{:S(2)}) %all-to-all-start) | async-done | bytes 1081376 | tf_op jit(solution)/shard_map/all_to_all | solution.py:413
  30.1 1.1 %copy-done.2 = f32[2,256,384]{2,1,0:T(8,128)S(1)} copy-done((f32[2,256,384]{2,1,0:T(8,128)S(1)}, f32[2,256,384]{2,1,0:T(8,128)}, u32[]{:S(2)}) %copy-start.2) | copy-done | bytes 786456
  31.2 7.7 %grid_and_step.1 = (f32[2,256,384]{2,1,0:T(8,128)S(1)}, bf16[4,8,128]{2,1,0:T(8,128)(2,1)S(1)}, bf16[4,8,128]{2,1,0:T(8,128)(2,1)S(1)}, bf16[144,384]{1,0:T(8,12...) custom-call(f32[2]{0:T(128)S(1)} %copy-done.5, ...), custom_call_target="tpu_custom_call" | custom-call | tf_op jit(solution)/shard_map/grid_and_step/pallas_call | solution.py:194
  38.9 1.3 %collective-permute-start.3 = (bf16[4,8,128]{2,1,0:T(8,128)(2,1)S(1)}, bf16[4,8,128]{2,1,0:T(8,128)(2,1)S(1)}, u32[]{:S(2)}, u32[]{:S(2)}) collective-permute-start(bf16[4,8,128]{2,1,0:T(8,128)(2,1)S(1)} %get-tuple-element.18), channel_id=1, source_target_pairs={{0,4},{4,8},{8,12},{12,16},{16,20},{20,24},{24,28},{1,5},{5,9},{9,... | collective-permute-start | bytes 24584 | tf_op jit(solution)/shard_map/ppermute | solution.py:418
  40.2 0.6 bitcast_dynamic-update-slice_fusion.10
  40.9 1.3 %collective-permute-start.4 = (bf16[4,8,128]{2,1,0:T(8,128)(2,1)S(1)}, bf16[4,8,128]{2,1,0:T(8,128)(2,1)S(1)}, u32[]{:S(2)}, u32[]{:S(2)}) collective-permute-start(bf16[4,8,128]{2,1,0:T(8,128)(2,1)S(1)} %get-tuple-element.19), channel_id=1, source_target_pairs={{4,0},{8,4},{12,8},{16,12},{20,16},{24,20},{28,24},{5,1},{9,5},{13... | collective-permute-start | bytes 24584 | tf_op jit(solution)/shard_map/ppermute | solution.py:419
  42.2 2.5 %collective-permute-done.4 = bf16[4,8,128]{2,1,0:T(8,128)(2,1)S(1)} collective-permute-done((bf16[4,8,128]{2,1,0:T(8,128)(2,1)S(1)}, bf16[4,8,128]{2,1,0:T(8,128)(2,1)S(1)}, u32[]{:S(2)}, u32[]{:S(2)}) %collective-permute-start.4) | collective-permute-done | bytes 8224 | tf_op jit(solution)/shard_map/ppermute | solution.py:419
  44.7 1.6 %collective-permute-start.5 = (bf16[16,128]{1,0:T(8,128)(2,1)S(1)}, bf16[16,128]{1,0:T(8,128)(2,1)S(1)}, u32[]{:S(2)}, u32[]{:S(2)}) collective-permute-start(bf16[16,128]{1,0:T(8,128)(2,1)S(1)} %get-tuple-element.30), channel_id=1, source_target_pairs={{0,1},{1,2},{2,3},{3,0},{4,5},{5,6},{6,7},{7,4},{8,9},{9,10},{10,1... | collective-permute-start | bytes 12296 | tf_op jit(solution)/shard_map/ppermute | solution.py:390
  46.3 0.6 bitcast_dynamic-update-slice_fusion.9
  46.9 1.6 %collective-permute-start = (bf16[144,384]{1,0:T(8,128)(2,1)S(1)}, bf16[144,384]{1,0:T(8,128)(2,1)S(1)}, u32[]{:S(2)}, u32[]{:S(2)}) collective-permute-start(bf16[144,384]{1,0:T(8,128)(2,1)S(1)} %get-tuple-element.15), channel_id=1, source_target_pairs={{0,1},{1,2},{2,3},{3,0},{4,5},{5,6},{6,7},{7,4},{8,9},{9,10},{10,1... | collective-permute-start | bytes 331784 | tf_op jit(solution)/shard_map/ppermute | solution.py:390
  48.5 1.2 %collective-permute-start.1 = (bf16[144,384]{1,0:T(8,128)(2,1)S(1)}, bf16[144,384]{1,0:T(8,128)(2,1)S(1)}, u32[]{:S(2)}, u32[]{:S(2)}) collective-permute-start(bf16[144,384]{1,0:T(8,128)(2,1)S(1)} %get-tuple-element.16), channel_id=1, source_target_pairs={{0,2},{1,3},{2,0},{3,1},{4,6},{5,7},{6,4},{7,5},{8,10},{9,11},{10,... | collective-permute-start | bytes 331784 | tf_op jit(solution)/shard_map/ppermute | solution.py:390
  49.7 2.7 %collective-permute-start.2 = (bf16[144,384]{1,0:T(8,128)(2,1)S(1)}, bf16[144,384]{1,0:T(8,128)(2,1)S(1)}, u32[]{:S(2)}, u32[]{:S(2)}) collective-permute-start(bf16[144,384]{1,0:T(8,128)(2,1)S(1)} %get-tuple-element.17), channel_id=1, source_target_pairs={{0,3},{1,0},{2,1},{3,2},{4,7},{5,4},{6,5},{7,6},{8,11},{9,8},{10,9... | collective-permute-start | bytes 331784 | tf_op jit(solution)/shard_map/ppermute | solution.py:390
  52.5 0.3 collective-permute-start.6
  52.8 1.3 %collective-permute-start.7 = (bf16[16,128]{1,0:T(8,128)(2,1)S(1)}, bf16[16,128]{1,0:T(8,128)(2,1)S(1)}, u32[]{:S(2)}, u32[]{:S(2)}) collective-permute-start(bf16[16,128]{1,0:T(8,128)(2,1)S(1)} %get-tuple-element.28), channel_id=1, source_target_pairs={{0,3},{1,0},{2,1},{3,2},{4,7},{5,4},{6,5},{7,6},{8,11},{9,8},{10,9... | collective-permute-start | bytes 12296 | tf_op jit(solution)/shard_map/ppermute | solution.py:390
  54.1 0.6 bitcast_dynamic-update-slice_fusion.8
  54.8 1.9 %copy.15 = bf16[3,10,8,8,64]{4,2,1,0,3:T(8,128)(2,1)} copy(bf16[3,10,8,8,64]{4,2,0,1,3:T(8,128)(2,1)} %bitcast_dynamic-update-slice_fusion.8) | data formatting | bytes 491520 | tf_op jit(solution)/shard_map/stack | solution.py:212
  56.7 1.9 %copy.16 = bf16[240,2,4,64]{0,3,2,1:T(8,128)(2,1)} copy(bf16[240,2,4,64]{3,0,1,2:T(8,128)(2,1)} %bitcast.62) | data formatting | bytes 491520 | tf_op jit(solution)/shard_map/transpose | solution.py:219
  58.6 1.1 %copy.22.first_ref = bf16[240,512]{1,0:T(8,128)(2,1)S(1)} copy(bf16[240,512]{0,1:T(8,128)(2,1)} %bitcast.81) | data formatting | bytes 491520 | tf_op jit(solution)/shard_map/reshape | solution.py:219
  59.7 2.0 %copy.17 = bf16[3,6,64,4,64]{4,3,2,1,0:T(4,128)(2,1)} copy(bf16[3,6,64,4,64]{2,4,0,1,3:T(8,128)(2,1)S(1)} %copy-done.6) | data formatting | bytes 1179648 | tf_op jit(solution)/shard_map/stack | solution.py:212
  61.7 2.2 %reshape.28.mid_ref = bf16[1152,256]{1,0:T(8,128)(2,1)S(1)} reshape(bf16[3,6,64,4,64]{4,3,2,1,0:T(4,128)(2,1)} %copy.17) | data formatting | bytes 1179648 | tf_op jit(solution)/shard_map/reshape | solution.py:220
  64.0 16.2 %denoise.1 = (bf16[128,384]{1,0:T(8,128)(2,1)S(1)}, bf16[128,384]{1,0:T(8,128)(2,1)S(1)}, bf16[128,384]{1,0:T(8,128)(2,1)S(1)}, bf16[128,384]{1,0:T(8,128)(2,1)S(1)}) custom-call(bf16[240,512]{1,0:T(8,128)(2,1)S(1)} %copy.22.first_ref, bf16[1152,256]{1,0:T(8,128)(2,1)S(1)} %reshape.28.mid_ref, bf16[768,192]{1,0:T(8,128)(2,1)S(1)} %pad_maximum_fusion.1.last_ref, ...), custom_call_target="tpu_custom_call" | custom-call | tf_op jit(solution)/shard_map/denoise/pallas_call | solution.py:345
  80.2 0.7 collective-permute-start.8
  80.9 2.6 %collective-permute-start.9 = (bf16[128,384]{1,0:T(8,128)(2,1)S(1)}, bf16[128,384]{1,0:T(8,128)(2,1)S(1)}, u32[]{:S(2)}, u32[]{:S(2)}) collective-permute-start(bf16[128,384]{1,0:T(8,128)(2,1)S(1)} %get-tuple-element.22), channel_id=1, source_target_pairs={{0,2},{1,3},{2,0},{3,1},{4,6},{5,7},{6,4},{7,5},{8,10},{9,11},{10,... | collective-permute-start | bytes 294920 | tf_op jit(solution)/shard_map/ppermute | solution.py:390
  83.5 0.9 collective-permute-start.10
  84.4 3.4 %collective-permute-done.8.rest_1_ = bf16[128,384]{1,0:T(8,128)(2,1)S(1)} collective-permute-done((bf16[128,384]{1,0:T(8,128)(2,1)S(1)}, bf16[128,384]{1,0:T(8,128)(2,1)S(1)}, u32[]{:S(2)}, u32[]{:S(2)}) %collective-permute-start.8) | collective-permute-done | bytes 98336 | tf_op jit(solution)/shard_map/ppermute | solution.py:390
  87.8 3.8 %collective-permute-done.9.rest_2_ = bf16[128,384]{1,0:T(8,128)(2,1)S(1)} collective-permute-done((bf16[128,384]{1,0:T(8,128)(2,1)S(1)}, bf16[128,384]{1,0:T(8,128)(2,1)S(1)}, u32[]{:S(2)}, u32[]{:S(2)}) %collective-permute-start.9) | collective-permute-done | bytes 98336 | tf_op jit(solution)/shard_map/ppermute | solution.py:390
  91.6 1.3 %finish.1 = (f32[2,256,384]{2,1,0:T(8,128)}, f32[2,256,384]{2,1,0:T(8,128)}) custom-call(f32[2,256,384]{2,1,0:T(8,128)S(1)} %get-tuple-element.13.shift_ref, bf16[128,384]{1,0:T(8,128)(2,1)S(1)} %get-tuple-element.20.rest_0_, bf16[128,384]{1,0:T(8,128)(2,1)S(1)} %collective-permute-done.8.rest_1_, bf16[128,384]{1,0:T(8,128)(2,1)S(1)} %collective-permute-done.9.rest_2_, ...), custom_call_target="tpu_custom_call" | custom-call | tf_op jit(solution)/shard_map/finish/pallas_call | solution.py:378
  (35 shorter events, 0.3 us)
Async XLA Ops:
  1.4 1.2 %copy-start = (bf16[2,32,64,64]{3,2,1,0:T(8,128)(2,1)S(1)}, bf16[2,32,64,64]{3,2,1,0:T(8,128)(2,1)}, u32[]{:S(2)}) copy-start(bf16[2,32,64,64]{3,2,1,0:T(8,128)(2,1)} %vis_ref.1) | copy-start | bytes 1572868
  2.6 0.8 copy-start.3
  3.5 0.7 copy-start.4
  9.0 5.3 %copy-start.7 = (bf16[8,64,3,3]{1,0,3,2:T(8,128)(2,1)S(1)}, bf16[8,64,3,3]{1,0,3,2:T(8,128)(2,1)}, u32[]{:S(2)}) copy-start(bf16[8,64,3,3]{1,0,3,2:T(8,128)(2,1)} %param.19) | copy-start | bytes 27652
  9.0 21.1 %all-to-all-start = ((bf16[8,528,128]{2,1,0:T(8,128)(2,1)}), bf16[8,528,128]{2,1,0:T(8,128)(2,1)S(1)}, u32[]{:S(2)}, u32[]{:S(2)}) async-start(bf16[8,528,128]{2,1,0:T(8,128)(2,1)} %pack_blocks.1), calls=%async_computation | async-start | bytes 2162688 | tf_op jit(solution)/shard_map/all_to_all | solution.py:413
  14.6 0.7 copy-start.8
  15.0 3.5 %copy-start.9 = (bf16[64,64,3,3]{1,0,3,2:T(8,128)(2,1)S(1)}, bf16[64,64,3,3]{1,0,3,2:T(8,128)(2,1)}, u32[]{:S(2)}) copy-start(bf16[64,64,3,3]{1,0,3,2:T(8,128)(2,1)} %param.18) | copy-start | bytes 221188
  18.8 11.3 %copy-start.1 = (f32[2,256,384]{2,1,0:T(8,128)S(1)}, f32[2,256,384]{2,1,0:T(8,128)}, u32[]{:S(2)}) copy-start(f32[2,256,384]{2,1,0:T(8,128)} %img_ref.1) | copy-start | bytes 2359300
  18.8 11.3 %copy-start.5 = (f32[2]{0:T(128)S(1)}, f32[2]{0:T(128)}, u32[]{:S(2)}) copy-start(f32[2]{0:T(128)} %step_ref.1) | copy-start | bytes 28
  30.1 1.1 %copy-start.2 = (f32[2,256,384]{2,1,0:T(8,128)S(1)}, f32[2,256,384]{2,1,0:T(8,128)}, u32[]{:S(2)}) copy-start(f32[2,256,384]{2,1,0:T(8,128)} %dual_ref.1) | copy-start | bytes 2359300
  38.9 3.2 %collective-permute-start.3 = (bf16[4,8,128]{2,1,0:T(8,128)(2,1)S(1)}, bf16[4,8,128]{2,1,0:T(8,128)(2,1)S(1)}, u32[]{:S(2)}, u32[]{:S(2)}) collective-permute-start(bf16[4,8,128]{2,1,0:T(8,128)(2,1)S(1)} %get-tuple-element.18), channel_id=1, source_target_pairs={{0,4},{4,8},{8,12},{12,16},{16,20},{20,24},{24,28},{1,5},{5,9},{9,... | collective-permute-start | bytes 24584 | tf_op jit(solution)/shard_map/ppermute | solution.py:418
  40.9 3.8 %collective-permute-start.4 = (bf16[4,8,128]{2,1,0:T(8,128)(2,1)S(1)}, bf16[4,8,128]{2,1,0:T(8,128)(2,1)S(1)}, u32[]{:S(2)}, u32[]{:S(2)}) collective-permute-start(bf16[4,8,128]{2,1,0:T(8,128)(2,1)S(1)} %get-tuple-element.19), channel_id=1, source_target_pairs={{4,0},{8,4},{12,8},{16,12},{20,16},{24,20},{28,24},{5,1},{9,5},{13... | collective-permute-start | bytes 24584 | tf_op jit(solution)/shard_map/ppermute | solution.py:419
  44.7 8.1 %collective-permute-start.5 = (bf16[16,128]{1,0:T(8,128)(2,1)S(1)}, bf16[16,128]{1,0:T(8,128)(2,1)S(1)}, u32[]{:S(2)}, u32[]{:S(2)}) collective-permute-start(bf16[16,128]{1,0:T(8,128)(2,1)S(1)} %get-tuple-element.30), channel_id=1, source_target_pairs={{0,1},{1,2},{2,3},{3,0},{4,5},{5,6},{6,7},{7,4},{8,9},{9,10},{10,1... | collective-permute-start | bytes 12296 | tf_op jit(solution)/shard_map/ppermute | solution.py:390
  46.9 12.7 %copy-start.6 = (bf16[3,6,64,4,64]{2,4,0,1,3:T(8,128)(2,1)S(1)}, bf16[3,6,64,4,64]{2,4,0,1,3:T(8,128)(2,1)}, u32[]{:S(2)}) copy-start(bf16[3,6,64,4,64]{2,4,0,1,3:T(8,128)(2,1)} %pad_maximum_fusion) | copy-start | bytes 1769476
  46.9 17.0 %collective-permute-start = (bf16[144,384]{1,0:T(8,128)(2,1)S(1)}, bf16[144,384]{1,0:T(8,128)(2,1)S(1)}, u32[]{:S(2)}, u32[]{:S(2)}) collective-permute-start(bf16[144,384]{1,0:T(8,128)(2,1)S(1)} %get-tuple-element.15), channel_id=1, source_target_pairs={{0,1},{1,2},{2,3},{3,0},{4,5},{5,6},{6,7},{7,4},{8,9},{9,10},{10,1... | collective-permute-start | bytes 331784 | tf_op jit(solution)/shard_map/ppermute | solution.py:390
  48.5 15.4 %collective-permute-start.1 = (bf16[144,384]{1,0:T(8,128)(2,1)S(1)}, bf16[144,384]{1,0:T(8,128)(2,1)S(1)}, u32[]{:S(2)}, u32[]{:S(2)}) collective-permute-start(bf16[144,384]{1,0:T(8,128)(2,1)S(1)} %get-tuple-element.16), channel_id=1, source_target_pairs={{0,2},{1,3},{2,0},{3,1},{4,6},{5,7},{6,4},{7,5},{8,10},{9,11},{10,... | collective-permute-start | bytes 331784 | tf_op jit(solution)/shard_map/ppermute | solution.py:390
  49.7 14.2 %collective-permute-start.2 = (bf16[144,384]{1,0:T(8,128)(2,1)S(1)}, bf16[144,384]{1,0:T(8,128)(2,1)S(1)}, u32[]{:S(2)}, u32[]{:S(2)}) collective-permute-start(bf16[144,384]{1,0:T(8,128)(2,1)S(1)} %get-tuple-element.17), channel_id=1, source_target_pairs={{0,3},{1,0},{2,1},{3,2},{4,7},{5,4},{6,5},{7,6},{8,11},{9,8},{10,9... | collective-permute-start | bytes 331784 | tf_op jit(solution)/shard_map/ppermute | solution.py:390
  52.5 11.5 %collective-permute-start.6 = (bf16[16,128]{1,0:T(8,128)(2,1)S(1)}, bf16[16,128]{1,0:T(8,128)(2,1)S(1)}, u32[]{:S(2)}, u32[]{:S(2)}) collective-permute-start(bf16[16,128]{1,0:T(8,128)(2,1)S(1)} %get-tuple-element.29), channel_id=1, source_target_pairs={{0,2},{1,3},{2,0},{3,1},{4,6},{5,7},{6,4},{7,5},{8,10},{9,11},{10,... | collective-permute-start | bytes 12296 | tf_op jit(solution)/shard_map/ppermute | solution.py:390
  52.8 11.1 %collective-permute-start.7 = (bf16[16,128]{1,0:T(8,128)(2,1)S(1)}, bf16[16,128]{1,0:T(8,128)(2,1)S(1)}, u32[]{:S(2)}, u32[]{:S(2)}) collective-permute-start(bf16[16,128]{1,0:T(8,128)(2,1)S(1)} %get-tuple-element.28), channel_id=1, source_target_pairs={{0,3},{1,0},{2,1},{3,2},{4,7},{5,4},{6,5},{7,6},{8,11},{9,8},{10,9... | collective-permute-start | bytes 12296 | tf_op jit(solution)/shard_map/ppermute | solution.py:390
  80.2 7.6 %collective-permute-start.8 = (bf16[128,384]{1,0:T(8,128)(2,1)S(1)}, bf16[128,384]{1,0:T(8,128)(2,1)S(1)}, u32[]{:S(2)}, u32[]{:S(2)}) collective-permute-start(bf16[128,384]{1,0:T(8,128)(2,1)S(1)} %get-tuple-element.21), channel_id=1, source_target_pairs={{0,1},{1,2},{2,3},{3,0},{4,5},{5,6},{6,7},{7,4},{8,9},{9,10},{10,1... | collective-permute-start | bytes 294920 | tf_op jit(solution)/shard_map/ppermute | solution.py:390
  80.9 10.7 %collective-permute-start.9 = (bf16[128,384]{1,0:T(8,128)(2,1)S(1)}, bf16[128,384]{1,0:T(8,128)(2,1)S(1)}, u32[]{:S(2)}, u32[]{:S(2)}) collective-permute-start(bf16[128,384]{1,0:T(8,128)(2,1)S(1)} %get-tuple-element.22), channel_id=1, source_target_pairs={{0,2},{1,3},{2,0},{3,1},{4,6},{5,7},{6,4},{7,5},{8,10},{9,11},{10,... | collective-permute-start | bytes 294920 | tf_op jit(solution)/shard_map/ppermute | solution.py:390
  83.5 8.1 %collective-permute-start.10 = (bf16[128,384]{1,0:T(8,128)(2,1)S(1)}, bf16[128,384]{1,0:T(8,128)(2,1)S(1)}, u32[]{:S(2)}, u32[]{:S(2)}) collective-permute-start(bf16[128,384]{1,0:T(8,128)(2,1)S(1)} %get-tuple-element.23), channel_id=1, source_target_pairs={{0,3},{1,0},{2,1},{3,2},{4,7},{5,4},{6,5},{7,6},{8,11},{9,8},{10,9... | collective-permute-start | bytes 294920 | tf_op jit(solution)/shard_map/ppermute | solution.py:390

commit v2 on v1

--- a/solution.py
+++ b/solution.py
@@ -14,11 +14,12 @@
 PAD = 8
 GROUP = 8
 CH = 64
+CHUNKS = 4
 BF = jnp.bfloat16
 F32 = jnp.float32
 
 
-def params(mib=48):
+def params(mib=24):
     return pltpu.CompilerParams(vmem_limit_bytes=mib << 20)
 
 
@@ -35,26 +36,41 @@
     vis_rows = subs * pairs * S
     pos_rows = -(-2 * subs * pairs // 16) * 16
 
-    def kernel(dest_ref, slot_ref, vis_ref, pos_ref, out_ref, count_ref, place_ref):
-        out_ref[...] = jnp.zeros(out_ref.shape, BF)
+    chunk = blocks // CHUNKS
+
+    def kernel(
+        dest_hbm, slot_hbm, vis_hbm, pos_hbm, out_ref,
+        dest_ref, slot_ref, vis_ref, pos_ref, count_ref, place_ref, side_ref, sems,
+    ):
+        small = [
+            pltpu.make_async_copy(dest_hbm, dest_ref, sems.at[CHUNKS]),
+            pltpu.make_async_copy(slot_hbm, slot_ref, sems.at[CHUNKS + 1]),
+            pltpu.make_async_copy(pos_hbm, pos_ref, sems.at[CHUNKS + 2]),
+        ]
+        large = [
+            pltpu.make_async_copy(
+                vis_hbm.at[:, pl.ds(c * chunk, chunk)], vis_ref.at[:, pl.ds(c * chunk, chunk)], sems.at[c]
+            )
+            for c in range(CHUNKS)
+        ]
+        for copy in small + large:
+            copy.start()
+        side_ref[...] = jnp.zeros(side_ref.shape, BF)
         place_ref[...] = jnp.zeros(place_ref.shape, F32)
         for n in range(subs * facets):
             count_ref[n] = 0
-        lane = lax.broadcasted_iota(jnp.int32, (1, 2 * S), 1) // S
+        for copy in small:
+            copy.wait()
 
         def one(n, carry):
             for sub in range(subs):
-                facet = dest_ref[sub, n, 0]
+                facet = dest_ref[sub, n]
                 slot = slot_ref[sub, n]
                 count = count_ref[sub * facets + facet]
                 count_ref[sub * facets + facet] = count + 1
                 pair = count // 2
                 side = count - 2 * pair
-                half_mask = jnp.where(lane == side, 1.0, 0.0).astype(BF)
-                block = vis_ref[sub, n]
-                wide = jnp.concatenate([block, block], axis=1) * half_mask
-                row = pl.multiple_of((sub * pairs + pair) * S, S)
-                out_ref[facet, pl.ds(row, S), :] += wide
+                side_ref[side, facet, sub * pairs + pair] = vis_ref[sub, n]
                 where = facet * pos_rows + sub * pairs + pair
                 place = pos_ref[sub, n].astype(F32)
                 shift = (slot * HALF - CENTRE).astype(F32)
@@ -62,22 +78,34 @@
                 place_ref[side, pl.ds(where + subs * pairs, 1), :] = place[1:2] + shift
             return carry
 
-        lax.fori_loop(0, blocks, one, 0)
+        for c in range(CHUNKS):
+            large[c].wait()
+            lax.fori_loop(c * chunk, (c + 1) * chunk, one, 0, unroll=4)
+        for facet in range(facets):
+            both = jnp.concatenate([side_ref[0, facet], side_ref[1, facet]], axis=2)
+            out_ref[facet, :vis_rows, :] = both.reshape(vis_rows, 2 * S)
         both = jnp.concatenate([place_ref[0], place_ref[1]], axis=1).astype(BF)
         out_ref[:, vis_rows:, :] = both.reshape(facets, pos_rows, 2 * S)
 
+    hbm = pl.BlockSpec(memory_space=pltpu.HBM)
     return pl.pallas_call(
         kernel,
         out_shape=jax.ShapeDtypeStruct((facets, vis_rows + pos_rows, 2 * S), BF),
-        in_specs=[smem(), smem(), vmem(), vmem()],
+        in_specs=[hbm] * 4,
         out_specs=vmem(),
         scratch_shapes=[
+            pltpu.SMEM((subs, blocks), jnp.int32),
+            pltpu.SMEM((subs, blocks), jnp.int32),
+            pltpu.VMEM((subs, blocks, S, S), BF),
+            pltpu.VMEM((subs, blocks, 2, S), jnp.int32),
             pltpu.SMEM((subs * facets,), jnp.int32),
             pltpu.VMEM((2, facets * pos_rows, S), F32),
+            pltpu.VMEM((2, facets, subs * pairs, S, S), BF),
+            pltpu.SemaphoreType.DMA((CHUNKS + 3,)),
         ],
-        compiler_params=params(),
+        compiler_params=params(60),
         name="pack_blocks",
-    )(destinations, column_slots, visibility, uv_positions)
+    )(destinations[..., 0], column_slots, visibility, uv_positions)
 
 
 def taps(row, col):
@@ -109,29 +137,29 @@
 
     def kernel(step_ref, rec_ref, img_ref, dual_ref, shift_ref, edge_l, edge_r, *rest):
         piece_refs = rest[:bands]
-        acc_ref, den_ref = rest[bands:]
-        acc_ref[...] = jnp.zeros(acc_ref.shape, F32)
+        place_ref, acc_ref, den_ref = rest[bands:]
+        place_ref[...] = rec_ref[:, vis_rows:, :].astype(F32)
+        one = jnp.ones((), BF)
+        none = jnp.zeros((), BF)
         lane = lax.broadcasted_iota(jnp.int32, (1, 2 * S), 1)
         left = jnp.where(lane < S, 1.0, 0.0).astype(BF)
         right = jnp.where(lane < S, 0.0, 1.0).astype(BF)
         zero = jnp.zeros((2 * S, 2 * S), BF)
-        row_id = lax.broadcasted_iota(jnp.int32, (rows, 2 * S), 0).astype(F32)
-        col_id = lax.broadcasted_iota(jnp.int32, (width, 2 * S), 0).astype(F32) - CENTRE
-
-        def one(it, carry):
+        row_id = lax.broadcasted_iota(jnp.int32, (rows, 2 * S), 0).astype(F32).astype(BF)
+        col_id = (lax.broadcasted_iota(jnp.int32, (width, 2 * S), 0) - CENTRE).astype(F32).astype(BF)
+
+        for it in range(facets // sources):
             for sub in range(subs):
                 first, second = [], []
                 for q in range(per):
                     source = it * sources + q // pairs
-                    pair = q % pairs
-                    block = rec_ref[source, pl.ds((sub * pairs + pair) * S, S), :]
+                    at = sub * pairs + q % pairs
+                    block = rec_ref[source, at * S : (at + 1) * S, :]
                     diag = jnp.concatenate([block * left, block * right], axis=0)
-                    place = rec_ref[source, vis_rows : vis_rows + 16, :].astype(F32)
-                    at = sub * pairs + pair
-                    u_row = place[at : at + 1]
-                    v_row = place[at + subs * pairs : at + subs * pairs + 1]
-                    u_hot = jnp.where(row_id == u_row, 1.0, 0.0).astype(BF)
-                    v_hot = jnp.where(col_id == v_row, 1.0, 0.0).astype(BF)
+                    u_row = place_ref[source, at : at + 1, :].astype(BF)
+                    v_row = place_ref[source, at + subs * pairs : at + subs * pairs + 1, :].astype(BF)
+                    u_hot = jnp.where(row_id == u_row, one, none)
+                    v_hot = jnp.where(col_id == v_row, one, none)
                     first.append((u_hot, diag))
                     second.append(v_hot)
                 spread = []
@@ -145,12 +173,11 @@
                         axis=0,
                     )
                     spread.append(dot(hot, block).astype(BF))
-                acc_ref[sub] += contract_last(
+                term = contract_last(
                     jnp.concatenate(spread, axis=1), jnp.concatenate(second, axis=1)
                 )
-            return carry
-
-        lax.fori_loop(0, facets // sources, one, 0)
+                acc_ref[sub] = term if it == 0 else acc_ref[sub] + term
+
         u_taps = taps(
             lax.broadcasted_iota(jnp.int32, (rows, rows), 1),
             lax.broadcasted_iota(jnp.int32, (rows, rows), 0),
@@ -195,9 +222,10 @@
         kernel,
         out_shape=[jax.ShapeDtypeStruct(image.shape, F32), edge, edge]
         + [jax.ShapeDtypeStruct((subs * piece, width), BF)] * bands,
-        in_specs=[smem(), vmem(), vmem(), vmem()],
+        in_specs=[smem()] + [vmem()] * 3,
         out_specs=[vmem()] * (3 + bands),
         scratch_shapes=[
+            pltpu.VMEM((facets, received.shape[1] - vis_rows, 2 * S), F32),
             pltpu.VMEM((subs, rows, width), F32),
             pltpu.VMEM((subs, (bands - 1) * band_rows + HALF, width), F32),
         ],
@@ -206,27 +234,65 @@
     )(steps, received, image, dual)
 
 
-def toeplitz(weights, outs, ins):
-    w = weights.transpose(3, 2, 1, 0)
-    cols = [jnp.pad(w, ((0, 0), (o, ins - 3 - o), (0, 0), (0, 0))) for o in range(outs)]
-    return jnp.stack(cols, axis=3)
-
-
 def weight_matrices(conv_first, conv_middle, conv_last):
-    first = toeplitz(conv_first, GROUP, GROUP + 2)
     ci = conv_first.shape[1]
-    first = first.reshape(3 * (GROUP + 2) * ci, GROUP // 2, 2, CH)
-    first = first.transpose(0, 2, 1, 3).reshape(3 * (GROUP + 2) * ci, GROUP * CH)
-    middle = toeplitz(conv_middle, GROUP // 2, GROUP // 2 + 2).reshape(
-        3 * (GROUP // 2 + 2) * CH, GROUP // 2 * CH
-    )
-    last = toeplitz(conv_last, GROUP, GROUP + 2)
     co = conv_last.shape[0]
-    last = last.transpose(1, 2, 0, 4, 3).reshape(GROUP + 2, CH, 3 * co * GROUP)
-    main = last[:GROUP].reshape(GROUP // 2, 2, CH, -1).transpose(1, 0, 2, 3)
-    main = main.reshape(GROUP * CH, 3 * co * GROUP)
-    tail = jnp.pad(last[GROUP:], ((0, 0), (0, CH), (0, 0))).reshape(4 * CH, 3 * co * GROUP)
-    return first, middle, jnp.concatenate([main, tail], axis=0)
+    first = conv_first.transpose(3, 2, 1, 0)
+    middle = conv_middle.transpose(3, 2, 1, 0)
+    last = conv_last[:, :, ::-1].transpose(3, 1, 2, 0).reshape(3, CH, 3 * co)
+    ins = GROUP + 2
+    outs = GROUP * co
+
+    def kernel(first_ref, mid_ref, last_ref, one_ref, two_ref, three_ref):
+        zero = jnp.zeros((ci, CH), F32)
+        rows = []
+        for t in range(3):
+            for r in range(ins):
+                parts = []
+                for phase in range(2):
+                    for k in range(GROUP // 2):
+                        dy = r - 2 * k - phase
+                        parts.append(first_ref[t, dy].astype(F32) if 0 <= dy < 3 else zero)
+                rows.append(jnp.concatenate(parts, axis=1))
+        one_ref[...] = jnp.concatenate(rows, axis=0).astype(BF)
+        zero = jnp.zeros((CH, CH), BF)
+        for t in range(3):
+            for r in range(GROUP // 2 + 2):
+                parts = [
+                    mid_ref[t, r - k] if 0 <= r - k < 3 else zero for k in range(GROUP // 2)
+                ]
+                at = (t * (GROUP // 2 + 2) + r) * CH
+                two_ref[at : at + CH, :] = jnp.concatenate(parts, axis=1)
+        three_ref[...] = jnp.zeros(three_ref.shape, BF)
+        lane = lax.broadcasted_iota(jnp.int32, (CH, 128), 1)
+        keep = jnp.where(lane < outs, 1.0, 0.0)
+        for r in range(ins):
+            taps = []
+            for t in range(3):
+                base = jnp.concatenate(
+                    [last_ref[t].astype(F32), jnp.zeros((CH, 128 - 3 * co), F32)], axis=1
+                )
+                taps.append(pltpu.roll(base, (r - 2) * co % 128, 1) * keep)
+            block = jnp.concatenate([taps[0] + pltpu.roll(taps[1], outs, 1), taps[2]], axis=1)
+            if r < GROUP:
+                at = (r % 2 * (GROUP // 2) + r // 2) * CH
+            else:
+                at = GROUP * CH + (r - GROUP) * 2 * CH
+            three_ref[at : at + CH, :] = block.astype(BF)
+
+    return pl.pallas_call(
+        kernel,
+        out_shape=[
+            jax.ShapeDtypeStruct((3 * ins * ci, GROUP * CH), BF),
+            jax.ShapeDtypeStruct((3 * (GROUP // 2 + 2) * CH, GROUP // 2 * CH), BF),
+            jax.ShapeDtypeStruct(((GROUP + 4) * CH, 256), BF),
+        ],
+        in_specs=[vmem()] * 3,
+        out_specs=[vmem()] * 3,
+        compiler_params=params(),
+        cost_estimate=pl.CostEstimate(flops=1 << 20, bytes_accessed=1 << 20, transcendentals=0),
+        name="weight_matrices",
+    )(first, middle, last)
 
 
 def denoise(pieces, edges, first, middle, last, subs, bands, band_rows, width):
@@ -273,10 +339,10 @@
         lane_id = lax.broadcasted_iota(jnp.int32, (1, GROUP * CH), 1)
         lane_row = lane_id // (GROUP // 2 * CH) + 2 * (lane_id // CH % (GROUP // 2))
 
-        def layer_one(g, carry):
-            top = pl.multiple_of(g * GROUP * channels, GROUP)
+        def layer_one(g):
+            top = g * GROUP * channels
             x = jnp.concatenate(
-                [x_ref[part, pl.ds(top, in_rows * channels), :] for part in range(lanes // 128)], axis=1
+                [x_ref[part, top : top + in_rows * channels, :] for part in range(lanes // 128)], axis=1
             )
             stack = jnp.concatenate(
                 [pltpu.roll(x, 1, 1) * inside, x * inside, pltpu.roll(x, lanes - 1, 1) * inside], axis=0
@@ -286,12 +352,10 @@
             row = lane_row + (g * GROUP + 1 - HALO) + me * band_rows
             keep = jnp.where((row >= 0) & (row < band_rows * bands), 1.0, 0.0)
             one_ref[g, 0:cols, :] = (jnp.maximum(hidden, 0.0) * keep).astype(BF)
-            return carry
-
-        lax.fori_loop(0, groups, layer_one, 0)
+
         block = GROUP // 2 * CH
 
-        def layer_two(g, carry):
+        def layer_two(g):
             row = lane_row + (g * GROUP - 1) + me * band_rows
             keep = jnp.where((row >= 0) & (row < band_rows * bands), 1.0, 0.0)
             for phase in range(2):
@@ -305,15 +369,13 @@
                 two_ref[g, :, phase * block : (phase + 1) * block] = (
                     jnp.maximum(hidden, 0.0) * part
                 ).astype(BF)
-            return carry
-
-        lax.fori_loop(0, groups, layer_two, 0)
+
         out_ch = channels * GROUP
         out_col = lax.broadcasted_iota(jnp.int32, (1, width), 1)
         has_left = jnp.where((out_col > 0) | (facet > 0), 1.0, 0.0)
         has_right = jnp.where((out_col < width - 1) | (facet < facets - 1), 1.0, 0.0)
 
-        def layer_three(g, carry):
+        def layer_three(g):
             hidden = jnp.concatenate(
                 [
                     two_ref[g],
@@ -327,20 +389,29 @@
             noise = (
                 y[:out_ch, base - 1 : base - 1 + width] * has_left
                 + y[out_ch : 2 * out_ch, base : base + width]
-                + y[2 * out_ch :, base + 1 : base + 1 + width] * has_right
+                + y[2 * out_ch : 3 * out_ch, base + 1 : base + 1 + width] * has_right
             )
-            noise_ref[:, pl.ds(pl.multiple_of(g * GROUP, GROUP), GROUP), :] = noise.reshape(
-                channels, GROUP, width
-            )
-            return carry
-
-        lax.fori_loop(0, groups - 1, layer_three, 0)
+            for part in range(width // 128):
+                noise_ref[part, g * out_ch : (g + 1) * out_ch, :] = noise[
+                    :, part * 128 : (part + 1) * 128
+                ]
+
+        for g in range(groups + 4):
+            if g < groups:
+                layer_one(g)
+            if 0 <= g - 2 < groups:
+                layer_two(g - 2)
+            if 0 <= g - 4 < groups - 1:
+                layer_three(g - 4)
         for k in range(bands):
             band = lax.rem(me + k, bands)
             for sub in range(subs):
-                out_refs[k][sub * band_rows : (sub + 1) * band_rows, :] = noise_ref[
-                    band * subs + sub
-                ].astype(BF)
+                for part in range(width // 128):
+                    out_refs[k][
+                        sub * band_rows : (sub + 1) * band_rows, part * 128 : (part + 1) * 128
+                    ] = noise_ref[
+                        part, pl.ds(band * subs + sub, band_rows, stride=channels), :
+                    ].astype(BF)
 
     return pl.pallas_call(
         kernel,
@@ -351,9 +422,9 @@
             pltpu.VMEM((lanes // 128, (groups * GROUP + 2) * channels, 128), F32),
             pltpu.VMEM((groups + 1, tall, GROUP * CH), BF),
             pltpu.VMEM((groups, cols, GROUP * CH), BF),
-            pltpu.VMEM((channels, band_rows, width), F32),
+            pltpu.VMEM((width // 128, band_rows * channels, 128), F32),
         ],
-        compiler_params=params(),
+        compiler_params=params(32),
         name="denoise",
     )(first, middle, last, *pieces, *edges)
 

time: 93.6 us -> 74.6 us (0.80)
  blocking collectives: 0 us -> 21 us
  local copies, waits for them, and re-layouts: 20 us -> 0.32 us
  Pallas kernels: 30 us -> 20.6 us
  starting transfers between devices: 20.9 us -> 15.8 us
  waiting for transfers between devices: 19.6 us -> 15.7 us
  other arithmetic: 1.43 us -> 0 us
    all_to_all x0 -> x1, blocking collectives: none -> 21 us  [body(): lax.all_to_all(packed, 'facet', split_axis=0, concat_axis=0, tiled=True)]
    all_to_all x1 -> x0, waiting for transfers between devices: 9.92 us -> none  [body(): lax.all_to_all(packed, 'facet', split_axis=0, concat_axis=0, tiled=True)]
    unnamed x37 -> x16, local copies, waits for them, and re-layouts: 9.41 us -> 0.2 us
    pallas_call x1, Pallas kernels: 16.2 us -> 8.89 us  [denoise(): pl.pallas_call(kernel, out_shape=[jax.ShapeDtypeStruct((subs * band_rows,...]
    ppermute x9, waiting for transfers between devices: 7.22 us -> 13.7 us  [exchange(): lax.ppermute(parts[k], 'band', [(i, (i + k) % bands) for i in range(bands)])]
    all_to_all x1 -> x0, starting transfers between devices: 5.3 us -> none  [body(): lax.all_to_all(packed, 'facet', split_axis=0, concat_axis=0, tiled=True)]
    another operation x5 -> x0, local copies, waits for them, and re-layouts: 4.79 us -> none  [toeplitz(): return jnp.stack(cols, axis=3)]
    reshape x2, local copies, waits for them, and re-layouts: 3.29 us -> 0.11 us  [weight_matrices(): last = conv_last[:, :, ::-1].transpose(3, 1, 2, 0).reshape(3, CH, 3 * co)]
  transfers between devices with their start and end apart: 12 -> 11, of which waited for: 4 -> 4; matrix products, arithmetic and copies ran while one was open for 18% -> 0% of each run, Pallas kernels for 0% -> 1%
where the time goes in v2:
time: 74.6 us; the launch traced here: 74.3 us
  blocking collectives  21 us (28%)
  Pallas kernels  20.6 us (28%)
  starting transfers between devices  15.8 us (21%)
  waiting for transfers between devices  15.7 us (21%)
  between operations  0.83 us (1%)
    all_to_all x1, blocking collectives, body(): lax.all_to_all(packed, 'facet', split_axis=0, concat_axis=0, tiled=True)  21 us
    ppermute x9, waiting for transfers between devices, exchange(): lax.ppermute(parts[k], 'band', [(i, (i + k) % bands) for i in range(bands)])  13.7 us
    ppermute x9, starting transfers between devices, exchange(): lax.ppermute(parts[k], 'band', [(i, (i + k) % bands) for i in range(bands)])  12.7 us
    pallas_call x1, Pallas kernels, denoise(): pl.pallas_call(kernel, out_shape=[jax.ShapeDtypeStruct((subs * band_rows,...  8.89 us
    pallas_call x1, Pallas kernels, grid_and_step(): pl.pallas_call(kernel, out_shape=[jax.ShapeDtypeStruct(image.shape, F32),...  6.32 us
    pallas_call x1, Pallas kernels, pack_blocks(): pl.pallas_call(kernel, out_shape=jax.ShapeDtypeStruct((facets, vis_rows +...  3.28 us
    ppermute x1, waiting for transfers between devices, body(): lax.ppermute(edge_l, 'facet', [(i + 1, i) for i in range(facets - 1)])  1.99 us
    ppermute x1, starting transfers between devices, body(): lax.ppermute(edge_r, 'facet', [(i, i + 1) for i in range(facets - 1)])  1.86 us
  transfers between devices with their start and end apart: 11, of which 4 were waited for; matrix products, arithmetic and copies ran while one was open for 0% of the time, Pallas kernels for 1%

profile of v2, /device:TPU:0, one launch (start us, length us, event | category | flops | bytes accessed | tf_op | source)
XLA Modules:
  0.0 74.3 jit_solution(419117441700005954)
XLA Ops:
  0.6 3.3 %pack_blocks.1 = bf16[8,528,128]{2,1,0:T(8,128)(2,1)} custom-call(s32[2,32]{1,0:T(2,128)} %bitcast.19, s32[2,32]{1,0:T(2,128)} %slot_hbm.1, bf16[2,32,64,64]{3,2,1,0:T(8,128)(2,1)} %vis_hbm.1, s32[2,32,2,64]{3,2,1,0:T(2,128)} %pos_hbm.1), custom_call_target="tpu_custom_call" | custom-call | tf_op jit(solution)/shard_map/pack_blocks/pallas_call | solution.py:91
  3.9 0.0 copy-start
  3.9 0.0 copy-start.1
  3.9 0.0 copy-start.2
  4.0 21.0 %all_to_all.5.rec_ref = bf16[8,528,128]{2,1,0:T(8,128)(2,1)S(1)} all-to-all(bf16[8,528,128]{2,1,0:T(8,128)(2,1)} %pack_blocks.1), channel_id=1, replica_groups=mesh['facet'=8,'band'=4] {'facet'}, dimensions={0} | all-to-all | bytes 2162688 | tf_op jit(solution)/shard_map/all_to_all | solution.py:484
  25.0 0.0 copy-done
  25.0 0.0 copy-done.1
  25.0 0.0 copy-done.2
  25.0 0.0 copy-start.4
  25.0 0.0 copy-start.5
  25.0 0.0 copy-start.3
  25.0 6.3 %grid_and_step.1 = (f32[2,256,384]{2,1,0:T(8,128)S(1)}, bf16[4,8,128]{2,1,0:T(8,128)(2,1)S(1)}, bf16[4,8,128]{2,1,0:T(8,128)(2,1)S(1)}, bf16[144,384]{1,0:T(8,12...) custom-call(f32[2]{0:T(128)S(1)} %copy-done.2, ...), custom_call_target="tpu_custom_call" | custom-call | tf_op jit(solution)/shard_map/grid_and_step/pallas_call | solution.py:221
  31.3 1.9 %collective-permute-start.3 = (bf16[4,8,128]{2,1,0:T(8,128)(2,1)S(1)}, bf16[4,8,128]{2,1,0:T(8,128)(2,1)S(1)}, u32[]{:S(2)}, u32[]{:S(2)}) collective-permute-start(bf16[4,8,128]{2,1,0:T(8,128)(2,1)S(1)} %get-tuple-element.24), channel_id=1, source_target_pairs={{0,4},{4,8},{8,12},{12,16},{16,20},{20,24},{24,28},{1,5},{5,9},{9,... | collective-permute-start | bytes 24584 | tf_op jit(solution)/shard_map/ppermute | solution.py:489
  33.3 1.3 %collective-permute-start.4 = (bf16[4,8,128]{2,1,0:T(8,128)(2,1)S(1)}, bf16[4,8,128]{2,1,0:T(8,128)(2,1)S(1)}, u32[]{:S(2)}, u32[]{:S(2)}) collective-permute-start(bf16[4,8,128]{2,1,0:T(8,128)(2,1)S(1)} %get-tuple-element.25), channel_id=1, source_target_pairs={{4,0},{8,4},{12,8},{16,12},{20,16},{24,20},{28,24},{5,1},{9,5},{13... | collective-permute-start | bytes 24584 | tf_op jit(solution)/shard_map/ppermute | solution.py:490
  34.6 0.0 collective-permute-done.3
  34.6 2.0 %collective-permute-done.4 = bf16[4,8,128]{2,1,0:T(8,128)(2,1)S(1)} collective-permute-done((bf16[4,8,128]{2,1,0:T(8,128)(2,1)S(1)}, bf16[4,8,128]{2,1,0:T(8,128)(2,1)S(1)}, u32[]{:S(2)}, u32[]{:S(2)}) %collective-permute-start.4) | collective-permute-done | bytes 8224 | tf_op jit(solution)/shard_map/ppermute | solution.py:490
  36.6 1.6 %collective-permute-start.5 = (bf16[16,128]{1,0:T(8,128)(2,1)S(1)}, bf16[16,128]{1,0:T(8,128)(2,1)S(1)}, u32[]{:S(2)}, u32[]{:S(2)}) collective-permute-start(bf16[16,128]{1,0:T(8,128)(2,1)S(1)} %get-tuple-element.32), channel_id=1, source_target_pairs={{0,1},{1,2},{2,3},{3,0},{4,5},{5,6},{6,7},{7,4},{8,9},{9,10},{10,1... | collective-permute-start | bytes 12296 | tf_op jit(solution)/shard_map/ppermute | solution.py:461
  38.2 0.0 copy-done.4
  38.2 1.6 %collective-permute-start = (bf16[144,384]{1,0:T(8,128)(2,1)S(1)}, bf16[144,384]{1,0:T(8,128)(2,1)S(1)}, u32[]{:S(2)}, u32[]{:S(2)}) collective-permute-start(bf16[144,384]{1,0:T(8,128)(2,1)S(1)} %get-tuple-element.21), channel_id=1, source_target_pairs={{0,1},{1,2},{2,3},{3,0},{4,5},{5,6},{6,7},{7,4},{8,9},{9,10},{10,1... | collective-permute-start | bytes 331784 | tf_op jit(solution)/shard_map/ppermute | solution.py:461
  39.8 1.2 %collective-permute-start.1 = (bf16[144,384]{1,0:T(8,128)(2,1)S(1)}, bf16[144,384]{1,0:T(8,128)(2,1)S(1)}, u32[]{:S(2)}, u32[]{:S(2)}) collective-permute-start(bf16[144,384]{1,0:T(8,128)(2,1)S(1)} %get-tuple-element.22), channel_id=1, source_target_pairs={{0,2},{1,3},{2,0},{3,1},{4,6},{5,7},{6,4},{7,5},{8,10},{9,11},{10,... | collective-permute-start | bytes 331784 | tf_op jit(solution)/shard_map/ppermute | solution.py:461
  41.0 2.7 %collective-permute-start.2 = (bf16[144,384]{1,0:T(8,128)(2,1)S(1)}, bf16[144,384]{1,0:T(8,128)(2,1)S(1)}, u32[]{:S(2)}, u32[]{:S(2)}) collective-permute-start(bf16[144,384]{1,0:T(8,128)(2,1)S(1)} %get-tuple-element.23), channel_id=1, source_target_pairs={{0,3},{1,0},{2,1},{3,2},{4,7},{5,4},{6,5},{7,6},{8,11},{9,8},{10,9... | collective-permute-start | bytes 331784 | tf_op jit(solution)/shard_map/ppermute | solution.py:461
  43.7 0.3 collective-permute-start.6
  44.1 0.0 collective-permute-done.5.rest_5_
  44.1 1.3 %collective-permute-start.7 = (bf16[16,128]{1,0:T(8,128)(2,1)S(1)}, bf16[16,128]{1,0:T(8,128)(2,1)S(1)}, u32[]{:S(2)}, u32[]{:S(2)}) collective-permute-start(bf16[16,128]{1,0:T(8,128)(2,1)S(1)} %get-tuple-element.30), channel_id=1, source_target_pairs={{0,3},{1,0},{2,1},{3,2},{4,7},{5,4},{6,5},{7,6},{8,11},{9,8},{10,9... | collective-permute-start | bytes 12296 | tf_op jit(solution)/shard_map/ppermute | solution.py:461
  45.4 0.0 copy-done.5
  45.4 0.0 copy-done.3
  45.5 0.1 copy.16
  45.6 0.1 copy.18.last_ref
  45.7 0.8 %weight_matrices.1 = (bf16[240,512]{1,0:T(8,128)(2,1)S(1)}, bf16[1152,256]{1,0:T(8,128)(2,1)S(1)}, bf16[768,256]{1,0:T(8,128)(2,1)S(1)}) custom-call(bf16[3,3,8,64]{3,2,1,0:T(8,128)(2,1)S(1)} %bitcast.18, bf16[3,3,64,64]{3,2,1,0:T(8,128)(2,1)S(1)} %bitcast.17, bf16[3,64,24]{2,1,0:T(8,128)(2,1)S(1)} %copy.18.last_ref), custom_call_target="tpu_custom_call" | custom-call | flops 1048576 | bytes 1048576 | tf_op jit(solution)/shard_map/weight_matrices/pallas_call | solution.py:283
  46.5 6.6 %collective-permute-done.6.rest_6_ = bf16[16,128]{1,0:T(8,128)(2,1)S(1)} collective-permute-done((bf16[16,128]{1,0:T(8,128)(2,1)S(1)}, bf16[16,128]{1,0:T(8,128)(2,1)S(1)}, u32[]{:S(2)}, u32[]{:S(2)}) %collective-permute-start.6) | collective-permute-done | bytes 4128 | tf_op jit(solution)/shard_map/ppermute | solution.py:461
  53.2 0.0 collective-permute-done.7.rest_7_
  53.2 0.0 collective-permute-done.rest_1_
  53.2 0.0 collective-permute-done.1.rest_2_
  53.2 0.0 collective-permute-done.2.rest_3_
  53.2 8.9 %denoise.1 = (bf16[128,384]{1,0:T(8,128)(2,1)S(1)}, bf16[128,384]{1,0:T(8,128)(2,1)S(1)}, bf16[128,384]{1,0:T(8,128)(2,1)S(1)}, bf16[128,384]{1,0:T(8,128)(2,1)S(1)}) custom-call(bf16[240,512]{1,0:T(8,128)(2,1)S(1)} %get-tuple-element.17.first_ref, bf16[1152,256]{1,0:T(8,128)(2,1)S(1)} %get-tuple-element.18.mid_ref, ...), custom_call_target="tpu_custom_call" | custom-call | tf_op jit(solution)/shard_map/denoise/pallas_call | solution.py:416
  62.1 0.7 collective-permute-start.8
  62.8 0.6 collective-permute-start.9
  63.4 2.6 %collective-permute-start.10 = (bf16[128,384]{1,0:T(8,128)(2,1)S(1)}, bf16[128,384]{1,0:T(8,128)(2,1)S(1)}, u32[]{:S(2)}, u32[]{:S(2)}) collective-permute-start(bf16[128,384]{1,0:T(8,128)(2,1)S(1)} %get-tuple-element.29), channel_id=1, source_target_pairs={{0,3},{1,0},{2,1},{3,2},{4,7},{5,4},{6,5},{7,6},{8,11},{9,8},{10,9... | collective-permute-start | bytes 294920 | tf_op jit(solution)/shard_map/ppermute | solution.py:461
  66.0 3.7 %collective-permute-done.8.rest_1_ = bf16[128,384]{1,0:T(8,128)(2,1)S(1)} collective-permute-done((bf16[128,384]{1,0:T(8,128)(2,1)S(1)}, bf16[128,384]{1,0:T(8,128)(2,1)S(1)}, u32[]{:S(2)}, u32[]{:S(2)}) %collective-permute-start.8) | collective-permute-done | bytes 98336 | tf_op jit(solution)/shard_map/ppermute | solution.py:461
  69.7 3.4 %collective-permute-done.9.rest_2_ = bf16[128,384]{1,0:T(8,128)(2,1)S(1)} collective-permute-done((bf16[128,384]{1,0:T(8,128)(2,1)S(1)}, bf16[128,384]{1,0:T(8,128)(2,1)S(1)}, u32[]{:S(2)}, u32[]{:S(2)}) %collective-permute-start.9) | collective-permute-done | bytes 98336 | tf_op jit(solution)/shard_map/ppermute | solution.py:461
  73.1 0.0 collective-permute-done.10.rest_3_
  73.1 1.3 %finish.1 = (f32[2,256,384]{2,1,0:T(8,128)}, f32[2,256,384]{2,1,0:T(8,128)}) custom-call(f32[2,256,384]{2,1,0:T(8,128)S(1)} %get-tuple-element.16.shift_ref, bf16[128,384]{1,0:T(8,128)(2,1)S(1)} %get-tuple-element.26.rest_0_, bf16[128,384]{1,0:T(8,128)(2,1)S(1)} %collective-permute-done.8.rest_1_, bf16[128,384]{1,0:T(8,128)(2,1)S(1)} %collective-permute-done.9.rest_2_, ...), custom_call_target="tpu_custom_call" | custom-call | tf_op jit(solution)/shard_map/finish/pallas_call | solution.py:449
  (6 shorter events, 0.0 us)
Async XLA Ops:
  3.9 21.1 %copy-start = (f32[2,256,384]{2,1,0:T(8,128)S(1)}, f32[2,256,384]{2,1,0:T(8,128)}, u32[]{:S(2)}) copy-start(f32[2,256,384]{2,1,0:T(8,128)} %img_ref.1) | copy-start | bytes 2359300
  3.9 21.1 %copy-start.1 = (f32[2,256,384]{2,1,0:T(8,128)S(1)}, f32[2,256,384]{2,1,0:T(8,128)}, u32[]{:S(2)}) copy-start(f32[2,256,384]{2,1,0:T(8,128)} %dual_ref.1) | copy-start | bytes 2359300
  3.9 21.0 %copy-start.2 = (f32[2]{0:T(128)S(1)}, f32[2]{0:T(128)}, u32[]{:S(2)}) copy-start(f32[2]{0:T(128)} %step_ref.1) | copy-start | bytes 28
  25.0 13.2 %copy-start.4 = (bf16[8,64,3,3]{1,0,3,2:T(8,128)(2,1)S(1)}, bf16[8,64,3,3]{1,0,3,2:T(8,128)(2,1)}, u32[]{:S(2)}) copy-start(bf16[8,64,3,3]{1,0,3,2:T(8,128)(2,1)} %param.19) | copy-start | bytes 27652
  25.0 20.4 %copy-start.5 = (bf16[64,8,3,3]{0,1,3,2:T(8,128)(2,1)S(1)}, bf16[64,8,3,3]{0,1,3,2:T(8,128)(2,1)}, u32[]{:S(2)}) copy-start(bf16[64,8,3,3]{0,1,3,2:T(8,128)(2,1)} %param.17) | copy-start | bytes 27652
  25.0 20.4 %copy-start.3 = (bf16[64,64,3,3]{1,0,3,2:T(8,128)(2,1)S(1)}, bf16[64,64,3,3]{1,0,3,2:T(8,128)(2,1)}, u32[]{:S(2)}) copy-start(bf16[64,64,3,3]{1,0,3,2:T(8,128)(2,1)} %param.18) | copy-start | bytes 221188
  31.3 3.2 %collective-permute-start.3 = (bf16[4,8,128]{2,1,0:T(8,128)(2,1)S(1)}, bf16[4,8,128]{2,1,0:T(8,128)(2,1)S(1)}, u32[]{:S(2)}, u32[]{:S(2)}) collective-permute-start(bf16[4,8,128]{2,1,0:T(8,128)(2,1)S(1)} %get-tuple-element.24), channel_id=1, source_target_pairs={{0,4},{4,8},{8,12},{12,16},{16,20},{20,24},{24,28},{1,5},{5,9},{9,... | collective-permute-start | bytes 24584 | tf_op jit(solution)/shard_map/ppermute | solution.py:489
  33.3 3.3 %collective-permute-start.4 = (bf16[4,8,128]{2,1,0:T(8,128)(2,1)S(1)}, bf16[4,8,128]{2,1,0:T(8,128)(2,1)S(1)}, u32[]{:S(2)}, u32[]{:S(2)}) collective-permute-start(bf16[4,8,128]{2,1,0:T(8,128)(2,1)S(1)} %get-tuple-element.25), channel_id=1, source_target_pairs={{4,0},{8,4},{12,8},{16,12},{20,16},{24,20},{28,24},{5,1},{9,5},{13... | collective-permute-start | bytes 24584 | tf_op jit(solution)/shard_map/ppermute | solution.py:490
  36.6 7.5 %collective-permute-start.5 = (bf16[16,128]{1,0:T(8,128)(2,1)S(1)}, bf16[16,128]{1,0:T(8,128)(2,1)S(1)}, u32[]{:S(2)}, u32[]{:S(2)}) collective-permute-start(bf16[16,128]{1,0:T(8,128)(2,1)S(1)} %get-tuple-element.32), channel_id=1, source_target_pairs={{0,1},{1,2},{2,3},{3,0},{4,5},{5,6},{6,7},{7,4},{8,9},{9,10},{10,1... | collective-permute-start | bytes 12296 | tf_op jit(solution)/shard_map/ppermute | solution.py:461
  38.2 14.9 %collective-permute-start = (bf16[144,384]{1,0:T(8,128)(2,1)S(1)}, bf16[144,384]{1,0:T(8,128)(2,1)S(1)}, u32[]{:S(2)}, u32[]{:S(2)}) collective-permute-start(bf16[144,384]{1,0:T(8,128)(2,1)S(1)} %get-tuple-element.21), channel_id=1, source_target_pairs={{0,1},{1,2},{2,3},{3,0},{4,5},{5,6},{6,7},{7,4},{8,9},{9,10},{10,1... | collective-permute-start | bytes 331784 | tf_op jit(solution)/shard_map/ppermute | solution.py:461
  39.8 13.4 %collective-permute-start.1 = (bf16[144,384]{1,0:T(8,128)(2,1)S(1)}, bf16[144,384]{1,0:T(8,128)(2,1)S(1)}, u32[]{:S(2)}, u32[]{:S(2)}) collective-permute-start(bf16[144,384]{1,0:T(8,128)(2,1)S(1)} %get-tuple-element.22), channel_id=1, source_target_pairs={{0,2},{1,3},{2,0},{3,1},{4,6},{5,7},{6,4},{7,5},{8,10},{9,11},{10,... | collective-permute-start | bytes 331784 | tf_op jit(solution)/shard_map/ppermute | solution.py:461
  41.0 12.1 %collective-permute-start.2 = (bf16[144,384]{1,0:T(8,128)(2,1)S(1)}, bf16[144,384]{1,0:T(8,128)(2,1)S(1)}, u32[]{:S(2)}, u32[]{:S(2)}) collective-permute-start(bf16[144,384]{1,0:T(8,128)(2,1)S(1)} %get-tuple-element.23), channel_id=1, source_target_pairs={{0,3},{1,0},{2,1},{3,2},{4,7},{5,4},{6,5},{7,6},{8,11},{9,8},{10,9... | collective-permute-start | bytes 331784 | tf_op jit(solution)/shard_map/ppermute | solution.py:461
  43.7 9.4 %collective-permute-start.6 = (bf16[16,128]{1,0:T(8,128)(2,1)S(1)}, bf16[16,128]{1,0:T(8,128)(2,1)S(1)}, u32[]{:S(2)}, u32[]{:S(2)}) collective-permute-start(bf16[16,128]{1,0:T(8,128)(2,1)S(1)} %get-tuple-element.31), channel_id=1, source_target_pairs={{0,2},{1,3},{2,0},{3,1},{4,6},{5,7},{6,4},{7,5},{8,10},{9,11},{10,... | collective-permute-start | bytes 12296 | tf_op jit(solution)/shard_map/ppermute | solution.py:461
  44.1 9.1 %collective-permute-start.7 = (bf16[16,128]{1,0:T(8,128)(2,1)S(1)}, bf16[16,128]{1,0:T(8,128)(2,1)S(1)}, u32[]{:S(2)}, u32[]{:S(2)}) collective-permute-start(bf16[16,128]{1,0:T(8,128)(2,1)S(1)} %get-tuple-element.30), channel_id=1, source_target_pairs={{0,3},{1,0},{2,1},{3,2},{4,7},{5,4},{6,5},{7,6},{8,11},{9,8},{10,9... | collective-permute-start | bytes 12296 | tf_op jit(solution)/shard_map/ppermute | solution.py:461
  62.1 7.6 %collective-permute-start.8 = (bf16[128,384]{1,0:T(8,128)(2,1)S(1)}, bf16[128,384]{1,0:T(8,128)(2,1)S(1)}, u32[]{:S(2)}, u32[]{:S(2)}) collective-permute-start(bf16[128,384]{1,0:T(8,128)(2,1)S(1)} %get-tuple-element.27), channel_id=1, source_target_pairs={{0,1},{1,2},{2,3},{3,0},{4,5},{5,6},{6,7},{7,4},{8,9},{9,10},{10,1... | collective-permute-start | bytes 294920 | tf_op jit(solution)/shard_map/ppermute | solution.py:461
  62.8 10.3 %collective-permute-start.9 = (bf16[128,384]{1,0:T(8,128)(2,1)S(1)}, bf16[128,384]{1,0:T(8,128)(2,1)S(1)}, u32[]{:S(2)}, u32[]{:S(2)}) collective-permute-start(bf16[128,384]{1,0:T(8,128)(2,1)S(1)} %get-tuple-element.28), channel_id=1, source_target_pairs={{0,2},{1,3},{2,0},{3,1},{4,6},{5,7},{6,4},{7,5},{8,10},{9,11},{10,... | collective-permute-start | bytes 294920 | tf_op jit(solution)/shard_map/ppermute | solution.py:461
  63.4 9.7 %collective-permute-start.10 = (bf16[128,384]{1,0:T(8,128)(2,1)S(1)}, bf16[128,384]{1,0:T(8,128)(2,1)S(1)}, u32[]{:S(2)}, u32[]{:S(2)}) collective-permute-start(bf16[128,384]{1,0:T(8,128)(2,1)S(1)} %get-tuple-element.29), channel_id=1, source_target_pairs={{0,3},{1,0},{2,1},{3,2},{4,7},{5,4},{6,5},{7,6},{8,11},{9,8},{10,9... | collective-permute-start | bytes 294920 | tf_op jit(solution)/shard_map/ppermute | solution.py:461

commit v3 on v2

--- a/solution.py
+++ b/solution.py
@@ -31,16 +31,44 @@
     return pl.BlockSpec(memory_space=pltpu.SMEM)
 
 
-def pack_blocks(visibility, uv_positions, destinations, column_slots, facets, pairs):
+def taps(row, col):
+    offset = col - row
+    value = jnp.exp(-0.5 * ((offset.astype(F32) - (KW - 1) / 2.0) / (KW / 4.0)) ** 2)
+    return jnp.where((offset >= 0) & (offset < KW), value, 0.0).astype(BF)
+
+
+def contract_last(a, b):
+    return lax.dot_general(a, b, (((1,), (1,)), ((), ())), preferred_element_type=F32)
+
+
+def contract_first(a, b):
+    return lax.dot_general(a, b, (((0,), (0,)), ((), ())), preferred_element_type=F32)
+
+
+def dot(a, b):
+    return jnp.dot(a, b, preferred_element_type=F32)
+
+
+def tap_matrix(size):
+    shape = (size, size)
+    return taps(lax.broadcasted_iota(jnp.int32, shape, 1), lax.broadcasted_iota(jnp.int32, shape, 0))
+
+
+def pack_blocks(
+    visibility, uv_positions, destinations, column_slots, image, dual, steps, facets, pairs
+):
+    rows, width = image.shape[1:]
     subs, blocks = visibility.shape[:2]
     vis_rows = subs * pairs * S
     pos_rows = -(-2 * subs * pairs // 16) * 16
 
     chunk = blocks // CHUNKS
+    halo_rows = 2 * HALO * subs * (rows // 128)
 
     def kernel(
-        dest_hbm, slot_hbm, vis_hbm, pos_hbm, out_ref,
-        dest_ref, slot_ref, vis_ref, pos_ref, count_ref, place_ref, side_ref, sems,
+        dest_hbm, slot_hbm, vis_hbm, pos_hbm, img_hbm, dual_hbm, step_hbm, out_hbm,
+        dest_ref, slot_ref, vis_ref, pos_ref, edge_ref, step_ref, count_ref, place_ref, side_ref,
+        main_ref, halo_ref, sems,
     ):
         small = [
             pltpu.make_async_copy(dest_hbm, dest_ref, sems.at[CHUNKS]),
@@ -53,12 +81,59 @@
             )
             for c in range(CHUNKS)
         ]
-        for copy in small + large:
+        edges = [
+            pltpu.make_async_copy(step_hbm, step_ref, sems.at[CHUNKS + 3]),
+        ] + [
+            pltpu.make_async_copy(
+                ref.at[:, :, pl.ds(at, 128)], edge_ref.at[n, side], sems.at[CHUNKS + 4 + 2 * n + side]
+            )
+            for n, ref in enumerate((img_hbm, dual_hbm))
+            for side, at in enumerate((0, width - 128))
+        ]
+        for copy in small + large + edges:
             copy.start()
         side_ref[...] = jnp.zeros(side_ref.shape, BF)
         place_ref[...] = jnp.zeros(place_ref.shape, F32)
         for n in range(subs * facets):
             count_ref[n] = 0
+        wide = facets * 4 * HALO
+        cell_row = lax.broadcasted_iota(jnp.int32, (4 * HALO, 2 * S), 0)
+        cell_lane = lax.broadcasted_iota(jnp.int32, (4 * HALO, 2 * S), 1)
+        cell = cell_row % HALO + (width - KW - HALO + 1) * (cell_row // HALO % 2) - CENTRE
+        cell = jnp.where(cell_lane // S == cell_row // (2 * HALO), cell, 2 * P_SIZE)
+        cell = cell.astype(F32).astype(BF)
+        lane = lax.broadcasted_iota(jnp.int32, (1, 4 * HALO), 1)
+        mine = [
+            jnp.where(lane // (2 * HALO) == block, 1.0, 0.0).astype(BF) for block in range(2)
+        ]
+        row_id = lax.broadcasted_iota(jnp.int32, (rows, 2 * S), 0).astype(F32).astype(BF)
+        yes = jnp.ones((), BF)
+        no = jnp.zeros((), BF)
+        shape = (wide, facets * 2 * HALO)
+        src = lax.broadcasted_iota(jnp.int32, shape, 0)
+        dst = lax.broadcasted_iota(jnp.int32, shape, 1)
+        halo_side = dst // HALO % 2
+        meets = (src // (4 * HALO) == dst // (2 * HALO) + 2 * halo_side - 1) & (
+            src // HALO % 2 == 1 - halo_side
+        )
+        offset = dst % HALO - src % HALO + (KW - 1) * (1 - halo_side)
+        v_taps = jnp.where(meets, taps(0, offset).astype(F32), 0.0).astype(BF)
+        u_taps = tap_matrix(rows)
+        me = lax.axis_index("facet")
+        shape = (128, facets * 2 * HALO)
+        src = lax.broadcasted_iota(jnp.int32, shape, 0)
+        dst = lax.broadcasted_iota(jnp.int32, shape, 1)
+        halo_side = dst // HALO % 2
+        pick = [
+            jnp.where(
+                (src == dst % HALO + (128 - HALO) * side)
+                & (halo_side == 1 - side)
+                & (dst // (2 * HALO) == me + 2 * side - 1),
+                1.0,
+                0.0,
+            ).astype(BF)
+            for side in range(2)
+        ]
         for copy in small:
             copy.wait()
 
@@ -83,47 +158,76 @@
             lax.fori_loop(c * chunk, (c + 1) * chunk, one, 0, unroll=4)
         for facet in range(facets):
             both = jnp.concatenate([side_ref[0, facet], side_ref[1, facet]], axis=2)
-            out_ref[facet, :vis_rows, :] = both.reshape(vis_rows, 2 * S)
-        both = jnp.concatenate([place_ref[0], place_ref[1]], axis=1).astype(BF)
-        out_ref[:, vis_rows:, :] = both.reshape(facets, pos_rows, 2 * S)
+            main_ref[facet, :vis_rows, :] = both.reshape(vis_rows, 2 * S)
+        both = jnp.concatenate([place_ref[0], place_ref[1]], axis=1)
+        main_ref[:, vis_rows:, :] = both.astype(BF).reshape(facets, pos_rows, 2 * S)
+        sent = [
+            pltpu.make_async_copy(
+                main_ref, out_hbm.at[:, pl.ds(0, vis_rows + pos_rows)], sems.at[CHUNKS + 8]
+            ),
+            pltpu.make_async_copy(
+                halo_ref, out_hbm.at[:, pl.ds(vis_rows + pos_rows, halo_rows)], sems.at[CHUNKS + 9]
+            ),
+        ]
+        sent[0].start()
+
+        for copy in edges:
+            copy.wait()
+        halos = []
+        for sub in range(subs):
+            totals = []
+            for facet in range(facets):
+                hots, parts = [], []
+                for pair in range(pairs):
+                    at = sub * pairs + pair
+                    where = facet * pos_rows + at
+                    u_row = both[where : where + 1].astype(BF)
+                    v_row = both[where + subs * pairs : where + subs * pairs + 1].astype(BF)
+                    hots.append(jnp.where(row_id == u_row, yes, no))
+                    hot = jnp.where(cell == v_row, yes, no)
+                    found = contract_last(main_ref[facet, at * S : (at + 1) * S, :], hot).astype(BF)
+                    parts += [found * mine[0], found * mine[1]]
+                totals.append(dot(jnp.concatenate(hots, axis=1), jnp.concatenate(parts, axis=0)))
+            total = jnp.concatenate(totals, axis=1)
+            gradient = dot(dot(u_taps, total.astype(BF)).astype(BF), v_taps)
+            halo = -step_ref[sub] * gradient
+            for side in range(2):
+                base = edge_ref[0, side, sub] + edge_ref[1, side, sub]
+                halo += dot(base.astype(BF), pick[side])
+            halos.append(halo.T.reshape(facets, 2 * HALO, rows))
+        halo = jnp.concatenate(halos, axis=1).astype(BF)
+        height = 2 * HALO * subs
+        for part in range(rows // 128):
+            halo_ref[:, part * height : (part + 1) * height, :] = halo[
+                :, :, part * 128 : (part + 1) * 128
+            ]
+        sent[1].start()
+        for copy in sent:
+            copy.wait()
 
     hbm = pl.BlockSpec(memory_space=pltpu.HBM)
     return pl.pallas_call(
         kernel,
-        out_shape=jax.ShapeDtypeStruct((facets, vis_rows + pos_rows, 2 * S), BF),
-        in_specs=[hbm] * 4,
-        out_specs=vmem(),
+        out_shape=jax.ShapeDtypeStruct((facets, vis_rows + pos_rows + halo_rows, 2 * S), BF),
+        in_specs=[hbm] * 7,
+        out_specs=hbm,
         scratch_shapes=[
             pltpu.SMEM((subs, blocks), jnp.int32),
             pltpu.SMEM((subs, blocks), jnp.int32),
             pltpu.VMEM((subs, blocks, S, S), BF),
             pltpu.VMEM((subs, blocks, 2, S), jnp.int32),
+            pltpu.VMEM((2, 2, subs, rows, 128), F32),
+            pltpu.SMEM((subs,), F32),
             pltpu.SMEM((subs * facets,), jnp.int32),
             pltpu.VMEM((2, facets * pos_rows, S), F32),
             pltpu.VMEM((2, facets, subs * pairs, S, S), BF),
-            pltpu.SemaphoreType.DMA((CHUNKS + 3,)),
+            pltpu.VMEM((facets, vis_rows + pos_rows, 2 * S), BF),
+            pltpu.VMEM((facets, halo_rows, 2 * S), BF),
+            pltpu.SemaphoreType.DMA((CHUNKS + 10,)),
         ],
         compiler_params=params(60),
         name="pack_blocks",
-    )(destinations[..., 0], column_slots, visibility, uv_positions)
-
-
-def taps(row, col):
-    offset = col - row
-    value = jnp.exp(-0.5 * ((offset.astype(F32) - (KW - 1) / 2.0) / (KW / 4.0)) ** 2)
-    return jnp.where((offset >= 0) & (offset < KW), value, 0.0).astype(BF)
-
-
-def contract_last(a, b):
-    return lax.dot_general(a, b, (((1,), (1,)), ((), ())), preferred_element_type=F32)
-
-
-def contract_first(a, b):
-    return lax.dot_general(a, b, (((0,), (0,)), ((), ())), preferred_element_type=F32)
-
-
-def dot(a, b):
-    return jnp.dot(a, b, preferred_element_type=F32)
+    )(destinations[..., 0], column_slots, visibility, uv_positions, image, dual, steps)
 
 
 def grid_and_step(received, image, dual, steps, pairs, bands):
@@ -134,11 +238,13 @@
     sources = per // pairs
     band_rows = rows // bands
     piece = band_rows + 2 * HALO
-
-    def kernel(step_ref, rec_ref, img_ref, dual_ref, shift_ref, edge_l, edge_r, *rest):
+    pos_rows = -(-2 * subs * pairs // 16) * 16
+    height = 2 * HALO * subs
+
+    def kernel(step_ref, rec_ref, img_ref, dual_ref, shift_ref, *rest):
         piece_refs = rest[:bands]
-        place_ref, acc_ref, den_ref = rest[bands:]
-        place_ref[...] = rec_ref[:, vis_rows:, :].astype(F32)
+        place_ref, acc_ref, den_ref, halo_ref = rest[bands:]
+        place_ref[...] = rec_ref[:, vis_rows : vis_rows + pos_rows, :].astype(F32)
         one = jnp.ones((), BF)
         none = jnp.zeros((), BF)
         lane = lax.broadcasted_iota(jnp.int32, (1, 2 * S), 1)
@@ -178,10 +284,7 @@
                 )
                 acc_ref[sub] = term if it == 0 else acc_ref[sub] + term
 
-        u_taps = taps(
-            lax.broadcasted_iota(jnp.int32, (rows, rows), 1),
-            lax.broadcasted_iota(jnp.int32, (rows, rows), 0),
-        )
+        u_taps = tap_matrix(rows)
         v_taps = taps(
             lax.broadcasted_iota(jnp.int32, (width, width), 0),
             lax.broadcasted_iota(jnp.int32, (width, width), 1),
@@ -198,36 +301,36 @@
             shifted = stepped + dual_ref[sub]
             shift_ref[sub] = shifted
             den_ref[sub, HALO : HALO + rows, :] = shifted
+        halo = jnp.sum(rec_ref[:, vis_rows + pos_rows :, :].astype(F32), axis=0)
+        parts = [halo[n * height : (n + 1) * height] for n in range(rows // 128)]
+        halo = jnp.concatenate(parts + [jnp.zeros((height, 128), F32)], axis=1)
+        steps_in = 128 // band_rows
+        for n in range(steps_in):
+            shift = (HALO - n * band_rows) % (rows + 128)
+            moved = pltpu.roll(halo, shift, 1)
+            for tile in range(bands // steps_in):
+                halo_ref[tile * steps_in + n] = moved[:, tile * 128 : (tile + 1) * 128]
+        blank = jnp.zeros((height, width - 128), F32)
         for k in range(bands):
-            start = pl.multiple_of(lax.rem(me + k, bands) * band_rows, band_rows)
+            band = lax.rem(me + k, bands)
+            start = pl.multiple_of(band * band_rows, band_rows)
             piece_refs[k][...] = jnp.concatenate(
-                [den_ref[sub, pl.ds(start, piece), :] for sub in range(subs)], axis=0
+                [den_ref[sub, pl.ds(start, piece), :] for sub in range(subs)]
+                + [jnp.concatenate([halo_ref[band], blank], axis=1)],
+                axis=0,
             ).astype(BF)
-        pick_row = lax.broadcasted_iota(jnp.int32, (subs * HALO, HALF), 0)
-        pick_lane = lax.broadcasted_iota(jnp.int32, (subs * HALO, HALF), 1)
-        for k in range(bands):
-            for ref, at, base in ((edge_l, 0, 0), (edge_r, width - HALF, HALF - HALO)):
-                total = None
-                for sub in range(subs):
-                    pick = jnp.where(
-                        (pick_row // HALO == sub) & (pick_lane == base + pick_row % HALO), 1.0, 0.0
-                    ).astype(BF)
-                    part = den_ref[sub, k * band_rows : k * band_rows + HALF, at : at + HALF].astype(BF)
-                    term = contract_last(pick, part)
-                    total = term if total is None else total + term
-                ref[k] = total.astype(BF)
-
-    edge = jax.ShapeDtypeStruct((bands, subs * HALO, HALF), BF)
+
     return pl.pallas_call(
         kernel,
-        out_shape=[jax.ShapeDtypeStruct(image.shape, F32), edge, edge]
-        + [jax.ShapeDtypeStruct((subs * piece, width), BF)] * bands,
+        out_shape=[jax.ShapeDtypeStruct(image.shape, F32)]
+        + [jax.ShapeDtypeStruct((subs * piece + height, width), BF)] * bands,
         in_specs=[smem()] + [vmem()] * 3,
-        out_specs=[vmem()] * (3 + bands),
+        out_specs=[vmem()] * (1 + bands),
         scratch_shapes=[
-            pltpu.VMEM((facets, received.shape[1] - vis_rows, 2 * S), F32),
+            pltpu.VMEM((facets, pos_rows, 2 * S), F32),
             pltpu.VMEM((subs, rows, width), F32),
-            pltpu.VMEM((subs, (bands - 1) * band_rows + HALF, width), F32),
+            pltpu.VMEM((subs, rows + 2 * HALO, width), F32),
+            pltpu.VMEM((bands, height, 128), F32),
         ],
         compiler_params=params(),
         name="grid_and_step",
@@ -295,7 +398,7 @@
     )(first, middle, last)
 
 
-def denoise(pieces, edges, first, middle, last, subs, bands, band_rows, width):
+def denoise(pieces, first, middle, last, subs, bands, band_rows, width):
     channels = subs * bands
     piece = band_rows + 2 * HALO
     groups = band_rows // GROUP + 1
@@ -307,24 +410,23 @@
 
     def kernel(first_ref, mid_ref, last_ref, *rest):
         piece_refs = rest[:bands]
-        edge_refs = rest[bands : 2 * bands]
-        out_refs = rest[2 * bands : 3 * bands]
-        x_ref, one_ref, two_ref, noise_ref = rest[3 * bands :]
+        out_refs = rest[bands : 2 * bands]
+        x_ref, one_ref, two_ref, noise_ref = rest[2 * bands :]
         me = lax.axis_index("band")
         facet = lax.axis_index("facet")
         x_ref[:, piece * channels :, :] = jnp.zeros((lanes // 128, 2 * channels, 128), F32)
         one_ref[groups] = jnp.zeros(one_ref.shape[1:], BF)
         place_row = lax.broadcasted_iota(jnp.int32, (2 * subs * HALO, lanes), 0)
         place_lane = lax.broadcasted_iota(jnp.int32, (2 * subs * HALO, lanes), 1)
-        side = place_row // (subs * HALO)
+        side = place_row // HALO % 2
         spot = jnp.where(side == 0, PAD - HALO, PAD + width) + place_row % HALO
         for k in range(bands):
             band = lax.rem(me + bands - k, bands)
             for sub in range(subs):
                 put = jnp.where(
-                    (place_lane == spot) & (place_row // HALO % subs == sub), 1.0, 0.0
+                    (place_lane == spot) & (place_row // (2 * HALO) == sub), 1.0, 0.0
                 ).astype(BF)
-                halo = contract_first(edge_refs[k][...], put)[:piece]
+                halo = contract_first(piece_refs[k][subs * piece :, 0:128], put)[:piece]
                 own = piece_refs[k][sub * piece : (sub + 1) * piece, :].astype(F32)
                 own = jnp.concatenate([own, jnp.zeros((piece, lanes - width), F32)], axis=1)
                 own = pltpu.roll(own, PAD, 1) + halo
@@ -416,7 +518,7 @@
     return pl.pallas_call(
         kernel,
         out_shape=[jax.ShapeDtypeStruct((subs * band_rows, width), BF)] * bands,
-        in_specs=[vmem()] * (3 + 2 * bands),
+        in_specs=[vmem()] * (3 + bands),
         out_specs=[vmem()] * bands,
         scratch_shapes=[
             pltpu.VMEM((lanes // 128, (groups * GROUP + 2) * channels, 128), F32),
@@ -426,7 +528,7 @@
         ],
         compiler_params=params(32),
         name="denoise",
-    )(first, middle, last, *pieces, *edges)
+    )(first, middle, last, *pieces)
 
 
 def finish(shifted, noises, bands):
@@ -480,22 +582,22 @@
     subs, blocks = visibility.shape[:2]
     rows, width = image_cube.shape[1:]
     pairs = max(2, 2 * blocks // facets) // 2
-    packed = pack_blocks(visibility, uv_positions, destinations, column_slots, facets, pairs)
+    packed = pack_blocks(
+        visibility,
+        uv_positions,
+        destinations,
+        column_slots,
+        image_cube,
+        dual_cube,
+        step_sizes,
+        facets,
+        pairs,
+    )
     received = lax.all_to_all(packed, "facet", split_axis=0, concat_axis=0, tiled=True)
     weights = weight_matrices(conv_first, conv_middle, conv_last)
-    shifted, edge_l, edge_r, *pieces = grid_and_step(
-        received, image_cube, dual_cube, step_sizes, pairs, bands
-    )
-    from_left = lax.ppermute(edge_r, "facet", [(i, i + 1) for i in range(facets - 1)])
-    from_right = lax.ppermute(edge_l, "facet", [(i + 1, i) for i in range(facets - 1)])
-    edge = jnp.concatenate([from_left, from_right], axis=1)
-    me = lax.axis_index("band")
-    edge_parts = [
-        lax.dynamic_index_in_dim(edge, (me + k) % bands, 0, keepdims=False) for k in range(bands)
-    ]
+    shifted, *pieces = grid_and_step(received, image_cube, dual_cube, step_sizes, pairs, bands)
     pieces = exchange(pieces, bands)
-    edges = exchange(edge_parts, bands)
-    noises = denoise(pieces, edges, *weights, subs, bands, rows // bands, width)
+    noises = denoise(pieces, *weights, subs, bands, rows // bands, width)
     return tuple(finish(shifted, exchange(noises, bands), bands))
 
 

time: 74.6 us -> 69.9 us (0.937)
  starting transfers between devices: 15.8 us -> 11.2 us
  waiting for transfers between devices: 15.7 us -> 11.3 us
  Pallas kernels: 20.6 us -> 24.6 us
    pallas_call x1, Pallas kernels: 3.28 us -> 7.62 us  [pack_blocks(): pl.pallas_call(kernel, out_shape=jax.ShapeDtypeStruct((facets, vis_rows +...]
    ppermute x2 -> x0, starting transfers between devices: 3.15 us -> none  [the longest x1 1.86 us: body(): lax.ppermute(edge_r, 'facet', [(i, i + 1) for i in range(facets - 1)])]
    ppermute x9 -> x6, waiting for transfers between devices: 13.7 us -> 11.3 us  [exchange(): lax.ppermute(parts[k], 'band', [(i, (i + k) % bands) for i in range(bands)])]
    ppermute x2 -> x0, waiting for transfers between devices: 1.99 us -> none  [the longest x1 1.99 us: body(): lax.ppermute(edge_l, 'facet', [(i + 1, i) for i in range(facets - 1)])]
    ppermute x9 -> x6, starting transfers between devices: 12.7 us -> 11.2 us  [exchange(): lax.ppermute(parts[k], 'band', [(i, (i + k) % bands) for i in range(bands)])]
  transfers between devices with their start and end apart: 11 -> 6, of which waited for: 4 -> 5; matrix products, arithmetic and copies ran while one was open for 0% -> 0% of each run, Pallas kernels for 1% -> 1%
where the time goes in v3:
time: 69.9 us; the launch traced here: 69.7 us
  Pallas kernels  24.6 us (35%)
  blocking collectives  21.7 us (31%)
  waiting for transfers between devices  11.3 us (16%)
  starting transfers between devices  11.2 us (16%)
  between operations  0.75 us (1%)
    all_to_all x1, blocking collectives, body(): lax.all_to_all(packed, 'facet', split_axis=0, concat_axis=0, tiled=True)  21.7 us
    ppermute x6, waiting for transfers between devices, exchange(): lax.ppermute(parts[k], 'band', [(i, (i + k) % bands) for i in range(bands)])  11.3 us
    ppermute x6, starting transfers between devices, exchange(): lax.ppermute(parts[k], 'band', [(i, (i + k) % bands) for i in range(bands)])  11.2 us
    pallas_call x1, Pallas kernels, denoise(): pl.pallas_call(kernel, out_shape=[jax.ShapeDtypeStruct((subs * band_rows,...  8.83 us
    pallas_call x1, Pallas kernels, pack_blocks(): pl.pallas_call(kernel, out_shape=jax.ShapeDtypeStruct((facets, vis_rows +...  7.62 us
    pallas_call x1, Pallas kernels, grid_and_step(): pl.pallas_call(kernel, out_shape=[jax.ShapeDtypeStruct(image.shape, F32)]...  6.01 us
  transfers between devices with their start and end apart: 6, of which 5 were waited for; matrix products, arithmetic and copies ran while one was open for 0% of the time, Pallas kernels for 1%

profile of v3, /device:TPU:0, one launch (start us, length us, event | category | flops | bytes accessed | tf_op | source)
XLA Modules:
  0.0 69.7 jit_solution(2708680298360307662)
XLA Ops:
  0.6 7.6 %pack_blocks.1 = bf16[8,560,128]{2,1,0:T(8,128)(2,1)} custom-call(s32[2,32]{1,0:T(2,128)} %bitcast.11, s32[2,32]{1,0:T(2,128)} %slot_hbm.1, bf16[2,32,64,64]{3,2,1,0:T(8,128)(2,1)} %vis_hbm.1, s32[2,32,2,64]{3,2,1,0:T(2,128)} %pos_hbm.1, f32[2,256,384]{2,1,0:T(8,128)} %img_ref.1, f32[2,256,384]{2,1,0:T(8,128)} %dual_ref.1, f32[2]{0:T(128)} %step_ref.1), custom_call_target="tpu_custom_call" | custom-call | tf_op jit(solution)/shard_map/pack_blocks/pallas_call | solution.py:209
  8.3 0.0 copy-start
  8.3 0.0 copy-start.1
  8.3 0.0 copy-start.2
  8.3 21.7 %all_to_all.5.rec_ref = bf16[8,560,128]{2,1,0:T(8,128)(2,1)S(1)} all-to-all(bf16[8,560,128]{2,1,0:T(8,128)(2,1)} %pack_blocks.1), channel_id=1, replica_groups=mesh['facet'=8,'band'=4] {'facet'}, dimensions={0} | all-to-all | bytes 2293760 | tf_op jit(solution)/shard_map/all_to_all | solution.py:596
  30.0 0.0 copy-done
  30.0 0.0 copy-done.1
  30.0 0.0 copy-done.2
  30.0 0.0 copy-start.4
  30.0 0.0 copy-start.3
  30.0 0.0 copy-start.5
  30.1 6.0 %grid_and_step.1 = (f32[2,256,384]{2,1,0:T(8,128)S(1)}, bf16[160,384]{1,0:T(8,128)(2,1)S(1)}, bf16[160,384]{1,0:T(8,128)(2,1)S(1)}, bf16[160,384]{1,0:T(8,128)(2,1)S(1)}, bf16[160,384]{1,0:T(8,128)(2,1)S(1)}) custom-call(f32[2]{0:T(128)S(1)} %copy-done.2, bf16[8,560,128]{2,1,0:T(8,128)(2,1)S(1)} %all_to_all.5.rec_ref, f32[2,256,384]{2,1,0:T(8,128)S(1)} %copy-done, ...), custom_call_target="tpu_custom_call" | custom-call | tf_op jit(solution)/shard_map/grid_and_step/pallas_call | solution.py:323
  36.1 1.6 %collective-permute-start = (bf16[160,384]{1,0:T(8,128)(2,1)S(1)}, bf16[160,384]{1,0:T(8,128)(2,1)S(1)}, u32[]{:S(2)}, u32[]{:S(2)}) collective-permute-start(bf16[160,384]{1,0:T(8,128)(2,1)S(1)} %get-tuple-element.19), channel_id=1, source_target_pairs={{0,1},{1,2},{2,3},{3,0},{4,5},{5,6},{6,7},{7,4},{8,9},{9,10},{10,1... | collective-permute-start | bytes 368648 | tf_op jit(solution)/shard_map/ppermute | solution.py:563
  37.7 2.6 %collective-permute-start.1 = (bf16[160,384]{1,0:T(8,128)(2,1)S(1)}, bf16[160,384]{1,0:T(8,128)(2,1)S(1)}, u32[]{:S(2)}, u32[]{:S(2)}) collective-permute-start(bf16[160,384]{1,0:T(8,128)(2,1)S(1)} %get-tuple-element.20), channel_id=1, source_target_pairs={{0,2},{1,3},{2,0},{3,1},{4,6},{5,7},{6,4},{7,5},{8,10},{9,11},{10,... | collective-permute-start | bytes 368648 | tf_op jit(solution)/shard_map/ppermute | solution.py:563
  40.3 1.4 %collective-permute-start.2 = (bf16[160,384]{1,0:T(8,128)(2,1)S(1)}, bf16[160,384]{1,0:T(8,128)(2,1)S(1)}, u32[]{:S(2)}, u32[]{:S(2)}) collective-permute-start(bf16[160,384]{1,0:T(8,128)(2,1)S(1)} %get-tuple-element.21), channel_id=1, source_target_pairs={{0,3},{1,0},{2,1},{3,2},{4,7},{5,4},{6,5},{7,6},{8,11},{9,8},{10,9... | collective-permute-start | bytes 368648 | tf_op jit(solution)/shard_map/ppermute | solution.py:563
  41.7 0.0 copy-done.4
  41.7 0.0 copy-done.3
  41.7 0.1 copy.16
  41.8 0.0 copy-done.5
  41.9 0.1 copy.18.last_ref
  42.0 0.8 %weight_matrices.1 = (bf16[240,512]{1,0:T(8,128)(2,1)S(1)}, bf16[1152,256]{1,0:T(8,128)(2,1)S(1)}, bf16[768,256]{1,0:T(8,128)(2,1)S(1)}) custom-call(bf16[3,3,8,64]{3,2,1,0:T(8,128)(2,1)S(1)} %bitcast.10, bf16[3,3,64,64]{3,2,1,0:T(8,128)(2,1)S(1)} %bitcast.9, bf16[3,64,24]{2,1,0:T(8,128)(2,1)S(1)} %copy.18.last_ref), custom_call_target="tpu_custom_call" | custom-call | flops 1048576 | bytes 1048576 | tf_op jit(solution)/shard_map/weight_matrices/pallas_call | solution.py:386
  42.8 1.4 %collective-permute-done.rest_1_ = bf16[160,384]{1,0:T(8,128)(2,1)S(1)} collective-permute-done((bf16[160,384]{1,0:T(8,128)(2,1)S(1)}, bf16[160,384]{1,0:T(8,128)(2,1)S(1)}, u32[]{:S(2)}, u32[]{:S(2)}) %collective-permute-start) | collective-permute-done | bytes 122912 | tf_op jit(solution)/shard_map/ppermute | solution.py:563
  44.2 4.0 %collective-permute-done.1.rest_2_ = bf16[160,384]{1,0:T(8,128)(2,1)S(1)} collective-permute-done((bf16[160,384]{1,0:T(8,128)(2,1)S(1)}, bf16[160,384]{1,0:T(8,128)(2,1)S(1)}, u32[]{:S(2)}, u32[]{:S(2)}) %collective-permute-start.1) | collective-permute-done | bytes 122912 | tf_op jit(solution)/shard_map/ppermute | solution.py:563
  48.3 0.0 collective-permute-done.2.rest_3_
  48.3 8.8 %denoise.1 = (bf16[128,384]{1,0:T(8,128)(2,1)S(1)}, bf16[128,384]{1,0:T(8,128)(2,1)S(1)}, bf16[128,384]{1,0:T(8,128)(2,1)S(1)}, bf16[128,384]{1,0:T(8,128)(2,1)S(1)}) custom-call(bf16[240,512]{1,0:T(8,128)(2,1)S(1)} %get-tuple-element.15.first_ref, bf16[1152,256]{1,0:T(8,128)(2,1)S(1)} %get-tuple-element.16.mid_ref, ...), custom_call_target="tpu_custom_call" | custom-call | tf_op jit(solution)/shard_map/denoise/pallas_call | solution.py:518
  57.1 3.1 %collective-permute-start.3 = (bf16[128,384]{1,0:T(8,128)(2,1)S(1)}, bf16[128,384]{1,0:T(8,128)(2,1)S(1)}, u32[]{:S(2)}, u32[]{:S(2)}) collective-permute-start(bf16[128,384]{1,0:T(8,128)(2,1)S(1)} %get-tuple-element.23), channel_id=1, source_target_pairs={{0,1},{1,2},{2,3},{3,0},{4,5},{5,6},{6,7},{7,4},{8,9},{9,10},{10,1... | collective-permute-start | bytes 294920 | tf_op jit(solution)/shard_map/ppermute | solution.py:563
  60.3 1.6 %collective-permute-start.4 = (bf16[128,384]{1,0:T(8,128)(2,1)S(1)}, bf16[128,384]{1,0:T(8,128)(2,1)S(1)}, u32[]{:S(2)}, u32[]{:S(2)}) collective-permute-start(bf16[128,384]{1,0:T(8,128)(2,1)S(1)} %get-tuple-element.24), channel_id=1, source_target_pairs={{0,2},{1,3},{2,0},{3,1},{4,6},{5,7},{6,4},{7,5},{8,10},{9,11},{10,... | collective-permute-start | bytes 294920 | tf_op jit(solution)/shard_map/ppermute | solution.py:563
  61.9 0.8 %collective-permute-start.5 = (bf16[128,384]{1,0:T(8,128)(2,1)S(1)}, bf16[128,384]{1,0:T(8,128)(2,1)S(1)}, u32[]{:S(2)}, u32[]{:S(2)}) collective-permute-start(bf16[128,384]{1,0:T(8,128)(2,1)S(1)} %get-tuple-element.25), channel_id=1, source_target_pairs={{0,3},{1,0},{2,1},{3,2},{4,7},{5,4},{6,5},{7,6},{8,11},{9,8},{10,9... | collective-permute-start | bytes 294920 | tf_op jit(solution)/shard_map/ppermute | solution.py:563
  62.7 2.0 %collective-permute-done.3.rest_1_ = bf16[128,384]{1,0:T(8,128)(2,1)S(1)} collective-permute-done((bf16[128,384]{1,0:T(8,128)(2,1)S(1)}, bf16[128,384]{1,0:T(8,128)(2,1)S(1)}, u32[]{:S(2)}, u32[]{:S(2)}) %collective-permute-start.3) | collective-permute-done | bytes 98336 | tf_op jit(solution)/shard_map/ppermute | solution.py:563
  64.7 3.6 %collective-permute-done.4.rest_2_ = bf16[128,384]{1,0:T(8,128)(2,1)S(1)} collective-permute-done((bf16[128,384]{1,0:T(8,128)(2,1)S(1)}, bf16[128,384]{1,0:T(8,128)(2,1)S(1)}, u32[]{:S(2)}, u32[]{:S(2)}) %collective-permute-start.4) | collective-permute-done | bytes 98336 | tf_op jit(solution)/shard_map/ppermute | solution.py:563
  68.2 0.2 collective-permute-done.5.rest_3_
  68.5 1.3 %finish.1 = (f32[2,256,384]{2,1,0:T(8,128)}, f32[2,256,384]{2,1,0:T(8,128)}) custom-call(f32[2,256,384]{2,1,0:T(8,128)S(1)} %get-tuple-element.14.shift_ref, bf16[128,384]{1,0:T(8,128)(2,1)S(1)} %get-tuple-element.22.rest_0_, bf16[128,384]{1,0:T(8,128)(2,1)S(1)} %collective-permute-done.3.rest_1_, bf16[128,384]{1,0:T(8,128)(2,1)S(1)} %collective-permute-done.4.rest_2_, ...), custom_call_target="tpu_custom_call" | custom-call | tf_op jit(solution)/shard_map/finish/pallas_call | solution.py:551
  (3 shorter events, 0.0 us)
Async XLA Ops:
  8.3 21.8 %copy-start = (f32[2,256,384]{2,1,0:T(8,128)S(1)}, f32[2,256,384]{2,1,0:T(8,128)}, u32[]{:S(2)}) copy-start(f32[2,256,384]{2,1,0:T(8,128)} %img_ref.1) | copy-start | bytes 2359300
  8.3 21.7 %copy-start.1 = (f32[2,256,384]{2,1,0:T(8,128)S(1)}, f32[2,256,384]{2,1,0:T(8,128)}, u32[]{:S(2)}) copy-start(f32[2,256,384]{2,1,0:T(8,128)} %dual_ref.1) | copy-start | bytes 2359300
  8.3 21.7 %copy-start.2 = (f32[2]{0:T(128)S(1)}, f32[2]{0:T(128)}, u32[]{:S(2)}) copy-start(f32[2]{0:T(128)} %step_ref.1) | copy-start | bytes 28
  30.0 11.6 %copy-start.4 = (bf16[64,8,3,3]{0,1,3,2:T(8,128)(2,1)S(1)}, bf16[64,8,3,3]{0,1,3,2:T(8,128)(2,1)}, u32[]{:S(2)}) copy-start(bf16[64,8,3,3]{0,1,3,2:T(8,128)(2,1)} %param.17) | copy-start | bytes 27652
  30.0 11.6 %copy-start.3 = (bf16[64,64,3,3]{1,0,3,2:T(8,128)(2,1)S(1)}, bf16[64,64,3,3]{1,0,3,2:T(8,128)(2,1)}, u32[]{:S(2)}) copy-start(bf16[64,64,3,3]{1,0,3,2:T(8,128)(2,1)} %param.18) | copy-start | bytes 221188
  30.0 11.8 %copy-start.5 = (bf16[8,64,3,3]{1,0,3,2:T(8,128)(2,1)S(1)}, bf16[8,64,3,3]{1,0,3,2:T(8,128)(2,1)}, u32[]{:S(2)}) copy-start(bf16[8,64,3,3]{1,0,3,2:T(8,128)(2,1)} %param.19) | copy-start | bytes 27652
  36.1 8.1 %collective-permute-start = (bf16[160,384]{1,0:T(8,128)(2,1)S(1)}, bf16[160,384]{1,0:T(8,128)(2,1)S(1)}, u32[]{:S(2)}, u32[]{:S(2)}) collective-permute-start(bf16[160,384]{1,0:T(8,128)(2,1)S(1)} %get-tuple-element.19), channel_id=1, source_target_pairs={{0,1},{1,2},{2,3},{3,0},{4,5},{5,6},{6,7},{7,4},{8,9},{9,10},{10,1... | collective-permute-start | bytes 368648 | tf_op jit(solution)/shard_map/ppermute | solution.py:563
  37.7 10.6 %collective-permute-start.1 = (bf16[160,384]{1,0:T(8,128)(2,1)S(1)}, bf16[160,384]{1,0:T(8,128)(2,1)S(1)}, u32[]{:S(2)}, u32[]{:S(2)}) collective-permute-start(bf16[160,384]{1,0:T(8,128)(2,1)S(1)} %get-tuple-element.20), channel_id=1, source_target_pairs={{0,2},{1,3},{2,0},{3,1},{4,6},{5,7},{6,4},{7,5},{8,10},{9,11},{10,... | collective-permute-start | bytes 368648 | tf_op jit(solution)/shard_map/ppermute | solution.py:563
  40.3 8.0 %collective-permute-start.2 = (bf16[160,384]{1,0:T(8,128)(2,1)S(1)}, bf16[160,384]{1,0:T(8,128)(2,1)S(1)}, u32[]{:S(2)}, u32[]{:S(2)}) collective-permute-start(bf16[160,384]{1,0:T(8,128)(2,1)S(1)} %get-tuple-element.21), channel_id=1, source_target_pairs={{0,3},{1,0},{2,1},{3,2},{4,7},{5,4},{6,5},{7,6},{8,11},{9,8},{10,9... | collective-permute-start | bytes 368648 | tf_op jit(solution)/shard_map/ppermute | solution.py:563
  57.1 7.6 %collective-permute-start.3 = (bf16[128,384]{1,0:T(8,128)(2,1)S(1)}, bf16[128,384]{1,0:T(8,128)(2,1)S(1)}, u32[]{:S(2)}, u32[]{:S(2)}) collective-permute-start(bf16[128,384]{1,0:T(8,128)(2,1)S(1)} %get-tuple-element.23), channel_id=1, source_target_pairs={{0,1},{1,2},{2,3},{3,0},{4,5},{5,6},{6,7},{7,4},{8,9},{9,10},{10,1... | collective-permute-start | bytes 294920 | tf_op jit(solution)/shard_map/ppermute | solution.py:563
  60.3 8.0 %collective-permute-start.4 = (bf16[128,384]{1,0:T(8,128)(2,1)S(1)}, bf16[128,384]{1,0:T(8,128)(2,1)S(1)}, u32[]{:S(2)}, u32[]{:S(2)}) collective-permute-start(bf16[128,384]{1,0:T(8,128)(2,1)S(1)} %get-tuple-element.24), channel_id=1, source_target_pairs={{0,2},{1,3},{2,0},{3,1},{4,6},{5,7},{6,4},{7,5},{8,10},{9,11},{10,... | collective-permute-start | bytes 294920 | tf_op jit(solution)/shard_map/ppermute | solution.py:563
  61.9 6.6 %collective-permute-start.5 = (bf16[128,384]{1,0:T(8,128)(2,1)S(1)}, bf16[128,384]{1,0:T(8,128)(2,1)S(1)}, u32[]{:S(2)}, u32[]{:S(2)}) collective-permute-start(bf16[128,384]{1,0:T(8,128)(2,1)S(1)} %get-tuple-element.25), channel_id=1, source_target_pairs={{0,3},{1,0},{2,1},{3,2},{4,7},{5,4},{6,5},{7,6},{8,11},{9,8},{10,9... | collective-permute-start | bytes 294920 | tf_op jit(solution)/shard_map/ppermute | solution.py:563

commit v4 on v3

--- a/solution.py
+++ b/solution.py
@@ -15,6 +15,7 @@
 GROUP = 8
 CH = 64
 CHUNKS = 4
+DEPTH = 2
 BF = jnp.bfloat16
 F32 = jnp.float32
 
@@ -102,9 +103,9 @@
         cell = cell_row % HALO + (width - KW - HALO + 1) * (cell_row // HALO % 2) - CENTRE
         cell = jnp.where(cell_lane // S == cell_row // (2 * HALO), cell, 2 * P_SIZE)
         cell = cell.astype(F32).astype(BF)
-        lane = lax.broadcasted_iota(jnp.int32, (1, 4 * HALO), 1)
+        lane = lax.broadcasted_iota(jnp.int32, (1, wide), 1)
         mine = [
-            jnp.where(lane // (2 * HALO) == block, 1.0, 0.0).astype(BF) for block in range(2)
+            jnp.where(lane // (2 * HALO) % 2 == block, 1.0, 0.0).astype(BF) for block in range(2)
         ]
         row_id = lax.broadcasted_iota(jnp.int32, (rows, 2 * S), 0).astype(F32).astype(BF)
         yes = jnp.ones((), BF)
@@ -175,9 +176,8 @@
             copy.wait()
         halos = []
         for sub in range(subs):
-            totals = []
+            hots, parts = [], []
             for facet in range(facets):
-                hots, parts = [], []
                 for pair in range(pairs):
                     at = sub * pairs + pair
                     where = facet * pos_rows + at
@@ -185,10 +185,14 @@
                     v_row = both[where + subs * pairs : where + subs * pairs + 1].astype(BF)
                     hots.append(jnp.where(row_id == u_row, yes, no))
                     hot = jnp.where(cell == v_row, yes, no)
-                    found = contract_last(main_ref[facet, at * S : (at + 1) * S, :], hot).astype(BF)
+                    found = contract_last(main_ref[facet, at * S : (at + 1) * S, :], hot)
+                    left, right = facet * 4 * HALO, (facets - facet - 1) * 4 * HALO
+                    row = [jnp.zeros((S, left), F32)] if left else []
+                    row += [found]
+                    row += [jnp.zeros((S, right), F32)] if right else []
+                    found = jnp.concatenate(row, axis=1).astype(BF)
                     parts += [found * mine[0], found * mine[1]]
-                totals.append(dot(jnp.concatenate(hots, axis=1), jnp.concatenate(parts, axis=0)))
-            total = jnp.concatenate(totals, axis=1)
+            total = dot(jnp.concatenate(hots, axis=1), jnp.concatenate(parts, axis=0))
             gradient = dot(dot(u_taps, total.astype(BF)).astype(BF), v_taps)
             halo = -step_ref[sub] * gradient
             for side in range(2):
@@ -254,6 +258,8 @@
         row_id = lax.broadcasted_iota(jnp.int32, (rows, 2 * S), 0).astype(F32).astype(BF)
         col_id = (lax.broadcasted_iota(jnp.int32, (width, 2 * S), 0) - CENTRE).astype(F32).astype(BF)
 
+        spreads = [[] for _ in range(subs)]
+        hots = [[] for _ in range(subs)]
         for it in range(facets // sources):
             for sub in range(subs):
                 first, second = [], []
@@ -279,10 +285,14 @@
                         axis=0,
                     )
                     spread.append(dot(hot, block).astype(BF))
-                term = contract_last(
-                    jnp.concatenate(spread, axis=1), jnp.concatenate(second, axis=1)
-                )
-                acc_ref[sub] = term if it == 0 else acc_ref[sub] + term
+                spreads[sub] += spread
+                hots[sub] += second
+                if it % DEPTH == DEPTH - 1:
+                    term = contract_last(
+                        jnp.concatenate(spreads[sub], axis=1), jnp.concatenate(hots[sub], axis=1)
+                    )
+                    acc_ref[sub] = term if it < DEPTH else acc_ref[sub] + term
+                    spreads[sub], hots[sub] = [], []
 
         u_taps = tap_matrix(rows)
         v_taps = taps(

time: 69.9 us -> 66.5 us (0.951)
  Pallas kernels: 24.6 us -> 21.1 us
    pallas_call x1, Pallas kernels: 7.62 us -> 5.5 us  [pack_blocks(): pl.pallas_call(kernel, out_shape=jax.ShapeDtypeStruct((facets, vis_rows +...]
    pallas_call x1, Pallas kernels: 6.01 us -> 4.7 us  [grid_and_step(): pl.pallas_call(kernel, out_shape=[jax.ShapeDtypeStruct(image.shape, F32)]...]
where the time goes in v4:
time: 66.5 us; the launch traced here: 66.3 us
  blocking collectives  21.7 us (33%)
  Pallas kernels  21.1 us (32%)
  waiting for transfers between devices  11.3 us (17%)
  starting transfers between devices  11.1 us (17%)
  between operations  0.75 us (1%)
    all_to_all x1, blocking collectives, body(): lax.all_to_all(packed, 'facet', split_axis=0, concat_axis=0, tiled=True)  21.7 us
    ppermute x6, waiting for transfers between devices, exchange(): lax.ppermute(parts[k], 'band', [(i, (i + k) % bands) for i in range(bands)])  11.3 us
    ppermute x6, starting transfers between devices, exchange(): lax.ppermute(parts[k], 'band', [(i, (i + k) % bands) for i in range(bands)])  11.1 us
    pallas_call x1, Pallas kernels, denoise(): pl.pallas_call(kernel, out_shape=[jax.ShapeDtypeStruct((subs * band_rows,...  8.83 us
    pallas_call x1, Pallas kernels, pack_blocks(): pl.pallas_call(kernel, out_shape=jax.ShapeDtypeStruct((facets, vis_rows +...  5.5 us
    pallas_call x1, Pallas kernels, grid_and_step(): pl.pallas_call(kernel, out_shape=[jax.ShapeDtypeStruct(image.shape, F32)]...  4.7 us
  transfers between devices with their start and end apart: 6, of which 5 were waited for; matrix products, arithmetic and copies ran while one was open for 0% of the time, Pallas kernels for 1%

profile of v4, /device:TPU:0, one launch (start us, length us, event | category | flops | bytes accessed | tf_op | source)
XLA Modules:
  0.0 66.3 jit_solution(1414430541166488837)
XLA Ops:
  0.6 5.5 %pack_blocks.1 = bf16[8,560,128]{2,1,0:T(8,128)(2,1)} custom-call(s32[2,32]{1,0:T(2,128)} %bitcast.11, s32[2,32]{1,0:T(2,128)} %slot_hbm.1, bf16[2,32,64,64]{3,2,1,0:T(8,128)(2,1)} %vis_hbm.1, s32[2,32,2,64]{3,2,1,0:T(2,128)} %pos_hbm.1, f32[2,256,384]{2,1,0:T(8,128)} %img_ref.1, f32[2,256,384]{2,1,0:T(8,128)} %dual_ref.1, f32[2]{0:T(128)} %step_ref.1), custom_call_target="tpu_custom_call" | custom-call | tf_op jit(solution)/shard_map/pack_blocks/pallas_call | solution.py:213
  6.1 0.0 copy-start
  6.1 0.0 copy-start.1
  6.2 0.0 copy-start.2
  6.2 21.7 %all_to_all.5.rec_ref = bf16[8,560,128]{2,1,0:T(8,128)(2,1)S(1)} all-to-all(bf16[8,560,128]{2,1,0:T(8,128)(2,1)} %pack_blocks.1), channel_id=1, replica_groups=mesh['facet'=8,'band'=4] {'facet'}, dimensions={0} | all-to-all | bytes 2293760 | tf_op jit(solution)/shard_map/all_to_all | solution.py:606
  27.9 0.0 copy-done
  27.9 0.0 copy-done.1
  27.9 0.0 copy-done.2
  27.9 0.0 copy-start.4
  27.9 0.0 copy-start.3
  27.9 0.0 copy-start.5
  27.9 4.7 %grid_and_step.1 = (f32[2,256,384]{2,1,0:T(8,128)S(1)}, bf16[160,384]{1,0:T(8,128)(2,1)S(1)}, bf16[160,384]{1,0:T(8,128)(2,1)S(1)}, bf16[160,384]{1,0:T(8,128)(2,1)S(1)}, bf16[160,384]{1,0:T(8,128)(2,1)S(1)}) custom-call(f32[2]{0:T(128)S(1)} %copy-done.2, bf16[8,560,128]{2,1,0:T(8,128)(2,1)S(1)} %all_to_all.5.rec_ref, f32[2,256,384]{2,1,0:T(8,128)S(1)} %copy-done, ...), custom_call_target="tpu_custom_call" | custom-call | tf_op jit(solution)/shard_map/grid_and_step/pallas_call | solution.py:333
  32.6 1.6 %collective-permute-start = (bf16[160,384]{1,0:T(8,128)(2,1)S(1)}, bf16[160,384]{1,0:T(8,128)(2,1)S(1)}, u32[]{:S(2)}, u32[]{:S(2)}) collective-permute-start(bf16[160,384]{1,0:T(8,128)(2,1)S(1)} %get-tuple-element.19), channel_id=1, source_target_pairs={{0,1},{1,2},{2,3},{3,0},{4,5},{5,6},{6,7},{7,4},{8,9},{9,10},{10,1... | collective-permute-start | bytes 368648 | tf_op jit(solution)/shard_map/ppermute | solution.py:573
  34.3 2.6 %collective-permute-start.1 = (bf16[160,384]{1,0:T(8,128)(2,1)S(1)}, bf16[160,384]{1,0:T(8,128)(2,1)S(1)}, u32[]{:S(2)}, u32[]{:S(2)}) collective-permute-start(bf16[160,384]{1,0:T(8,128)(2,1)S(1)} %get-tuple-element.20), channel_id=1, source_target_pairs={{0,2},{1,3},{2,0},{3,1},{4,6},{5,7},{6,4},{7,5},{8,10},{9,11},{10,... | collective-permute-start | bytes 368648 | tf_op jit(solution)/shard_map/ppermute | solution.py:573
  36.9 1.4 %collective-permute-start.2 = (bf16[160,384]{1,0:T(8,128)(2,1)S(1)}, bf16[160,384]{1,0:T(8,128)(2,1)S(1)}, u32[]{:S(2)}, u32[]{:S(2)}) collective-permute-start(bf16[160,384]{1,0:T(8,128)(2,1)S(1)} %get-tuple-element.21), channel_id=1, source_target_pairs={{0,3},{1,0},{2,1},{3,2},{4,7},{5,4},{6,5},{7,6},{8,11},{9,8},{10,9... | collective-permute-start | bytes 368648 | tf_op jit(solution)/shard_map/ppermute | solution.py:573
  38.2 0.0 copy-done.4
  38.2 0.0 copy-done.3
  38.2 0.1 copy.16
  38.4 0.0 copy-done.5
  38.4 0.1 copy.18.last_ref
  38.5 0.8 %weight_matrices.1 = (bf16[240,512]{1,0:T(8,128)(2,1)S(1)}, bf16[1152,256]{1,0:T(8,128)(2,1)S(1)}, bf16[768,256]{1,0:T(8,128)(2,1)S(1)}) custom-call(bf16[3,3,8,64]{3,2,1,0:T(8,128)(2,1)S(1)} %bitcast.10, bf16[3,3,64,64]{3,2,1,0:T(8,128)(2,1)S(1)} %bitcast.9, bf16[3,64,24]{2,1,0:T(8,128)(2,1)S(1)} %copy.18.last_ref), custom_call_target="tpu_custom_call" | custom-call | flops 1048576 | bytes 1048576 | tf_op jit(solution)/shard_map/weight_matrices/pallas_call | solution.py:396
  39.3 1.5 %collective-permute-done.rest_1_ = bf16[160,384]{1,0:T(8,128)(2,1)S(1)} collective-permute-done((bf16[160,384]{1,0:T(8,128)(2,1)S(1)}, bf16[160,384]{1,0:T(8,128)(2,1)S(1)}, u32[]{:S(2)}, u32[]{:S(2)}) %collective-permute-start) | collective-permute-done | bytes 122912 | tf_op jit(solution)/shard_map/ppermute | solution.py:573
  40.8 4.0 %collective-permute-done.1.rest_2_ = bf16[160,384]{1,0:T(8,128)(2,1)S(1)} collective-permute-done((bf16[160,384]{1,0:T(8,128)(2,1)S(1)}, bf16[160,384]{1,0:T(8,128)(2,1)S(1)}, u32[]{:S(2)}, u32[]{:S(2)}) %collective-permute-start.1) | collective-permute-done | bytes 122912 | tf_op jit(solution)/shard_map/ppermute | solution.py:573
  44.8 0.0 collective-permute-done.2.rest_3_
  44.8 8.8 %denoise.1 = (bf16[128,384]{1,0:T(8,128)(2,1)S(1)}, bf16[128,384]{1,0:T(8,128)(2,1)S(1)}, bf16[128,384]{1,0:T(8,128)(2,1)S(1)}, bf16[128,384]{1,0:T(8,128)(2,1)S(1)}) custom-call(bf16[240,512]{1,0:T(8,128)(2,1)S(1)} %get-tuple-element.15.first_ref, bf16[1152,256]{1,0:T(8,128)(2,1)S(1)} %get-tuple-element.16.mid_ref, ...), custom_call_target="tpu_custom_call" | custom-call | tf_op jit(solution)/shard_map/denoise/pallas_call | solution.py:528
  53.7 3.1 %collective-permute-start.3 = (bf16[128,384]{1,0:T(8,128)(2,1)S(1)}, bf16[128,384]{1,0:T(8,128)(2,1)S(1)}, u32[]{:S(2)}, u32[]{:S(2)}) collective-permute-start(bf16[128,384]{1,0:T(8,128)(2,1)S(1)} %get-tuple-element.23), channel_id=1, source_target_pairs={{0,1},{1,2},{2,3},{3,0},{4,5},{5,6},{6,7},{7,4},{8,9},{9,10},{10,1... | collective-permute-start | bytes 294920 | tf_op jit(solution)/shard_map/ppermute | solution.py:573
  56.8 1.6 %collective-permute-start.4 = (bf16[128,384]{1,0:T(8,128)(2,1)S(1)}, bf16[128,384]{1,0:T(8,128)(2,1)S(1)}, u32[]{:S(2)}, u32[]{:S(2)}) collective-permute-start(bf16[128,384]{1,0:T(8,128)(2,1)S(1)} %get-tuple-element.24), channel_id=1, source_target_pairs={{0,2},{1,3},{2,0},{3,1},{4,6},{5,7},{6,4},{7,5},{8,10},{9,11},{10,... | collective-permute-start | bytes 294920 | tf_op jit(solution)/shard_map/ppermute | solution.py:573
  58.4 0.8 %collective-permute-start.5 = (bf16[128,384]{1,0:T(8,128)(2,1)S(1)}, bf16[128,384]{1,0:T(8,128)(2,1)S(1)}, u32[]{:S(2)}, u32[]{:S(2)}) collective-permute-start(bf16[128,384]{1,0:T(8,128)(2,1)S(1)} %get-tuple-element.25), channel_id=1, source_target_pairs={{0,3},{1,0},{2,1},{3,2},{4,7},{5,4},{6,5},{7,6},{8,11},{9,8},{10,9... | collective-permute-start | bytes 294920 | tf_op jit(solution)/shard_map/ppermute | solution.py:573
  59.3 2.0 %collective-permute-done.3.rest_1_ = bf16[128,384]{1,0:T(8,128)(2,1)S(1)} collective-permute-done((bf16[128,384]{1,0:T(8,128)(2,1)S(1)}, bf16[128,384]{1,0:T(8,128)(2,1)S(1)}, u32[]{:S(2)}, u32[]{:S(2)}) %collective-permute-start.3) | collective-permute-done | bytes 98336 | tf_op jit(solution)/shard_map/ppermute | solution.py:573
  61.2 3.6 %collective-permute-done.4.rest_2_ = bf16[128,384]{1,0:T(8,128)(2,1)S(1)} collective-permute-done((bf16[128,384]{1,0:T(8,128)(2,1)S(1)}, bf16[128,384]{1,0:T(8,128)(2,1)S(1)}, u32[]{:S(2)}, u32[]{:S(2)}) %collective-permute-start.4) | collective-permute-done | bytes 98336 | tf_op jit(solution)/shard_map/ppermute | solution.py:573
  64.8 0.2 collective-permute-done.5.rest_3_
  65.0 1.3 %finish.1 = (f32[2,256,384]{2,1,0:T(8,128)}, f32[2,256,384]{2,1,0:T(8,128)}) custom-call(f32[2,256,384]{2,1,0:T(8,128)S(1)} %get-tuple-element.14.shift_ref, bf16[128,384]{1,0:T(8,128)(2,1)S(1)} %get-tuple-element.22.rest_0_, bf16[128,384]{1,0:T(8,128)(2,1)S(1)} %collective-permute-done.3.rest_1_, bf16[128,384]{1,0:T(8,128)(2,1)S(1)} %collective-permute-done.4.rest_2_, ...), custom_call_target="tpu_custom_call" | custom-call | tf_op jit(solution)/shard_map/finish/pallas_call | solution.py:561
  (3 shorter events, 0.0 us)
Async XLA Ops:
  6.1 21.8 %copy-start = (f32[2,256,384]{2,1,0:T(8,128)S(1)}, f32[2,256,384]{2,1,0:T(8,128)}, u32[]{:S(2)}) copy-start(f32[2,256,384]{2,1,0:T(8,128)} %img_ref.1) | copy-start | bytes 2359300
  6.1 21.8 %copy-start.1 = (f32[2,256,384]{2,1,0:T(8,128)S(1)}, f32[2,256,384]{2,1,0:T(8,128)}, u32[]{:S(2)}) copy-start(f32[2,256,384]{2,1,0:T(8,128)} %dual_ref.1) | copy-start | bytes 2359300
  6.2 21.7 %copy-start.2 = (f32[2]{0:T(128)S(1)}, f32[2]{0:T(128)}, u32[]{:S(2)}) copy-start(f32[2]{0:T(128)} %step_ref.1) | copy-start | bytes 28
  27.9 10.3 %copy-start.4 = (bf16[64,8,3,3]{0,1,3,2:T(8,128)(2,1)S(1)}, bf16[64,8,3,3]{0,1,3,2:T(8,128)(2,1)}, u32[]{:S(2)}) copy-start(bf16[64,8,3,3]{0,1,3,2:T(8,128)(2,1)} %param.17) | copy-start | bytes 27652
  27.9 10.3 %copy-start.3 = (bf16[64,64,3,3]{1,0,3,2:T(8,128)(2,1)S(1)}, bf16[64,64,3,3]{1,0,3,2:T(8,128)(2,1)}, u32[]{:S(2)}) copy-start(bf16[64,64,3,3]{1,0,3,2:T(8,128)(2,1)} %param.18) | copy-start | bytes 221188
  27.9 10.5 %copy-start.5 = (bf16[8,64,3,3]{1,0,3,2:T(8,128)(2,1)S(1)}, bf16[8,64,3,3]{1,0,3,2:T(8,128)(2,1)}, u32[]{:S(2)}) copy-start(bf16[8,64,3,3]{1,0,3,2:T(8,128)(2,1)} %param.19) | copy-start | bytes 27652
  32.6 8.2 %collective-permute-start = (bf16[160,384]{1,0:T(8,128)(2,1)S(1)}, bf16[160,384]{1,0:T(8,128)(2,1)S(1)}, u32[]{:S(2)}, u32[]{:S(2)}) collective-permute-start(bf16[160,384]{1,0:T(8,128)(2,1)S(1)} %get-tuple-element.19), channel_id=1, source_target_pairs={{0,1},{1,2},{2,3},{3,0},{4,5},{5,6},{6,7},{7,4},{8,9},{9,10},{10,1... | collective-permute-start | bytes 368648 | tf_op jit(solution)/shard_map/ppermute | solution.py:573
  34.3 10.5 %collective-permute-start.1 = (bf16[160,384]{1,0:T(8,128)(2,1)S(1)}, bf16[160,384]{1,0:T(8,128)(2,1)S(1)}, u32[]{:S(2)}, u32[]{:S(2)}) collective-permute-start(bf16[160,384]{1,0:T(8,128)(2,1)S(1)} %get-tuple-element.20), channel_id=1, source_target_pairs={{0,2},{1,3},{2,0},{3,1},{4,6},{5,7},{6,4},{7,5},{8,10},{9,11},{10,... | collective-permute-start | bytes 368648 | tf_op jit(solution)/shard_map/ppermute | solution.py:573
  36.9 8.0 %collective-permute-start.2 = (bf16[160,384]{1,0:T(8,128)(2,1)S(1)}, bf16[160,384]{1,0:T(8,128)(2,1)S(1)}, u32[]{:S(2)}, u32[]{:S(2)}) collective-permute-start(bf16[160,384]{1,0:T(8,128)(2,1)S(1)} %get-tuple-element.21), channel_id=1, source_target_pairs={{0,3},{1,0},{2,1},{3,2},{4,7},{5,4},{6,5},{7,6},{8,11},{9,8},{10,9... | collective-permute-start | bytes 368648 | tf_op jit(solution)/shard_map/ppermute | solution.py:573
  53.7 7.6 %collective-permute-start.3 = (bf16[128,384]{1,0:T(8,128)(2,1)S(1)}, bf16[128,384]{1,0:T(8,128)(2,1)S(1)}, u32[]{:S(2)}, u32[]{:S(2)}) collective-permute-start(bf16[128,384]{1,0:T(8,128)(2,1)S(1)} %get-tuple-element.23), channel_id=1, source_target_pairs={{0,1},{1,2},{2,3},{3,0},{4,5},{5,6},{6,7},{7,4},{8,9},{9,10},{10,1... | collective-permute-start | bytes 294920 | tf_op jit(solution)/shard_map/ppermute | solution.py:573
  56.8 8.0 %collective-permute-start.4 = (bf16[128,384]{1,0:T(8,128)(2,1)S(1)}, bf16[128,384]{1,0:T(8,128)(2,1)S(1)}, u32[]{:S(2)}, u32[]{:S(2)}) collective-permute-start(bf16[128,384]{1,0:T(8,128)(2,1)S(1)} %get-tuple-element.24), channel_id=1, source_target_pairs={{0,2},{1,3},{2,0},{3,1},{4,6},{5,7},{6,4},{7,5},{8,10},{9,11},{10,... | collective-permute-start | bytes 294920 | tf_op jit(solution)/shard_map/ppermute | solution.py:573
  58.4 6.6 %collective-permute-start.5 = (bf16[128,384]{1,0:T(8,128)(2,1)S(1)}, bf16[128,384]{1,0:T(8,128)(2,1)S(1)}, u32[]{:S(2)}, u32[]{:S(2)}) collective-permute-start(bf16[128,384]{1,0:T(8,128)(2,1)S(1)} %get-tuple-element.25), channel_id=1, source_target_pairs={{0,3},{1,0},{2,1},{3,2},{4,7},{5,4},{6,5},{7,6},{8,11},{9,8},{10,9... | collective-permute-start | bytes 294920 | tf_op jit(solution)/shard_map/ppermute | solution.py:573

commit v5 on v4

--- a/solution.py
+++ b/solution.py
@@ -66,11 +66,10 @@
     chunk = blocks // CHUNKS
     halo_rows = 2 * HALO * subs * (rows // 128)
 
-    def kernel(
-        dest_hbm, slot_hbm, vis_hbm, pos_hbm, img_hbm, dual_hbm, step_hbm, out_hbm,
-        dest_ref, slot_ref, vis_ref, pos_ref, edge_ref, step_ref, count_ref, place_ref, side_ref,
-        main_ref, halo_ref, sems,
-    ):
+    def kernel(dest_hbm, slot_hbm, vis_hbm, pos_hbm, img_hbm, dual_hbm, step_hbm, *rest):
+        out_refs, rest = rest[:facets], rest[facets:]
+        dest_ref, slot_ref, vis_ref, pos_ref, edge_ref, step_ref, count_ref = rest[:7]
+        place_ref, side_ref, main_ref, halo_ref, sems = rest[7:]
         small = [
             pltpu.make_async_copy(dest_hbm, dest_ref, sems.at[CHUNKS]),
             pltpu.make_async_copy(slot_hbm, slot_ref, sems.at[CHUNKS + 1]),
@@ -162,15 +161,24 @@
             main_ref[facet, :vis_rows, :] = both.reshape(vis_rows, 2 * S)
         both = jnp.concatenate([place_ref[0], place_ref[1]], axis=1)
         main_ref[:, vis_rows:, :] = both.astype(BF).reshape(facets, pos_rows, 2 * S)
+        spot = lax.axis_index("facet")
+        main_rows = vis_rows + pos_rows
         sent = [
             pltpu.make_async_copy(
-                main_ref, out_hbm.at[:, pl.ds(0, vis_rows + pos_rows)], sems.at[CHUNKS + 8]
-            ),
+                main_ref.at[spot ^ k], out_refs[k].at[pl.ds(0, main_rows)], sems.at[CHUNKS + 8 + k]
+            )
+            for k in range(facets)
+        ]
+        sent_halo = [
             pltpu.make_async_copy(
-                halo_ref, out_hbm.at[:, pl.ds(vis_rows + pos_rows, halo_rows)], sems.at[CHUNKS + 9]
-            ),
+                halo_ref.at[spot ^ k],
+                out_refs[k].at[pl.ds(main_rows, halo_rows)],
+                sems.at[CHUNKS + 8 + facets + k],
+            )
+            for k in range(facets)
         ]
-        sent[0].start()
+        for copy in sent:
+            copy.start()
 
         for copy in edges:
             copy.wait()
@@ -205,16 +213,17 @@
             halo_ref[:, part * height : (part + 1) * height, :] = halo[
                 :, :, part * 128 : (part + 1) * 128
             ]
-        sent[1].start()
-        for copy in sent:
+        for copy in sent_halo:
+            copy.start()
+        for copy in sent + sent_halo:
             copy.wait()
 
     hbm = pl.BlockSpec(memory_space=pltpu.HBM)
     return pl.pallas_call(
         kernel,
-        out_shape=jax.ShapeDtypeStruct((facets, vis_rows + pos_rows + halo_rows, 2 * S), BF),
+        out_shape=[jax.ShapeDtypeStruct((vis_rows + pos_rows + halo_rows, 2 * S), BF)] * facets,
         in_specs=[hbm] * 7,
-        out_specs=hbm,
+        out_specs=[hbm] * facets,
         scratch_shapes=[
             pltpu.SMEM((subs, blocks), jnp.int32),
             pltpu.SMEM((subs, blocks), jnp.int32),
@@ -227,7 +236,7 @@
             pltpu.VMEM((2, facets, subs * pairs, S, S), BF),
             pltpu.VMEM((facets, vis_rows + pos_rows, 2 * S), BF),
             pltpu.VMEM((facets, halo_rows, 2 * S), BF),
-            pltpu.SemaphoreType.DMA((CHUNKS + 10,)),
+            pltpu.SemaphoreType.DMA((CHUNKS + 8 + 2 * facets,)),
         ],
         compiler_params=params(60),
         name="pack_blocks",
@@ -235,7 +244,7 @@
 
 
 def grid_and_step(received, image, dual, steps, pairs, bands):
-    facets = received.shape[0]
+    facets = len(received)
     subs, rows, width = image.shape
     vis_rows = subs * pairs * S
     per = 4
@@ -245,10 +254,13 @@
     pos_rows = -(-2 * subs * pairs // 16) * 16
     height = 2 * HALO * subs
 
-    def kernel(step_ref, rec_ref, img_ref, dual_ref, shift_ref, *rest):
+    def kernel(step_ref, img_ref, dual_ref, *rest):
+        rec_refs, rest = rest[:facets], rest[facets:]
+        shift_ref, rest = rest[0], rest[1:]
         piece_refs = rest[:bands]
         place_ref, acc_ref, den_ref, halo_ref = rest[bands:]
-        place_ref[...] = rec_ref[:, vis_rows : vis_rows + pos_rows, :].astype(F32)
+        for source in range(facets):
+            place_ref[source] = rec_refs[source][vis_rows : vis_rows + pos_rows, :].astype(F32)
         one = jnp.ones((), BF)
         none = jnp.zeros((), BF)
         lane = lax.broadcasted_iota(jnp.int32, (1, 2 * S), 1)
@@ -266,7 +278,7 @@
                 for q in range(per):
                     source = it * sources + q // pairs
                     at = sub * pairs + q % pairs
-                    block = rec_ref[source, at * S : (at + 1) * S, :]
+                    block = rec_refs[source][at * S : (at + 1) * S, :]
                     diag = jnp.concatenate([block * left, block * right], axis=0)
                     u_row = place_ref[source, at : at + 1, :].astype(BF)
                     v_row = place_ref[source, at + subs * pairs : at + subs * pairs + 1, :].astype(BF)
@@ -311,7 +323,7 @@
             shifted = stepped + dual_ref[sub]
             shift_ref[sub] = shifted
             den_ref[sub, HALO : HALO + rows, :] = shifted
-        halo = jnp.sum(rec_ref[:, vis_rows + pos_rows :, :].astype(F32), axis=0)
+        halo = sum(ref[vis_rows + pos_rows :, :].astype(F32) for ref in rec_refs)
         parts = [halo[n * height : (n + 1) * height] for n in range(rows // 128)]
         halo = jnp.concatenate(parts + [jnp.zeros((height, 128), F32)], axis=1)
         steps_in = 128 // band_rows
@@ -334,7 +346,7 @@
         kernel,
         out_shape=[jax.ShapeDtypeStruct(image.shape, F32)]
         + [jax.ShapeDtypeStruct((subs * piece + height, width), BF)] * bands,
-        in_specs=[smem()] + [vmem()] * 3,
+        in_specs=[smem()] + [vmem()] * (2 + facets),
         out_specs=[vmem()] * (1 + bands),
         scratch_shapes=[
             pltpu.VMEM((facets, pos_rows, 2 * S), F32),
@@ -344,7 +356,7 @@
         ],
         compiler_params=params(),
         name="grid_and_step",
-    )(steps, received, image, dual)
+    )(steps, image, dual, *received)
 
 
 def weight_matrices(conv_first, conv_middle, conv_last):
@@ -603,7 +615,10 @@
         facets,
         pairs,
     )
-    received = lax.all_to_all(packed, "facet", split_axis=0, concat_axis=0, tiled=True)
+    received = [packed[0]] + [
+        lax.ppermute(packed[k], "facet", [(i, i ^ k) for i in range(facets)])
+        for k in range(1, facets)
+    ]
     weights = weight_matrices(conv_first, conv_middle, conv_last)
     shifted, *pieces = grid_and_step(received, image_cube, dual_cube, step_sizes, pairs, bands)
     pieces = exchange(pieces, bands)

time: 66.5 us -> 64.9 us (0.976)
  blocking collectives: 21.7 us -> 0 us
  starting transfers between devices: 11.1 us -> 20.7 us
  waiting for transfers between devices: 11.3 us -> 20.2 us
  local copies, waits for them, and re-layouts: 0.3 us -> 1.76 us
    all_to_all x1 -> x0, blocking collectives: 21.7 us -> none  [body(): lax.all_to_all(packed, 'facet', split_axis=0, concat_axis=0, tiled=True)]
    ppermute x0 -> x7, starting transfers between devices: none -> 9.26 us  [body(): lax.ppermute(packed[k], 'facet', [(i, i ^ k) for i in range(facets)])]
    ppermute x0 -> x7, waiting for transfers between devices: none -> 8.71 us  [body(): lax.ppermute(packed[k], 'facet', [(i, i ^ k) for i in range(facets)])]
    unnamed x15 -> x17, local copies, waits for them, and re-layouts: 0.2 us -> 1.65 us
  transfers between devices with their start and end apart: 6 -> 13, of which waited for: 5 -> 8; matrix products, arithmetic and copies ran while one was open for 0% -> 0% of each run, Pallas kernels for 1% -> 1%
where the time goes in v5:
time: 64.9 us; the launch traced here: 64.7 us
  Pallas kernels  21.4 us (33%)
  starting transfers between devices  20.7 us (32%)
  waiting for transfers between devices  20.2 us (31%)
  local copies, waits for them, and re-layouts  1.76 us (3%)
  between operations  0.73 us (1%)
    ppermute x6, starting transfers between devices, exchange(): lax.ppermute(parts[k], 'band', [(i, (i + k) % bands) for i in range(bands)])  11.5 us
    ppermute x6, waiting for transfers between devices, exchange(): lax.ppermute(parts[k], 'band', [(i, (i + k) % bands) for i in range(bands)])  11.5 us
    ppermute x7, starting transfers between devices, body(): lax.ppermute(packed[k], 'facet', [(i, i ^ k) for i in range(facets)])  9.26 us
    pallas_call x1, Pallas kernels, denoise(): pl.pallas_call(kernel, out_shape=[jax.ShapeDtypeStruct((subs * band_rows,...  8.87 us
    ppermute x7, waiting for transfers between devices, body(): lax.ppermute(packed[k], 'facet', [(i, i ^ k) for i in range(facets)])  8.71 us
    pallas_call x1, Pallas kernels, pack_blocks(): pl.pallas_call(kernel, out_shape=[jax.ShapeDtypeStruct((vis_rows + pos_ro...  5.7 us
    pallas_call x1, Pallas kernels, grid_and_step(): pl.pallas_call(kernel, out_shape=[jax.ShapeDtypeStruct(image.shape, F32)]...  4.7 us
    unnamed x17, local copies, waits for them, and re-layouts  1.65 us
  transfers between devices with their start and end apart: 13, of which 8 were waited for; matrix products, arithmetic and copies ran while one was open for 0% of the time, Pallas kernels for 1%

profile of v5, /device:TPU:0, one launch (start us, length us, event | category | flops | bytes accessed | tf_op | source)
XLA Modules:
  0.0 64.7 jit_solution(13935401964727550342)
XLA Ops:
  0.6 0.0 copy-start
  0.6 0.0 copy-start.1
  0.7 5.7 %pack_blocks.1 = (bf16[560,128]{1,0:T(8,128)(2,1)}, bf16[560,128]{1,0:T(8,128)(2,1)}, bf16[560,128]{1,0:T(8,128)(2,1)}, bf16[560,128]{1,0:T(8,128)(2,1)}, bf16[5...) custom-call(s32[2,32]{1,0:T(2,128)} %bitcast.11, ...), custom_call_target="tpu_custom_call" | custom-call | tf_op jit(solution)/shard_map/pack_blocks/pallas_call | solution.py:222
  6.4 0.5 collective-permute-start
  6.9 2.6 %collective-permute-start.1 = (bf16[560,128]{1,0:T(8,128)(2,1)}, bf16[560,128]{1,0:T(8,128)(2,1)S(1)}, u32[]{:S(2)}, u32[]{:S(2)}) collective-permute-start(bf16[560,128]{1,0:T(8,128)(2,1)} %get-tuple-element.24), channel_id=1, source_target_pairs={{0,8},{4,12},{8,0},{12,4},{16,24},{20,28},{24,16},{28,20},{1,9},{5... | collective-permute-start | bytes 430088 | tf_op jit(solution)/shard_map/ppermute | solution.py:619
  9.4 0.1 collective-permute-start.2
  9.5 1.8 %collective-permute-start.3 = (bf16[560,128]{1,0:T(8,128)(2,1)}, bf16[560,128]{1,0:T(8,128)(2,1)S(1)}, u32[]{:S(2)}, u32[]{:S(2)}) collective-permute-start(bf16[560,128]{1,0:T(8,128)(2,1)} %get-tuple-element.26), channel_id=1, source_target_pairs={{0,16},{4,20},{8,24},{12,28},{16,0},{20,4},{24,8},{28,12},{1,17},{... | collective-permute-start | bytes 430088 | tf_op jit(solution)/shard_map/ppermute | solution.py:619
  11.3 0.0 collective-permute-start.4
  11.3 0.0 collective-permute-done.rest_1_
  11.3 2.6 %collective-permute-start.5 = (bf16[560,128]{1,0:T(8,128)(2,1)}, bf16[560,128]{1,0:T(8,128)(2,1)S(1)}, u32[]{:S(2)}, u32[]{:S(2)}) collective-permute-start(bf16[560,128]{1,0:T(8,128)(2,1)} %get-tuple-element.28), channel_id=1, source_target_pairs={{0,24},{4,28},{8,16},{12,20},{16,8},{20,12},{24,0},{28,4},{1,25},{... | collective-permute-start | bytes 430088 | tf_op jit(solution)/shard_map/ppermute | solution.py:619
  13.9 0.4 collective-permute-done.1.rest_2_
  14.3 0.0 copy-start.3
  14.3 1.7 %collective-permute-start.6 = (bf16[560,128]{1,0:T(8,128)(2,1)}, bf16[560,128]{1,0:T(8,128)(2,1)S(1)}, u32[]{:S(2)}, u32[]{:S(2)}) collective-permute-start(bf16[560,128]{1,0:T(8,128)(2,1)} %get-tuple-element.29), channel_id=1, source_target_pairs={{0,28},{4,24},{8,20},{12,16},{16,12},{20,8},{24,4},{28,0},{1,29},{... | collective-permute-start | bytes 430088 | tf_op jit(solution)/shard_map/ppermute | solution.py:619
  16.0 0.9 %collective-permute-done.2.rest_3_ = bf16[560,128]{1,0:T(8,128)(2,1)S(1)} collective-permute-done((bf16[560,128]{1,0:T(8,128)(2,1)}, bf16[560,128]{1,0:T(8,128)(2,1)S(1)}, u32[]{:S(2)}, u32[]{:S(2)}) %collective-permute-start.2) | collective-permute-done | bytes 143392 | tf_op jit(solution)/shard_map/ppermute | solution.py:619
  16.9 0.0 collective-permute-done.3.rest_4_
  16.9 7.4 %collective-permute-done.4.rest_5_ = bf16[560,128]{1,0:T(8,128)(2,1)S(1)} collective-permute-done((bf16[560,128]{1,0:T(8,128)(2,1)}, bf16[560,128]{1,0:T(8,128)(2,1)S(1)}, u32[]{:S(2)}, u32[]{:S(2)}) %collective-permute-start.4) | collective-permute-done | bytes 143392 | tf_op jit(solution)/shard_map/ppermute | solution.py:619
  24.3 0.0 collective-permute-done.5.rest_6_
  24.3 0.0 collective-permute-done.6.rest_7_
  24.3 0.0 copy-done
  24.3 0.0 copy-done.1
  24.4 0.0 copy-done.3
  24.4 0.0 copy-start.2
  24.4 0.9 %copy-done.2 = bf16[560,128]{1,0:T(8,128)(2,1)S(1)} copy-done((bf16[560,128]{1,0:T(8,128)(2,1)S(1)}, bf16[560,128]{1,0:T(8,128)(2,1)}, u32[]{:S(2)}) %copy-start.2) | copy-done | bytes 143384
  25.3 0.0 copy-start.5
  25.3 0.0 copy-start.4
  25.3 4.7 %grid_and_step.1 = (f32[2,256,384]{2,1,0:T(8,128)S(1)}, bf16[160,384]{1,0:T(8,128)(2,1)S(1)}, bf16[160,384]{1,0:T(8,128)(2,1)S(1)}, bf16[160,384]{1,0:T(8,128)(2,1)S(1)}, bf16[160,384]{1,0:T(8,128)(2,1)S(1)}) custom-call(f32[2]{0:T(128)S(1)} %copy-done.3, f32[2,256,384]{2,1,0:T(8,128)S(1)} %copy-done, f32[2,256,384]{2,1,0:T(8,128)S(1)} %copy-done.1, ...), custom_call_target="tpu_custom_call" | custom-call | tf_op jit(solution)/shard_map/grid_and_step/pallas_call | solution.py:345
  30.0 1.9 %collective-permute-start.7 = (bf16[160,384]{1,0:T(8,128)(2,1)S(1)}, bf16[160,384]{1,0:T(8,128)(2,1)S(1)}, u32[]{:S(2)}, u32[]{:S(2)}) collective-permute-start(bf16[160,384]{1,0:T(8,128)(2,1)S(1)} %get-tuple-element.35), channel_id=1, source_target_pairs={{0,1},{1,2},{2,3},{3,0},{4,5},{5,6},{6,7},{7,4},{8,9},{9,10},{10,1... | collective-permute-start | bytes 368648 | tf_op jit(solution)/shard_map/ppermute | solution.py:585
  31.9 2.6 %collective-permute-start.8 = (bf16[160,384]{1,0:T(8,128)(2,1)S(1)}, bf16[160,384]{1,0:T(8,128)(2,1)S(1)}, u32[]{:S(2)}, u32[]{:S(2)}) collective-permute-start(bf16[160,384]{1,0:T(8,128)(2,1)S(1)} %get-tuple-element.36), channel_id=1, source_target_pairs={{0,2},{1,3},{2,0},{3,1},{4,6},{5,7},{6,4},{7,5},{8,10},{9,11},{10,... | collective-permute-start | bytes 368648 | tf_op jit(solution)/shard_map/ppermute | solution.py:585
  34.5 1.3 %collective-permute-start.9 = (bf16[160,384]{1,0:T(8,128)(2,1)S(1)}, bf16[160,384]{1,0:T(8,128)(2,1)S(1)}, u32[]{:S(2)}, u32[]{:S(2)}) collective-permute-start(bf16[160,384]{1,0:T(8,128)(2,1)S(1)} %get-tuple-element.37), channel_id=1, source_target_pairs={{0,3},{1,0},{2,1},{3,2},{4,7},{5,4},{6,5},{7,6},{8,11},{9,8},{10,9... | collective-permute-start | bytes 368648 | tf_op jit(solution)/shard_map/ppermute | solution.py:585
  35.8 0.0 copy-done.5
  35.8 0.0 copy-done.4
  35.8 0.0 copy-start.6
  35.9 0.1 copy.16
  36.0 0.6 copy-done.6
  36.6 0.1 copy.18.last_ref
  36.7 0.8 %weight_matrices.1 = (bf16[240,512]{1,0:T(8,128)(2,1)S(1)}, bf16[1152,256]{1,0:T(8,128)(2,1)S(1)}, bf16[768,256]{1,0:T(8,128)(2,1)S(1)}) custom-call(bf16[3,3,8,64]{3,2,1,0:T(8,128)(2,1)S(1)} %bitcast.10, bf16[3,3,64,64]{3,2,1,0:T(8,128)(2,1)S(1)} %bitcast.9, bf16[3,64,24]{2,1,0:T(8,128)(2,1)S(1)} %copy.18.last_ref), custom_call_target="tpu_custom_call" | custom-call | flops 1048576 | bytes 1048576 | tf_op jit(solution)/shard_map/weight_matrices/pallas_call | solution.py:408
  37.5 0.7 %collective-permute-done.7.rest_1_ = bf16[160,384]{1,0:T(8,128)(2,1)S(1)} collective-permute-done((bf16[160,384]{1,0:T(8,128)(2,1)S(1)}, bf16[160,384]{1,0:T(8,128)(2,1)S(1)}, u32[]{:S(2)}, u32[]{:S(2)}) %collective-permute-start.7) | collective-permute-done | bytes 122912 | tf_op jit(solution)/shard_map/ppermute | solution.py:585
  38.2 4.9 %collective-permute-done.8.rest_2_ = bf16[160,384]{1,0:T(8,128)(2,1)S(1)} collective-permute-done((bf16[160,384]{1,0:T(8,128)(2,1)S(1)}, bf16[160,384]{1,0:T(8,128)(2,1)S(1)}, u32[]{:S(2)}, u32[]{:S(2)}) %collective-permute-start.8) | collective-permute-done | bytes 122912 | tf_op jit(solution)/shard_map/ppermute | solution.py:585
  43.1 0.0 collective-permute-done.9.rest_3_
  43.1 8.9 %denoise.1 = (bf16[128,384]{1,0:T(8,128)(2,1)S(1)}, bf16[128,384]{1,0:T(8,128)(2,1)S(1)}, bf16[128,384]{1,0:T(8,128)(2,1)S(1)}, bf16[128,384]{1,0:T(8,128)(2,1)S(1)}) custom-call(bf16[240,512]{1,0:T(8,128)(2,1)S(1)} %get-tuple-element.31.first_ref, bf16[1152,256]{1,0:T(8,128)(2,1)S(1)} %get-tuple-element.32.mid_ref, ...), custom_call_target="tpu_custom_call" | custom-call | tf_op jit(solution)/shard_map/denoise/pallas_call | solution.py:540
  52.0 3.2 %collective-permute-start.10 = (bf16[128,384]{1,0:T(8,128)(2,1)S(1)}, bf16[128,384]{1,0:T(8,128)(2,1)S(1)}, u32[]{:S(2)}, u32[]{:S(2)}) collective-permute-start(bf16[128,384]{1,0:T(8,128)(2,1)S(1)} %get-tuple-element.39), channel_id=1, source_target_pairs={{0,1},{1,2},{2,3},{3,0},{4,5},{5,6},{6,7},{7,4},{8,9},{9,10},{10,1... | collective-permute-start | bytes 294920 | tf_op jit(solution)/shard_map/ppermute | solution.py:585
  55.2 1.6 %collective-permute-start.11 = (bf16[128,384]{1,0:T(8,128)(2,1)S(1)}, bf16[128,384]{1,0:T(8,128)(2,1)S(1)}, u32[]{:S(2)}, u32[]{:S(2)}) collective-permute-start(bf16[128,384]{1,0:T(8,128)(2,1)S(1)} %get-tuple-element.40), channel_id=1, source_target_pairs={{0,2},{1,3},{2,0},{3,1},{4,6},{5,7},{6,4},{7,5},{8,10},{9,11},{10,... | collective-permute-start | bytes 294920 | tf_op jit(solution)/shard_map/ppermute | solution.py:585
  56.8 0.8 %collective-permute-start.12 = (bf16[128,384]{1,0:T(8,128)(2,1)S(1)}, bf16[128,384]{1,0:T(8,128)(2,1)S(1)}, u32[]{:S(2)}, u32[]{:S(2)}) collective-permute-start(bf16[128,384]{1,0:T(8,128)(2,1)S(1)} %get-tuple-element.41), channel_id=1, source_target_pairs={{0,3},{1,0},{2,1},{3,2},{4,7},{5,4},{6,5},{7,6},{8,11},{9,8},{10,9... | collective-permute-start | bytes 294920 | tf_op jit(solution)/shard_map/ppermute | solution.py:585
  57.6 2.1 %collective-permute-done.10.rest_1_ = bf16[128,384]{1,0:T(8,128)(2,1)S(1)} collective-permute-done((bf16[128,384]{1,0:T(8,128)(2,1)S(1)}, bf16[128,384]{1,0:T(8,128)(2,1)S(1)}, u32[]{:S(2)}, u32[]{:S(2)}) %collective-permute-start.10) | collective-permute-done | bytes 98336 | tf_op jit(solution)/shard_map/ppermute | solution.py:585
  59.7 3.5 %collective-permute-done.11.rest_2_ = bf16[128,384]{1,0:T(8,128)(2,1)S(1)} collective-permute-done((bf16[128,384]{1,0:T(8,128)(2,1)S(1)}, bf16[128,384]{1,0:T(8,128)(2,1)S(1)}, u32[]{:S(2)}, u32[]{:S(2)}) %collective-permute-start.11) | collective-permute-done | bytes 98336 | tf_op jit(solution)/shard_map/ppermute | solution.py:585
  63.2 0.2 collective-permute-done.12.rest_3_
  63.5 1.3 %finish.1 = (f32[2,256,384]{2,1,0:T(8,128)}, f32[2,256,384]{2,1,0:T(8,128)}) custom-call(f32[2,256,384]{2,1,0:T(8,128)S(1)} %get-tuple-element.30.shift_ref, bf16[128,384]{1,0:T(8,128)(2,1)S(1)} %get-tuple-element.38.rest_0_, bf16[128,384]{1,0:T(8,128)(2,1)S(1)} %collective-permute-done.10.rest_1_, bf16[128,384]{1,0:T(8,128)(2,1)S(1)} %collective-permute-done.11.rest_2_, ...), custom_call_target="tpu_custom_call" | custom-call | tf_op jit(solution)/shard_map/finish/pallas_call | solution.py:573
  (3 shorter events, 0.0 us)
Async XLA Ops:
  0.6 23.7 %copy-start = (f32[2,256,384]{2,1,0:T(8,128)S(1)}, f32[2,256,384]{2,1,0:T(8,128)}, u32[]{:S(2)}) copy-start(f32[2,256,384]{2,1,0:T(8,128)} %img_ref.1) | copy-start | bytes 2359300
  0.6 23.7 %copy-start.1 = (f32[2,256,384]{2,1,0:T(8,128)S(1)}, f32[2,256,384]{2,1,0:T(8,128)}, u32[]{:S(2)}) copy-start(f32[2,256,384]{2,1,0:T(8,128)} %dual_ref.1) | copy-start | bytes 2359300
  6.4 4.9 %collective-permute-start = (bf16[560,128]{1,0:T(8,128)(2,1)}, bf16[560,128]{1,0:T(8,128)(2,1)S(1)}, u32[]{:S(2)}, u32[]{:S(2)}) collective-permute-start(bf16[560,128]{1,0:T(8,128)(2,1)} %get-tuple-element.23), channel_id=1, source_target_pairs={{0,4},{4,0},{8,12},{12,8},{16,20},{20,16},{24,28},{28,24},{1,5},{5... | collective-permute-start | bytes 430088 | tf_op jit(solution)/shard_map/ppermute | solution.py:619
  6.9 7.4 %collective-permute-start.1 = (bf16[560,128]{1,0:T(8,128)(2,1)}, bf16[560,128]{1,0:T(8,128)(2,1)S(1)}, u32[]{:S(2)}, u32[]{:S(2)}) collective-permute-start(bf16[560,128]{1,0:T(8,128)(2,1)} %get-tuple-element.24), channel_id=1, source_target_pairs={{0,8},{4,12},{8,0},{12,4},{16,24},{20,28},{24,16},{28,20},{1,9},{5... | collective-permute-start | bytes 430088 | tf_op jit(solution)/shard_map/ppermute | solution.py:619
  9.4 7.5 %collective-permute-start.2 = (bf16[560,128]{1,0:T(8,128)(2,1)}, bf16[560,128]{1,0:T(8,128)(2,1)S(1)}, u32[]{:S(2)}, u32[]{:S(2)}) collective-permute-start(bf16[560,128]{1,0:T(8,128)(2,1)} %get-tuple-element.25), channel_id=1, source_target_pairs={{0,12},{4,8},{8,4},{12,0},{16,28},{20,24},{24,20},{28,16},{1,13},{... | collective-permute-start | bytes 430088 | tf_op jit(solution)/shard_map/ppermute | solution.py:619
  9.5 7.4 %collective-permute-start.3 = (bf16[560,128]{1,0:T(8,128)(2,1)}, bf16[560,128]{1,0:T(8,128)(2,1)S(1)}, u32[]{:S(2)}, u32[]{:S(2)}) collective-permute-start(bf16[560,128]{1,0:T(8,128)(2,1)} %get-tuple-element.26), channel_id=1, source_target_pairs={{0,16},{4,20},{8,24},{12,28},{16,0},{20,4},{24,8},{28,12},{1,17},{... | collective-permute-start | bytes 430088 | tf_op jit(solution)/shard_map/ppermute | solution.py:619
  11.3 13.0 %collective-permute-start.4 = (bf16[560,128]{1,0:T(8,128)(2,1)}, bf16[560,128]{1,0:T(8,128)(2,1)S(1)}, u32[]{:S(2)}, u32[]{:S(2)}) collective-permute-start(bf16[560,128]{1,0:T(8,128)(2,1)} %get-tuple-element.27), channel_id=1, source_target_pairs={{0,20},{4,16},{8,28},{12,24},{16,4},{20,0},{24,12},{28,8},{1,21},{... | collective-permute-start | bytes 430088 | tf_op jit(solution)/shard_map/ppermute | solution.py:619
  11.3 13.0 %collective-permute-start.5 = (bf16[560,128]{1,0:T(8,128)(2,1)}, bf16[560,128]{1,0:T(8,128)(2,1)S(1)}, u32[]{:S(2)}, u32[]{:S(2)}) collective-permute-start(bf16[560,128]{1,0:T(8,128)(2,1)} %get-tuple-element.28), channel_id=1, source_target_pairs={{0,24},{4,28},{8,16},{12,20},{16,8},{20,12},{24,0},{28,4},{1,25},{... | collective-permute-start | bytes 430088 | tf_op jit(solution)/shard_map/ppermute | solution.py:619
  14.3 10.1 %copy-start.3 = (f32[2]{0:T(128)S(1)}, f32[2]{0:T(128)}, u32[]{:S(2)}) copy-start(f32[2]{0:T(128)} %step_ref.1) | copy-start | bytes 28
  14.3 10.1 %collective-permute-start.6 = (bf16[560,128]{1,0:T(8,128)(2,1)}, bf16[560,128]{1,0:T(8,128)(2,1)S(1)}, u32[]{:S(2)}, u32[]{:S(2)}) collective-permute-start(bf16[560,128]{1,0:T(8,128)(2,1)} %get-tuple-element.29), channel_id=1, source_target_pairs={{0,28},{4,24},{8,20},{12,16},{16,12},{20,8},{24,4},{28,0},{1,29},{... | collective-permute-start | bytes 430088 | tf_op jit(solution)/shard_map/ppermute | solution.py:619
  24.4 0.9 %copy-start.2 = (bf16[560,128]{1,0:T(8,128)(2,1)S(1)}, bf16[560,128]{1,0:T(8,128)(2,1)}, u32[]{:S(2)}) copy-start(bf16[560,128]{1,0:T(8,128)(2,1)} %get-tuple-element.22.rest_0_) | copy-start | bytes 430084
  25.3 10.6 %copy-start.5 = (bf16[64,8,3,3]{0,1,3,2:T(8,128)(2,1)S(1)}, bf16[64,8,3,3]{0,1,3,2:T(8,128)(2,1)}, u32[]{:S(2)}) copy-start(bf16[64,8,3,3]{0,1,3,2:T(8,128)(2,1)} %param.17) | copy-start | bytes 27652
  25.3 10.6 %copy-start.4 = (bf16[64,64,3,3]{1,0,3,2:T(8,128)(2,1)S(1)}, bf16[64,64,3,3]{1,0,3,2:T(8,128)(2,1)}, u32[]{:S(2)}) copy-start(bf16[64,64,3,3]{1,0,3,2:T(8,128)(2,1)} %param.18) | copy-start | bytes 221188
  30.0 8.2 %collective-permute-start.7 = (bf16[160,384]{1,0:T(8,128)(2,1)S(1)}, bf16[160,384]{1,0:T(8,128)(2,1)S(1)}, u32[]{:S(2)}, u32[]{:S(2)}) collective-permute-start(bf16[160,384]{1,0:T(8,128)(2,1)S(1)} %get-tuple-element.35), channel_id=1, source_target_pairs={{0,1},{1,2},{2,3},{3,0},{4,5},{5,6},{6,7},{7,4},{8,9},{9,10},{10,1... | collective-permute-start | bytes 368648 | tf_op jit(solution)/shard_map/ppermute | solution.py:585
  31.9 11.2 %collective-permute-start.8 = (bf16[160,384]{1,0:T(8,128)(2,1)S(1)}, bf16[160,384]{1,0:T(8,128)(2,1)S(1)}, u32[]{:S(2)}, u32[]{:S(2)}) collective-permute-start(bf16[160,384]{1,0:T(8,128)(2,1)S(1)} %get-tuple-element.36), channel_id=1, source_target_pairs={{0,2},{1,3},{2,0},{3,1},{4,6},{5,7},{6,4},{7,5},{8,10},{9,11},{10,... | collective-permute-start | bytes 368648 | tf_op jit(solution)/shard_map/ppermute | solution.py:585
  34.5 8.7 %collective-permute-start.9 = (bf16[160,384]{1,0:T(8,128)(2,1)S(1)}, bf16[160,384]{1,0:T(8,128)(2,1)S(1)}, u32[]{:S(2)}, u32[]{:S(2)}) collective-permute-start(bf16[160,384]{1,0:T(8,128)(2,1)S(1)} %get-tuple-element.37), channel_id=1, source_target_pairs={{0,3},{1,0},{2,1},{3,2},{4,7},{5,4},{6,5},{7,6},{8,11},{9,8},{10,9... | collective-permute-start | bytes 368648 | tf_op jit(solution)/shard_map/ppermute | solution.py:585
  35.8 0.7 %copy-start.6 = (bf16[8,64,3,3]{1,0,3,2:T(8,128)(2,1)S(1)}, bf16[8,64,3,3]{1,0,3,2:T(8,128)(2,1)}, u32[]{:S(2)}) copy-start(bf16[8,64,3,3]{1,0,3,2:T(8,128)(2,1)} %param.19) | copy-start | bytes 27652
  52.0 7.7 %collective-permute-start.10 = (bf16[128,384]{1,0:T(8,128)(2,1)S(1)}, bf16[128,384]{1,0:T(8,128)(2,1)S(1)}, u32[]{:S(2)}, u32[]{:S(2)}) collective-permute-start(bf16[128,384]{1,0:T(8,128)(2,1)S(1)} %get-tuple-element.39), channel_id=1, source_target_pairs={{0,1},{1,2},{2,3},{3,0},{4,5},{5,6},{6,7},{7,4},{8,9},{9,10},{10,1... | collective-permute-start | bytes 294920 | tf_op jit(solution)/shard_map/ppermute | solution.py:585
  55.2 8.0 %collective-permute-start.11 = (bf16[128,384]{1,0:T(8,128)(2,1)S(1)}, bf16[128,384]{1,0:T(8,128)(2,1)S(1)}, u32[]{:S(2)}, u32[]{:S(2)}) collective-permute-start(bf16[128,384]{1,0:T(8,128)(2,1)S(1)} %get-tuple-element.40), channel_id=1, source_target_pairs={{0,2},{1,3},{2,0},{3,1},{4,6},{5,7},{6,4},{7,5},{8,10},{9,11},{10,... | collective-permute-start | bytes 294920 | tf_op jit(solution)/shard_map/ppermute | solution.py:585
  56.8 6.6 %collective-permute-start.12 = (bf16[128,384]{1,0:T(8,128)(2,1)S(1)}, bf16[128,384]{1,0:T(8,128)(2,1)S(1)}, u32[]{:S(2)}, u32[]{:S(2)}) collective-permute-start(bf16[128,384]{1,0:T(8,128)(2,1)S(1)} %get-tuple-element.41), channel_id=1, source_target_pairs={{0,3},{1,0},{2,1},{3,2},{4,7},{5,4},{6,5},{7,6},{8,11},{9,8},{10,9... | collective-permute-start | bytes 294920 | tf_op jit(solution)/shard_map/ppermute | solution.py:585

commit v6 on v5

--- a/solution.py
+++ b/solution.py
@@ -315,9 +315,7 @@
         me = lax.axis_index("band")
         for sub in range(subs):
             total = acc_ref[sub]
-            high = total.astype(BF)
-            low = (total - high.astype(F32)).astype(BF)
-            half = dot(u_taps, high) + dot(u_taps, low)
+            half = dot(u_taps, total.astype(BF))
             gradient = dot(half.astype(BF), v_taps)
             stepped = img_ref[sub] - step_ref[sub] * gradient
             shifted = stepped + dual_ref[sub]

time: 64.9 us -> 64.8 us (level)
  no operation moved by 1% of the time
where the time goes in v6:
time: 64.8 us; the launch traced here: 64.6 us
  Pallas kernels  21.2 us (33%)
  starting transfers between devices  20.7 us (32%)
  waiting for transfers between devices  20.2 us (31%)
  local copies, waits for them, and re-layouts  1.76 us (3%)
  between operations  0.73 us (1%)
    ppermute x6, waiting for transfers between devices, exchange(): lax.ppermute(parts[k], 'band', [(i, (i + k) % bands) for i in range(bands)])  11.5 us
    ppermute x6, starting transfers between devices, exchange(): lax.ppermute(parts[k], 'band', [(i, (i + k) % bands) for i in range(bands)])  11.5 us
    ppermute x7, starting transfers between devices, body(): lax.ppermute(packed[k], 'facet', [(i, i ^ k) for i in range(facets)])  9.26 us
    pallas_call x1, Pallas kernels, denoise(): pl.pallas_call(kernel, out_shape=[jax.ShapeDtypeStruct((subs * band_rows,...  8.87 us
    ppermute x7, waiting for transfers between devices, body(): lax.ppermute(packed[k], 'facet', [(i, i ^ k) for i in range(facets)])  8.71 us
    pallas_call x1, Pallas kernels, pack_blocks(): pl.pallas_call(kernel, out_shape=[jax.ShapeDtypeStruct((vis_rows + pos_ro...  5.7 us
    pallas_call x1, Pallas kernels, grid_and_step(): pl.pallas_call(kernel, out_shape=[jax.ShapeDtypeStruct(image.shape, F32)]...  4.56 us
    unnamed x17, local copies, waits for them, and re-layouts  1.65 us
  transfers between devices with their start and end apart: 13, of which 8 were waited for; matrix products, arithmetic and copies ran while one was open for 0% of the time, Pallas kernels for 1%

profile of v6, /device:TPU:0, one launch (start us, length us, event | category | flops | bytes accessed | tf_op | source)
XLA Modules:
  0.0 64.6 jit_solution(7249395250244071560)
XLA Ops:
  0.6 0.0 copy-start
  0.6 0.0 copy-start.1
  0.7 5.7 %pack_blocks.1 = (bf16[560,128]{1,0:T(8,128)(2,1)}, bf16[560,128]{1,0:T(8,128)(2,1)}, bf16[560,128]{1,0:T(8,128)(2,1)}, bf16[560,128]{1,0:T(8,128)(2,1)}, bf16[5...) custom-call(s32[2,32]{1,0:T(2,128)} %bitcast.11, ...), custom_call_target="tpu_custom_call" | custom-call | tf_op jit(solution)/shard_map/pack_blocks/pallas_call | solution.py:222
  6.4 0.5 collective-permute-start
  6.9 2.6 %collective-permute-start.1 = (bf16[560,128]{1,0:T(8,128)(2,1)}, bf16[560,128]{1,0:T(8,128)(2,1)S(1)}, u32[]{:S(2)}, u32[]{:S(2)}) collective-permute-start(bf16[560,128]{1,0:T(8,128)(2,1)} %get-tuple-element.24), channel_id=1, source_target_pairs={{0,8},{4,12},{8,0},{12,4},{16,24},{20,28},{24,16},{28,20},{1,9},{5... | collective-permute-start | bytes 430088 | tf_op jit(solution)/shard_map/ppermute | solution.py:617
  9.4 0.1 collective-permute-start.2
  9.5 1.8 %collective-permute-start.3 = (bf16[560,128]{1,0:T(8,128)(2,1)}, bf16[560,128]{1,0:T(8,128)(2,1)S(1)}, u32[]{:S(2)}, u32[]{:S(2)}) collective-permute-start(bf16[560,128]{1,0:T(8,128)(2,1)} %get-tuple-element.26), channel_id=1, source_target_pairs={{0,16},{4,20},{8,24},{12,28},{16,0},{20,4},{24,8},{28,12},{1,17},{... | collective-permute-start | bytes 430088 | tf_op jit(solution)/shard_map/ppermute | solution.py:617
  11.3 0.0 collective-permute-start.4
  11.3 0.0 collective-permute-done.rest_1_
  11.3 2.6 %collective-permute-start.5 = (bf16[560,128]{1,0:T(8,128)(2,1)}, bf16[560,128]{1,0:T(8,128)(2,1)S(1)}, u32[]{:S(2)}, u32[]{:S(2)}) collective-permute-start(bf16[560,128]{1,0:T(8,128)(2,1)} %get-tuple-element.28), channel_id=1, source_target_pairs={{0,24},{4,28},{8,16},{12,20},{16,8},{20,12},{24,0},{28,4},{1,25},{... | collective-permute-start | bytes 430088 | tf_op jit(solution)/shard_map/ppermute | solution.py:617
  13.9 0.4 collective-permute-done.1.rest_2_
  14.3 0.0 copy-start.3
  14.3 1.7 %collective-permute-start.6 = (bf16[560,128]{1,0:T(8,128)(2,1)}, bf16[560,128]{1,0:T(8,128)(2,1)S(1)}, u32[]{:S(2)}, u32[]{:S(2)}) collective-permute-start(bf16[560,128]{1,0:T(8,128)(2,1)} %get-tuple-element.29), channel_id=1, source_target_pairs={{0,28},{4,24},{8,20},{12,16},{16,12},{20,8},{24,4},{28,0},{1,29},{... | collective-permute-start | bytes 430088 | tf_op jit(solution)/shard_map/ppermute | solution.py:617
  16.0 0.9 %collective-permute-done.2.rest_3_ = bf16[560,128]{1,0:T(8,128)(2,1)S(1)} collective-permute-done((bf16[560,128]{1,0:T(8,128)(2,1)}, bf16[560,128]{1,0:T(8,128)(2,1)S(1)}, u32[]{:S(2)}, u32[]{:S(2)}) %collective-permute-start.2) | collective-permute-done | bytes 143392 | tf_op jit(solution)/shard_map/ppermute | solution.py:617
  16.9 0.0 collective-permute-done.3.rest_4_
  16.9 7.4 %collective-permute-done.4.rest_5_ = bf16[560,128]{1,0:T(8,128)(2,1)S(1)} collective-permute-done((bf16[560,128]{1,0:T(8,128)(2,1)}, bf16[560,128]{1,0:T(8,128)(2,1)S(1)}, u32[]{:S(2)}, u32[]{:S(2)}) %collective-permute-start.4) | collective-permute-done | bytes 143392 | tf_op jit(solution)/shard_map/ppermute | solution.py:617
  24.3 0.0 collective-permute-done.5.rest_6_
  24.3 0.0 collective-permute-done.6.rest_7_
  24.3 0.0 copy-done
  24.3 0.0 copy-done.1
  24.4 0.0 copy-done.3
  24.4 0.0 copy-start.2
  24.4 0.9 %copy-done.2 = bf16[560,128]{1,0:T(8,128)(2,1)S(1)} copy-done((bf16[560,128]{1,0:T(8,128)(2,1)S(1)}, bf16[560,128]{1,0:T(8,128)(2,1)}, u32[]{:S(2)}) %copy-start.2) | copy-done | bytes 143384
  25.3 0.0 copy-start.5
  25.3 0.0 copy-start.4
  25.3 4.6 %grid_and_step.1 = (f32[2,256,384]{2,1,0:T(8,128)S(1)}, bf16[160,384]{1,0:T(8,128)(2,1)S(1)}, bf16[160,384]{1,0:T(8,128)(2,1)S(1)}, bf16[160,384]{1,0:T(8,128)(2,1)S(1)}, bf16[160,384]{1,0:T(8,128)(2,1)S(1)}) custom-call(f32[2]{0:T(128)S(1)} %copy-done.3, f32[2,256,384]{2,1,0:T(8,128)S(1)} %copy-done, f32[2,256,384]{2,1,0:T(8,128)S(1)} %copy-done.1, ...), custom_call_target="tpu_custom_call" | custom-call | tf_op jit(solution)/shard_map/grid_and_step/pallas_call | solution.py:343
  29.8 1.9 %collective-permute-start.7 = (bf16[160,384]{1,0:T(8,128)(2,1)S(1)}, bf16[160,384]{1,0:T(8,128)(2,1)S(1)}, u32[]{:S(2)}, u32[]{:S(2)}) collective-permute-start(bf16[160,384]{1,0:T(8,128)(2,1)S(1)} %get-tuple-element.35), channel_id=1, source_target_pairs={{0,1},{1,2},{2,3},{3,0},{4,5},{5,6},{6,7},{7,4},{8,9},{9,10},{10,1... | collective-permute-start | bytes 368648 | tf_op jit(solution)/shard_map/ppermute | solution.py:583
  31.8 2.6 %collective-permute-start.8 = (bf16[160,384]{1,0:T(8,128)(2,1)S(1)}, bf16[160,384]{1,0:T(8,128)(2,1)S(1)}, u32[]{:S(2)}, u32[]{:S(2)}) collective-permute-start(bf16[160,384]{1,0:T(8,128)(2,1)S(1)} %get-tuple-element.36), channel_id=1, source_target_pairs={{0,2},{1,3},{2,0},{3,1},{4,6},{5,7},{6,4},{7,5},{8,10},{9,11},{10,... | collective-permute-start | bytes 368648 | tf_op jit(solution)/shard_map/ppermute | solution.py:583
  34.3 1.3 %collective-permute-start.9 = (bf16[160,384]{1,0:T(8,128)(2,1)S(1)}, bf16[160,384]{1,0:T(8,128)(2,1)S(1)}, u32[]{:S(2)}, u32[]{:S(2)}) collective-permute-start(bf16[160,384]{1,0:T(8,128)(2,1)S(1)} %get-tuple-element.37), channel_id=1, source_target_pairs={{0,3},{1,0},{2,1},{3,2},{4,7},{5,4},{6,5},{7,6},{8,11},{9,8},{10,9... | collective-permute-start | bytes 368648 | tf_op jit(solution)/shard_map/ppermute | solution.py:583
  35.7 0.0 copy-done.5
  35.7 0.0 copy-done.4
  35.7 0.0 copy-start.6
  35.7 0.1 copy.16
  35.9 0.6 copy-done.6
  36.4 0.1 copy.18.last_ref
  36.5 0.8 %weight_matrices.1 = (bf16[240,512]{1,0:T(8,128)(2,1)S(1)}, bf16[1152,256]{1,0:T(8,128)(2,1)S(1)}, bf16[768,256]{1,0:T(8,128)(2,1)S(1)}) custom-call(bf16[3,3,8,64]{3,2,1,0:T(8,128)(2,1)S(1)} %bitcast.10, bf16[3,3,64,64]{3,2,1,0:T(8,128)(2,1)S(1)} %bitcast.9, bf16[3,64,24]{2,1,0:T(8,128)(2,1)S(1)} %copy.18.last_ref), custom_call_target="tpu_custom_call" | custom-call | flops 1048576 | bytes 1048576 | tf_op jit(solution)/shard_map/weight_matrices/pallas_call | solution.py:406
  37.4 0.7 %collective-permute-done.7.rest_1_ = bf16[160,384]{1,0:T(8,128)(2,1)S(1)} collective-permute-done((bf16[160,384]{1,0:T(8,128)(2,1)S(1)}, bf16[160,384]{1,0:T(8,128)(2,1)S(1)}, u32[]{:S(2)}, u32[]{:S(2)}) %collective-permute-start.7) | collective-permute-done | bytes 122912 | tf_op jit(solution)/shard_map/ppermute | solution.py:583
  38.1 4.9 %collective-permute-done.8.rest_2_ = bf16[160,384]{1,0:T(8,128)(2,1)S(1)} collective-permute-done((bf16[160,384]{1,0:T(8,128)(2,1)S(1)}, bf16[160,384]{1,0:T(8,128)(2,1)S(1)}, u32[]{:S(2)}, u32[]{:S(2)}) %collective-permute-start.8) | collective-permute-done | bytes 122912 | tf_op jit(solution)/shard_map/ppermute | solution.py:583
  43.0 0.0 collective-permute-done.9.rest_3_
  43.0 8.9 %denoise.1 = (bf16[128,384]{1,0:T(8,128)(2,1)S(1)}, bf16[128,384]{1,0:T(8,128)(2,1)S(1)}, bf16[128,384]{1,0:T(8,128)(2,1)S(1)}, bf16[128,384]{1,0:T(8,128)(2,1)S(1)}) custom-call(bf16[240,512]{1,0:T(8,128)(2,1)S(1)} %get-tuple-element.31.first_ref, bf16[1152,256]{1,0:T(8,128)(2,1)S(1)} %get-tuple-element.32.mid_ref, ...), custom_call_target="tpu_custom_call" | custom-call | tf_op jit(solution)/shard_map/denoise/pallas_call | solution.py:538
  51.9 3.2 %collective-permute-start.10 = (bf16[128,384]{1,0:T(8,128)(2,1)S(1)}, bf16[128,384]{1,0:T(8,128)(2,1)S(1)}, u32[]{:S(2)}, u32[]{:S(2)}) collective-permute-start(bf16[128,384]{1,0:T(8,128)(2,1)S(1)} %get-tuple-element.39), channel_id=1, source_target_pairs={{0,1},{1,2},{2,3},{3,0},{4,5},{5,6},{6,7},{7,4},{8,9},{9,10},{10,1... | collective-permute-start | bytes 294920 | tf_op jit(solution)/shard_map/ppermute | solution.py:583
  55.1 1.7 %collective-permute-start.11 = (bf16[128,384]{1,0:T(8,128)(2,1)S(1)}, bf16[128,384]{1,0:T(8,128)(2,1)S(1)}, u32[]{:S(2)}, u32[]{:S(2)}) collective-permute-start(bf16[128,384]{1,0:T(8,128)(2,1)S(1)} %get-tuple-element.40), channel_id=1, source_target_pairs={{0,2},{1,3},{2,0},{3,1},{4,6},{5,7},{6,4},{7,5},{8,10},{9,11},{10,... | collective-permute-start | bytes 294920 | tf_op jit(solution)/shard_map/ppermute | solution.py:583
  56.7 0.8 %collective-permute-start.12 = (bf16[128,384]{1,0:T(8,128)(2,1)S(1)}, bf16[128,384]{1,0:T(8,128)(2,1)S(1)}, u32[]{:S(2)}, u32[]{:S(2)}) collective-permute-start(bf16[128,384]{1,0:T(8,128)(2,1)S(1)} %get-tuple-element.41), channel_id=1, source_target_pairs={{0,3},{1,0},{2,1},{3,2},{4,7},{5,4},{6,5},{7,6},{8,11},{9,8},{10,9... | collective-permute-start | bytes 294920 | tf_op jit(solution)/shard_map/ppermute | solution.py:583
  57.5 2.1 %collective-permute-done.10.rest_1_ = bf16[128,384]{1,0:T(8,128)(2,1)S(1)} collective-permute-done((bf16[128,384]{1,0:T(8,128)(2,1)S(1)}, bf16[128,384]{1,0:T(8,128)(2,1)S(1)}, u32[]{:S(2)}, u32[]{:S(2)}) %collective-permute-start.10) | collective-permute-done | bytes 98336 | tf_op jit(solution)/shard_map/ppermute | solution.py:583
  59.6 3.5 %collective-permute-done.11.rest_2_ = bf16[128,384]{1,0:T(8,128)(2,1)S(1)} collective-permute-done((bf16[128,384]{1,0:T(8,128)(2,1)S(1)}, bf16[128,384]{1,0:T(8,128)(2,1)S(1)}, u32[]{:S(2)}, u32[]{:S(2)}) %collective-permute-start.11) | collective-permute-done | bytes 98336 | tf_op jit(solution)/shard_map/ppermute | solution.py:583
  63.1 0.2 collective-permute-done.12.rest_3_
  63.3 1.3 %finish.1 = (f32[2,256,384]{2,1,0:T(8,128)}, f32[2,256,384]{2,1,0:T(8,128)}) custom-call(f32[2,256,384]{2,1,0:T(8,128)S(1)} %get-tuple-element.30.shift_ref, bf16[128,384]{1,0:T(8,128)(2,1)S(1)} %get-tuple-element.38.rest_0_, bf16[128,384]{1,0:T(8,128)(2,1)S(1)} %collective-permute-done.10.rest_1_, bf16[128,384]{1,0:T(8,128)(2,1)S(1)} %collective-permute-done.11.rest_2_, ...), custom_call_target="tpu_custom_call" | custom-call | tf_op jit(solution)/shard_map/finish/pallas_call | solution.py:571
  (3 shorter events, 0.0 us)
Async XLA Ops:
  0.6 23.7 %copy-start = (f32[2,256,384]{2,1,0:T(8,128)S(1)}, f32[2,256,384]{2,1,0:T(8,128)}, u32[]{:S(2)}) copy-start(f32[2,256,384]{2,1,0:T(8,128)} %img_ref.1) | copy-start | bytes 2359300
  0.6 23.7 %copy-start.1 = (f32[2,256,384]{2,1,0:T(8,128)S(1)}, f32[2,256,384]{2,1,0:T(8,128)}, u32[]{:S(2)}) copy-start(f32[2,256,384]{2,1,0:T(8,128)} %dual_ref.1) | copy-start | bytes 2359300
  6.4 4.9 %collective-permute-start = (bf16[560,128]{1,0:T(8,128)(2,1)}, bf16[560,128]{1,0:T(8,128)(2,1)S(1)}, u32[]{:S(2)}, u32[]{:S(2)}) collective-permute-start(bf16[560,128]{1,0:T(8,128)(2,1)} %get-tuple-element.23), channel_id=1, source_target_pairs={{0,4},{4,0},{8,12},{12,8},{16,20},{20,16},{24,28},{28,24},{1,5},{5... | collective-permute-start | bytes 430088 | tf_op jit(solution)/shard_map/ppermute | solution.py:617
  6.9 7.4 %collective-permute-start.1 = (bf16[560,128]{1,0:T(8,128)(2,1)}, bf16[560,128]{1,0:T(8,128)(2,1)S(1)}, u32[]{:S(2)}, u32[]{:S(2)}) collective-permute-start(bf16[560,128]{1,0:T(8,128)(2,1)} %get-tuple-element.24), channel_id=1, source_target_pairs={{0,8},{4,12},{8,0},{12,4},{16,24},{20,28},{24,16},{28,20},{1,9},{5... | collective-permute-start | bytes 430088 | tf_op jit(solution)/shard_map/ppermute | solution.py:617
  9.4 7.5 %collective-permute-start.2 = (bf16[560,128]{1,0:T(8,128)(2,1)}, bf16[560,128]{1,0:T(8,128)(2,1)S(1)}, u32[]{:S(2)}, u32[]{:S(2)}) collective-permute-start(bf16[560,128]{1,0:T(8,128)(2,1)} %get-tuple-element.25), channel_id=1, source_target_pairs={{0,12},{4,8},{8,4},{12,0},{16,28},{20,24},{24,20},{28,16},{1,13},{... | collective-permute-start | bytes 430088 | tf_op jit(solution)/shard_map/ppermute | solution.py:617
  9.5 7.4 %collective-permute-start.3 = (bf16[560,128]{1,0:T(8,128)(2,1)}, bf16[560,128]{1,0:T(8,128)(2,1)S(1)}, u32[]{:S(2)}, u32[]{:S(2)}) collective-permute-start(bf16[560,128]{1,0:T(8,128)(2,1)} %get-tuple-element.26), channel_id=1, source_target_pairs={{0,16},{4,20},{8,24},{12,28},{16,0},{20,4},{24,8},{28,12},{1,17},{... | collective-permute-start | bytes 430088 | tf_op jit(solution)/shard_map/ppermute | solution.py:617
  11.3 13.0 %collective-permute-start.4 = (bf16[560,128]{1,0:T(8,128)(2,1)}, bf16[560,128]{1,0:T(8,128)(2,1)S(1)}, u32[]{:S(2)}, u32[]{:S(2)}) collective-permute-start(bf16[560,128]{1,0:T(8,128)(2,1)} %get-tuple-element.27), channel_id=1, source_target_pairs={{0,20},{4,16},{8,28},{12,24},{16,4},{20,0},{24,12},{28,8},{1,21},{... | collective-permute-start | bytes 430088 | tf_op jit(solution)/shard_map/ppermute | solution.py:617
  11.3 13.0 %collective-permute-start.5 = (bf16[560,128]{1,0:T(8,128)(2,1)}, bf16[560,128]{1,0:T(8,128)(2,1)S(1)}, u32[]{:S(2)}, u32[]{:S(2)}) collective-permute-start(bf16[560,128]{1,0:T(8,128)(2,1)} %get-tuple-element.28), channel_id=1, source_target_pairs={{0,24},{4,28},{8,16},{12,20},{16,8},{20,12},{24,0},{28,4},{1,25},{... | collective-permute-start | bytes 430088 | tf_op jit(solution)/shard_map/ppermute | solution.py:617
  14.3 10.1 %copy-start.3 = (f32[2]{0:T(128)S(1)}, f32[2]{0:T(128)}, u32[]{:S(2)}) copy-start(f32[2]{0:T(128)} %step_ref.1) | copy-start | bytes 28
  14.3 10.1 %collective-permute-start.6 = (bf16[560,128]{1,0:T(8,128)(2,1)}, bf16[560,128]{1,0:T(8,128)(2,1)S(1)}, u32[]{:S(2)}, u32[]{:S(2)}) collective-permute-start(bf16[560,128]{1,0:T(8,128)(2,1)} %get-tuple-element.29), channel_id=1, source_target_pairs={{0,28},{4,24},{8,20},{12,16},{16,12},{20,8},{24,4},{28,0},{1,29},{... | collective-permute-start | bytes 430088 | tf_op jit(solution)/shard_map/ppermute | solution.py:617
  24.4 0.9 %copy-start.2 = (bf16[560,128]{1,0:T(8,128)(2,1)S(1)}, bf16[560,128]{1,0:T(8,128)(2,1)}, u32[]{:S(2)}) copy-start(bf16[560,128]{1,0:T(8,128)(2,1)} %get-tuple-element.22.rest_0_) | copy-start | bytes 430084
  25.3 10.4 %copy-start.5 = (bf16[64,8,3,3]{0,1,3,2:T(8,128)(2,1)S(1)}, bf16[64,8,3,3]{0,1,3,2:T(8,128)(2,1)}, u32[]{:S(2)}) copy-start(bf16[64,8,3,3]{0,1,3,2:T(8,128)(2,1)} %param.17) | copy-start | bytes 27652
  25.3 10.4 %copy-start.4 = (bf16[64,64,3,3]{1,0,3,2:T(8,128)(2,1)S(1)}, bf16[64,64,3,3]{1,0,3,2:T(8,128)(2,1)}, u32[]{:S(2)}) copy-start(bf16[64,64,3,3]{1,0,3,2:T(8,128)(2,1)} %param.18) | copy-start | bytes 221188
  29.8 8.2 %collective-permute-start.7 = (bf16[160,384]{1,0:T(8,128)(2,1)S(1)}, bf16[160,384]{1,0:T(8,128)(2,1)S(1)}, u32[]{:S(2)}, u32[]{:S(2)}) collective-permute-start(bf16[160,384]{1,0:T(8,128)(2,1)S(1)} %get-tuple-element.35), channel_id=1, source_target_pairs={{0,1},{1,2},{2,3},{3,0},{4,5},{5,6},{6,7},{7,4},{8,9},{9,10},{10,1... | collective-permute-start | bytes 368648 | tf_op jit(solution)/shard_map/ppermute | solution.py:583
  31.8 11.3 %collective-permute-start.8 = (bf16[160,384]{1,0:T(8,128)(2,1)S(1)}, bf16[160,384]{1,0:T(8,128)(2,1)S(1)}, u32[]{:S(2)}, u32[]{:S(2)}) collective-permute-start(bf16[160,384]{1,0:T(8,128)(2,1)S(1)} %get-tuple-element.36), channel_id=1, source_target_pairs={{0,2},{1,3},{2,0},{3,1},{4,6},{5,7},{6,4},{7,5},{8,10},{9,11},{10,... | collective-permute-start | bytes 368648 | tf_op jit(solution)/shard_map/ppermute | solution.py:583
  34.3 8.7 %collective-permute-start.9 = (bf16[160,384]{1,0:T(8,128)(2,1)S(1)}, bf16[160,384]{1,0:T(8,128)(2,1)S(1)}, u32[]{:S(2)}, u32[]{:S(2)}) collective-permute-start(bf16[160,384]{1,0:T(8,128)(2,1)S(1)} %get-tuple-element.37), channel_id=1, source_target_pairs={{0,3},{1,0},{2,1},{3,2},{4,7},{5,4},{6,5},{7,6},{8,11},{9,8},{10,9... | collective-permute-start | bytes 368648 | tf_op jit(solution)/shard_map/ppermute | solution.py:583
  35.7 0.7 %copy-start.6 = (bf16[8,64,3,3]{1,0,3,2:T(8,128)(2,1)S(1)}, bf16[8,64,3,3]{1,0,3,2:T(8,128)(2,1)}, u32[]{:S(2)}) copy-start(bf16[8,64,3,3]{1,0,3,2:T(8,128)(2,1)} %param.19) | copy-start | bytes 27652
  51.9 7.7 %collective-permute-start.10 = (bf16[128,384]{1,0:T(8,128)(2,1)S(1)}, bf16[128,384]{1,0:T(8,128)(2,1)S(1)}, u32[]{:S(2)}, u32[]{:S(2)}) collective-permute-start(bf16[128,384]{1,0:T(8,128)(2,1)S(1)} %get-tuple-element.39), channel_id=1, source_target_pairs={{0,1},{1,2},{2,3},{3,0},{4,5},{5,6},{6,7},{7,4},{8,9},{9,10},{10,1... | collective-permute-start | bytes 294920 | tf_op jit(solution)/shard_map/ppermute | solution.py:583
  55.1 8.0 %collective-permute-start.11 = (bf16[128,384]{1,0:T(8,128)(2,1)S(1)}, bf16[128,384]{1,0:T(8,128)(2,1)S(1)}, u32[]{:S(2)}, u32[]{:S(2)}) collective-permute-start(bf16[128,384]{1,0:T(8,128)(2,1)S(1)} %get-tuple-element.40), channel_id=1, source_target_pairs={{0,2},{1,3},{2,0},{3,1},{4,6},{5,7},{6,4},{7,5},{8,10},{9,11},{10,... | collective-permute-start | bytes 294920 | tf_op jit(solution)/shard_map/ppermute | solution.py:583
  56.7 6.6 %collective-permute-start.12 = (bf16[128,384]{1,0:T(8,128)(2,1)S(1)}, bf16[128,384]{1,0:T(8,128)(2,1)S(1)}, u32[]{:S(2)}, u32[]{:S(2)}) collective-permute-start(bf16[128,384]{1,0:T(8,128)(2,1)S(1)} %get-tuple-element.41), channel_id=1, source_target_pairs={{0,3},{1,0},{2,1},{3,2},{4,7},{5,4},{6,5},{7,6},{8,11},{9,8},{10,9... | collective-permute-start | bytes 294920 | tf_op jit(solution)/shard_map/ppermute | solution.py:583
